TPU v7x, 32 devices: a whole 2x2x4 slice. The times are simulated.
32 devices in a mesh: ep: 8 (over z, y), es: 4 (over x, core).
Axes of the slice: x: 2, y: 2, z: 4, core: 2. Of those that a mesh axis runs over, the one named last changes fastest.
Arguments:
- tokens: bfloat16 [16384, 1024], P(('ep', 'es')), may hold values from -26 to 26
- cotangent: bfloat16 [16384, 1024], P(('ep', 'es')), may hold values from -6 to 6
- w_qkv: bfloat16 [1024, 3072], P(('ep', 'es')), may hold values from -0.1875 to 0.1875
- w_out: bfloat16 [1024, 1024], P(('ep', 'es')), may hold values from -6 to 6
- w_fc_in: bfloat16 [1024, 4096], P(('ep', 'es')), may hold values from -0.5 to 0.5
- w_fc_out: bfloat16 [4096, 1024], P(('ep', 'es')), may hold values from -0.25 to 0.25
- norm1_gain: bfloat16 [1024], P(('ep', 'es')), may hold values from 0.25 to 1.75
- norm1_bias: bfloat16 [1024], P(('ep', 'es')), may hold values from -0.119628906 to 0.119628906
- norm2_gain: bfloat16 [1024], P(('ep', 'es')), may hold values from 0.25 to 1.75
- norm2_bias: bfloat16 [1024], P(('ep', 'es')), may hold values from -1.796875 to 1.796875
- coef_weight: bfloat16 [1024, 2], P(('ep', 'es')), may hold values from -0.1875 to 0.1875
- expert_up: bfloat16 [8, 4096, 1024], P('ep', 'es'), may hold values from -0.5 to 0.5
- expert_down: bfloat16 [8, 4096, 1024], P('ep', 'es'), may hold values from -0.25 to 0.25
- routes: int32 [16384, 1], P(('ep', 'es')), may hold values from 0 to 7; in each aligned block of 512 rows (0 to 511, 512 to 1023, ...) at most 128 rows name the same one
- keep_mask: int32 [16384], P(('ep', 'es')), may hold values 0 or 1
Outputs:
- out_tokens: bfloat16 [16384, 1024], P(('ep', 'es'))
- grad_tokens: float32 [16384, 1024], P(('ep', 'es'))
- grad_w_qkv: float32 [1024, 3072], P(('ep', 'es'))
- grad_w_out: float32 [1024, 1024], P(('ep', 'es'))
- grad_w_fc_in: float32 [1024, 4096], P(('ep', 'es'))
- grad_w_fc_out: float32 [4096, 1024], P(('ep', 'es'))
- grad_norm1_gain: float32 [1024], P(('ep', 'es'))
- grad_norm1_bias: float32 [1024], P(('ep', 'es'))
- grad_norm2_gain: float32 [1024], P(('ep', 'es'))
- grad_norm2_bias: float32 [1024], P(('ep', 'es'))
- grad_coef_weight: float32 [1024, 2], P(('ep', 'es'))
- grad_expert_up: float32 [8, 4096, 1024], P('ep', 'es')
- grad_expert_down: float32 [8, 4096, 1024], P('ep', 'es')
Inputs may be any that keep to these rules, and one draw needn't show every extreme that they name: `routes`: within the rows of one device no expert is named more than 128 times, a bound that some block reaches.
All inputs are finite; a program needn't handle non-finite values. No bound on the sum of `keep_mask` on one device may be relied on, other than what follows from the above.
Results may differ from a plain program's by a relative error of at most 0.015.
Values may be sent and summed in bfloat16 or wider, within the bound.
No kernel may reach another device: no remote copies, remote signals or barrier semaphores. Data moves between devices by JAX's collectives and lax.ppermute only.
A program may use at most 320 MiB of HBM per device.

v0:
```python
import jax
import jax.numpy as jnp
from jax import lax
from jax.sharding import PartitionSpec as P

HEADS = 16
HEAD_DIM = 64


EPSILON = 1e-05
MASKED = -1e30
HIGHEST_PRECISION = lax.Precision.HIGHEST


def layer_norm(values, gain, offset):
    average = jnp.mean(values, axis=-1, keepdims=True)
    centred = values - average
    variance = jnp.mean(centred * centred, axis=-1, keepdims=True)
    return centred * lax.rsqrt(variance + EPSILON) * gain + offset


def exact_gelu(values):
    return jax.nn.gelu(values, approximate=False)


def matrix_product(left, right):
    return jnp.dot(left, right, preferred_element_type=jnp.float32)


def contract_rows(left, right):
    return lax.dot_general(
        left, right, (((0,), (0,)), ((), ())), preferred_element_type=jnp.float32
    )


def contract_columns(left, right):
    return lax.dot_general(
        left, right, (((1,), (1,)), ((), ())), preferred_element_type=jnp.float32
    )


def split_heads(values, groups):
    rows = values.shape[0]
    return values.reshape(rows, groups, HEADS // groups, HEAD_DIM).transpose(1, 0, 2, 3)


def join_heads(values):
    groups, blocks, block_rows, per_group, depth = values.shape
    return values.transpose(1, 2, 0, 3, 4).reshape(blocks * block_rows, groups * per_group * depth)


def causal_scores(query_block, start, keys_all, scale):
    block_rows = query_block.shape[0]
    scores = (
        jnp.einsum("qhd,khd->hqk", query_block, keys_all, preferred_element_type=jnp.float32)
        * scale
    )
    query_place = start + lax.broadcasted_iota(jnp.int32, (1, block_rows, 1), 1)
    key_place = lax.broadcasted_iota(jnp.int32, (1, 1, keys_all.shape[0]), 2)
    return jnp.where(key_place <= query_place, scores, MASKED)


def softmax_pair(logits):
    largest = jnp.max(logits, axis=-1, keepdims=True)
    expanded = jnp.exp(logits - largest)
    return expanded / jnp.sum(expanded, axis=-1, keepdims=True)


def attention_forward(queries, keys_all, values_all, scale, block_rows, offset):
    row_count = queries.shape[0]
    groups = HEADS // min(HEADS, 4)
    per_group = HEADS // groups
    blocks = row_count // block_rows
    starts = offset + jnp.arange(blocks, dtype=jnp.int32) * block_rows

    def one_group(operands):
        query_heads, key_heads, value_heads = operands
        query_blocks = query_heads.reshape(blocks, block_rows, per_group, HEAD_DIM)

        def one_block(inner_operands):
            query_block, start = inner_operands
            scores = causal_scores(query_block, start, key_heads, scale)
            largest = jnp.max(scores, axis=-1, keepdims=True)
            expanded = jnp.exp(scores - largest)
            totals = jnp.sum(expanded, axis=-1, keepdims=True)
            probs_low = (expanded / totals).astype(jnp.bfloat16)
            attended = jnp.einsum(
                "hqk,khd->qhd", probs_low, value_heads, preferred_element_type=jnp.float32
            )
            return (attended.astype(jnp.bfloat16), largest + jnp.log(totals))

        return lax.map(one_block, (query_blocks, starts))

    attended, log_totals = lax.map(
        one_group,
        (
            split_heads(queries, groups),
            split_heads(keys_all, groups),
            split_heads(values_all, groups),
        ),
    )
    return (join_heads(attended), log_totals)


def attention_backward(
    queries, keys_all, values_all, grad_attended, log_totals, scale, block_rows, offset
):
    row_count = queries.shape[0]
    seq_rows = keys_all.shape[0]
    groups = HEADS // min(HEADS, 4)
    per_group = HEADS // groups
    blocks = row_count // block_rows
    starts = offset + jnp.arange(blocks, dtype=jnp.int32) * block_rows

    def one_group(operands):
        query_heads, key_heads, value_heads, grad_heads, log_heads = operands
        query_blocks = query_heads.reshape(blocks, block_rows, per_group, HEAD_DIM)
        grad_blocks = grad_heads.reshape(blocks, block_rows, per_group, HEAD_DIM)

        def one_block(carry, inner_operands):
            grad_keys, grad_values = carry
            query_block, grad_block, log_block, start = inner_operands
            scores = causal_scores(query_block, start, key_heads, scale)
            probs = jnp.exp(scores - log_block)
            grad_values = grad_values + jnp.einsum(
                "hqk,qhd->khd",
                probs.astype(jnp.bfloat16),
                grad_block,
                preferred_element_type=jnp.float32,
            )
            grad_probs = jnp.einsum(
                "qhd,khd->hqk", grad_block, value_heads, preferred_element_type=jnp.float32
            )
            grad_scores = probs * (grad_probs - jnp.sum(probs * grad_probs, axis=-1, keepdims=True))
            grad_raw = (grad_scores * scale).astype(jnp.bfloat16)
            grad_query = jnp.einsum(
                "hqk,khd->qhd", grad_raw, key_heads, preferred_element_type=jnp.float32
            )
            grad_keys = grad_keys + jnp.einsum(
                "hqk,qhd->khd", grad_raw, query_block, preferred_element_type=jnp.float32
            )
            return ((grad_keys, grad_values), grad_query)

        zeros = jnp.zeros((seq_rows, per_group, HEAD_DIM), jnp.float32)
        return lax.scan(one_block, (zeros, zeros), (query_blocks, grad_blocks, log_heads, starts))

    (grad_keys, grad_values), grad_queries = lax.map(
        one_group,
        (
            split_heads(queries, groups),
            split_heads(keys_all, groups),
            split_heads(values_all, groups),
            split_heads(grad_attended, groups),
            log_totals,
        ),
    )
    grad_keys = grad_keys.transpose(1, 0, 2, 3).reshape(seq_rows, HEADS * HEAD_DIM)
    grad_values = grad_values.transpose(1, 0, 2, 3).reshape(seq_rows, HEADS * HEAD_DIM)
    return (join_heads(grad_queries), grad_keys, grad_values)


def on_device(
    tokens,
    cotangent,
    w_qkv,
    w_out,
    w_fc_in,
    w_fc_out,
    norm1_gain,
    norm1_bias,
    norm2_gain,
    norm2_bias,
    coef_weight,
    expert_up,
    expert_down,
    routes,
    keep_mask,
):
    (
        full_qkv,
        full_out,
        full_fc_in,
        full_fc_out,
        gain_one,
        bias_one,
        gain_two,
        bias_two,
        full_coef,
    ) = (
        lax.all_gather(w_qkv, ("ep", "es"), axis=0, tiled=True),
        lax.all_gather(w_out, ("ep", "es"), axis=0, tiled=True),
        lax.all_gather(w_fc_in, ("ep", "es"), axis=0, tiled=True),
        lax.all_gather(w_fc_out, ("ep", "es"), axis=0, tiled=True),
        lax.all_gather(norm1_gain, ("ep", "es"), axis=0, tiled=True),
        lax.all_gather(norm1_bias, ("ep", "es"), axis=0, tiled=True),
        lax.all_gather(norm2_gain, ("ep", "es"), axis=0, tiled=True),
        lax.all_gather(norm2_bias, ("ep", "es"), axis=0, tiled=True),
        lax.all_gather(coef_weight, ("ep", "es"), axis=0, tiled=True),
    )
    gain_one = gain_one.astype(jnp.float32)
    bias_one = bias_one.astype(jnp.float32)
    gain_two = gain_two.astype(jnp.float32)
    bias_two = bias_two.astype(jnp.float32)
    coef_full = full_coef.astype(jnp.float32)
    row_count, width = tokens.shape
    block_rows = min(row_count, 512)
    scale = HEAD_DIM ** (-0.5)
    offset = lax.axis_index("es") * row_count
    inputs = tokens.astype(jnp.float32)
    normed_one, norm_one_pull = jax.vjp(layer_norm, inputs, gain_one, bias_one)
    normed_one_low = normed_one.astype(jnp.bfloat16)
    qkv_low = matrix_product(normed_one_low, full_qkv).astype(jnp.bfloat16)
    queries = qkv_low[:, :width]
    keys_all, values_all = (
        lax.all_gather(qkv_low[:, width : 2 * width], "es", axis=0, tiled=True),
        lax.all_gather(qkv_low[:, 2 * width :], "es", axis=0, tiled=True),
    )
    attended, log_totals = attention_forward(
        queries, keys_all, values_all, scale, block_rows, offset
    )
    hidden = inputs + matrix_product(attended, full_out)
    normed_two, norm_two_pull = jax.vjp(layer_norm, hidden, gain_two, bias_two)
    normed_two_low = normed_two.astype(jnp.bfloat16)
    coefficients = softmax_pair(jnp.dot(normed_two, coef_full, precision=HIGHEST_PRECISION))
    inner = matrix_product(normed_two_low, full_fc_in)
    activated, gelu_pull = jax.vjp(exact_gelu, inner)
    activated_low = activated.astype(jnp.bfloat16)
    dense = matrix_product(activated_low, full_fc_out)
    experts = lax.axis_size("ep")
    capacity = 2 * row_count // experts
    expert_ids = routes[:, 0]
    onehot = (expert_ids[:, None] == lax.broadcasted_iota(jnp.int32, (1, experts), 1)).astype(
        jnp.int32
    )
    ranks = jnp.sum((jnp.cumsum(onehot, axis=0) - 1) * onehot, axis=1)
    slots = expert_ids * capacity + ranks
    keep = keep_mask.astype(jnp.float32)[:, None]
    outgoing = jnp.zeros((experts * capacity, width), jnp.bfloat16).at[slots].set(normed_two_low)
    received = lax.all_to_all(
        outgoing.reshape(experts, capacity, width), "ep", split_axis=0, concat_axis=0, tiled=True
    ).reshape(experts * capacity, width)
    gathered = lax.all_gather(received, "es", axis=0, tiled=True)
    expert_inner = contract_columns(gathered, expert_up[0])
    expert_act, expert_pull = jax.vjp(exact_gelu, expert_inner)
    expert_act_low = expert_act.astype(jnp.bfloat16)
    expert_rows = lax.psum_scatter(
        matrix_product(expert_act_low, expert_down[0]), "es", scatter_dimension=0, tiled=True
    )
    returned = lax.all_to_all(
        expert_rows.astype(jnp.bfloat16).reshape(experts, capacity, width),
        "ep",
        split_axis=0,
        concat_axis=0,
        tiled=True,
    ).reshape(experts * capacity, width)
    expert_tokens = returned[slots].astype(jnp.float32) * keep
    mixed = hidden + coefficients[:, 0:1] * dense + coefficients[:, 1:2] * expert_tokens
    out_tokens = mixed.astype(jnp.bfloat16)
    grad_out = cotangent.astype(jnp.float32)
    grad_pair = jnp.concatenate(
        [
            jnp.sum(grad_out * dense, axis=1, keepdims=True),
            jnp.sum(grad_out * expert_tokens, axis=1, keepdims=True),
        ],
        axis=1,
    )
    grad_logits = coefficients * (
        grad_pair - jnp.sum(coefficients * grad_pair, axis=1, keepdims=True)
    )
    grad_coef = jnp.dot(normed_two.T, grad_logits, precision=HIGHEST_PRECISION)
    grad_normed_two = jnp.dot(grad_logits, coef_full.T, precision=HIGHEST_PRECISION)
    grad_dense_low = (coefficients[:, 0:1] * grad_out).astype(jnp.bfloat16)
    grad_fc_out = contract_rows(activated_low, grad_dense_low)
    grad_inner_low = gelu_pull(contract_columns(grad_dense_low, full_fc_out))[0].astype(
        jnp.bfloat16
    )
    grad_fc_in = contract_rows(normed_two_low, grad_inner_low)
    grad_normed_two = grad_normed_two + contract_columns(grad_inner_low, full_fc_in)
    grad_expert_low = (coefficients[:, 1:2] * keep * grad_out).astype(jnp.bfloat16)
    outgoing_grad = (
        jnp.zeros((experts * capacity, width), jnp.bfloat16).at[slots].set(grad_expert_low)
    )
    grad_received = lax.all_to_all(
        outgoing_grad.reshape(experts, capacity, width),
        "ep",
        split_axis=0,
        concat_axis=0,
        tiled=True,
    ).reshape(experts * capacity, width)
    grad_gathered = lax.all_gather(grad_received, "es", axis=0, tiled=True)
    grad_down = contract_rows(expert_act_low, grad_gathered)[None]
    grad_expert_inner = expert_pull(contract_columns(grad_gathered, expert_down[0]))[0].astype(
        jnp.bfloat16
    )
    grad_up = contract_rows(grad_expert_inner, gathered)[None]
    grad_expert_rows = lax.psum_scatter(
        matrix_product(grad_expert_inner, expert_up[0]), "es", scatter_dimension=0, tiled=True
    )
    grad_back = lax.all_to_all(
        grad_expert_rows.astype(jnp.bfloat16).reshape(experts, capacity, width),
        "ep",
        split_axis=0,
        concat_axis=0,
        tiled=True,
    ).reshape(experts * capacity, width)
    grad_normed_two = grad_normed_two + grad_back[slots].astype(jnp.float32)
    grad_hidden_norm, grad_gain_two, grad_bias_two = norm_two_pull(grad_normed_two)
    grad_hidden = grad_out + grad_hidden_norm
    grad_att_low = grad_hidden.astype(jnp.bfloat16)
    grad_w_out = contract_rows(attended, grad_att_low)
    grad_attended = contract_columns(grad_att_low, full_out).astype(jnp.bfloat16)
    grad_queries, grad_keys_all, grad_values_all = attention_backward(
        queries, keys_all, values_all, grad_attended, log_totals, scale, block_rows, offset
    )
    grad_keys, grad_values = (
        lax.psum_scatter(grad_keys_all, "es", scatter_dimension=0, tiled=True),
        lax.psum_scatter(grad_values_all, "es", scatter_dimension=0, tiled=True),
    )
    grad_qkv_low = jnp.concatenate([grad_queries, grad_keys, grad_values], axis=1).astype(
        jnp.bfloat16
    )
    grad_w_qkv = contract_rows(normed_one_low, grad_qkv_low)
    grad_inputs_norm, grad_gain_one, grad_bias_one = norm_one_pull(
        contract_columns(grad_qkv_low, full_qkv)
    )
    grad_tokens = grad_hidden + grad_inputs_norm
    reduced = (
        lax.psum_scatter(grad_w_qkv, ("ep", "es"), scatter_dimension=0, tiled=True),
        lax.psum_scatter(grad_w_out, ("ep", "es"), scatter_dimension=0, tiled=True),
        lax.psum_scatter(grad_fc_in, ("ep", "es"), scatter_dimension=0, tiled=True),
        lax.psum_scatter(grad_fc_out, ("ep", "es"), scatter_dimension=0, tiled=True),
        lax.psum_scatter(grad_gain_one, ("ep", "es"), scatter_dimension=0, tiled=True),
        lax.psum_scatter(grad_bias_one, ("ep", "es"), scatter_dimension=0, tiled=True),
        lax.psum_scatter(grad_gain_two, ("ep", "es"), scatter_dimension=0, tiled=True),
        lax.psum_scatter(grad_bias_two, ("ep", "es"), scatter_dimension=0, tiled=True),
        lax.psum_scatter(grad_coef, ("ep", "es"), scatter_dimension=0, tiled=True),
    )
    return (
        out_tokens,
        grad_tokens,
        reduced[0],
        reduced[1],
        reduced[2],
        reduced[3],
        reduced[4],
        reduced[5],
        reduced[6],
        reduced[7],
        reduced[8],
        grad_up,
        grad_down,
    )


def solution(mesh):
    placed = (
        P(("ep", "es"), None),
        P(("ep", "es"), None),
        P(("ep", "es"), None),
        P(("ep", "es"), None),
        P(("ep", "es"), None),
        P(("ep", "es"), None),
        P(("ep", "es")),
        P(("ep", "es")),
        P(("ep", "es")),
        P(("ep", "es")),
        P(("ep", "es"), None),
        P("ep", "es", None),
        P("ep", "es", None),
        P(("ep", "es"), None),
        P(("ep", "es")),
    )
    return jax.shard_map(
        on_device,
        mesh=mesh,
        in_specs=placed,
        out_specs=(
            P(("ep", "es"), None),
            P(("ep", "es"), None),
            P(("ep", "es"), None),
            P(("ep", "es"), None),
            P(("ep", "es"), None),
            P(("ep", "es"), None),
            P(("ep", "es")),
            P(("ep", "es")),
            P(("ep", "es")),
            P(("ep", "es")),
            P(("ep", "es"), None),
            P("ep", "es", None),
            P("ep", "es", None),
        ),
        check_vma=False,
    )
```

profile of v0, /device:TPU:0, one launch (start us, length us, event | category | flops | bytes accessed | tf_op | source)
XLA Modules:
  0.0 2373.8 jit_solution(6762923505961703382)
XLA Ops:
  11.3 42.5 %all-reduce.9 = (bf16[1024]{0:T(1024)(128)(2,1)S(1)}, bf16[1024]{0:T(1024)(128)(2,1)S(1)}, bf16[1024]{0:T(1024)(128)(2,1)S(1)}, bf16[1024]{0:T(1024)(128)(2,1)S(1)}) all-reduce(bf16[1024]{0:T(1024)(128)(2,1)S(1)} %dynamic-update-slice.1, bf16[1024]{0:T(1024)(128)(2,1)S(1)} %dynamic-update-slice, ...), channel_id=1, replica_groups=mesh['ep'=8,'es'=4] {'ep','es'}, use_global_device_ids=true, to_apply=%add.1 | all-reduce | flops 4096 | bytes 16384
  97.8 27.0 %all-gather.12.cloned.1.call-done = bf16[2048,1024]{1,0:T(8,128)(2,1)} async-done(((bf16[512,1024]{1,0:T(8,128)(2,1)}), bf16[2048,1024]{1,0:T(8,128)(2,1)}) %all-gather.12.cloned.1.call-update) | async-done | bytes 4194320 | tf_op jit(solution)/shard_map/all_gather | solution.py:216
  131.2 30.3 %all-gather.14.cloned.1.call-done = bf16[2048,1024]{1,0:T(8,128)(2,1)} async-done(((bf16[512,1024]{1,0:T(8,128)(2,1)}), bf16[2048,1024]{1,0:T(8,128)(2,1)}) %all-gather.14.cloned.1.call-update) | async-done | bytes 4194320 | tf_op jit(solution)/shard_map/all_gather | solution.py:215
  168.0 68.8 %while.10 = (s32[]{:T(128)}, bf16[4,1,512,4,64]{2,4,3,1,0:T(8,128)(2,1)}, f32[4,1,4,512,1]{3,2,4,1,0:T(4,128)}, bf16[4,2048,4,64]{1,3,2,0:T(8,128)(2,1)}, s32[1]...) while((s32[]{:T(128)}, ...), condition=%wide.region_5.6_spmd, body=%wide.region_2.5_spmd.sunk | while | flops 1125251584 | bytes 57219672 | solution.py:94
  247.2 54.2 %all_to_all.20 = bf16[8,128,1024]{2,1,0:T(8,128)(2,1)} all-to-all(bf16[8,128,1024]{2,1,0:T(8,128)(2,1)} %bitcast.199), channel_id=1, replica_groups=mesh['ep'=8,'es'=4] {'ep'}, dimensions={0} | all-to-all | bytes 4194304 | tf_op jit(solution)/shard_map/all_to_all | solution.py:239
  301.7 56.3 %all-gather.22.cloned.1.call-done = bf16[4096,1024]{1,0:T(8,128)(2,1)} async-done(((bf16[1024,1024]{1,0:T(8,128)(2,1)}), bf16[4096,1024]{1,0:T(8,128)(2,1)}) %all-gather.22.cloned.1.call-update) | async-done | bytes 8388624 | tf_op jit(solution)/shard_map/all_gather | solution.py:242
  358.0 47.3 %multiply_convert_fusion.1 = (bf16[4096,1024]{1,0:T(8,128)(2,1)S(1)}, f32[4096,1024]{1,0:T(8,128)}, f32[4096,1024]{1,0:T(8,128)}) fusion(bf16[4096,1024]{1,0:T(8,128)(2,1)} %all-gather.22.cloned.1.call-done, bf16[1,1024,1024]{2,1,0:T(8,128)(2,1)S(1)} %copy-done), kind=kOutput, calls=%fused_computation.86 | convolution fusion | flops 8862564352 | bytes 52428800 | tf_op jit(solution)/shard_map/dot_general | solution.py:37
  421.8 40.4 %all-gather = bf16[32,32,2]{1,2,0:T(2,128)(2,1)S(1)} all-gather(bf16[1,32,2]{1,2,0:T(2,128)(2,1)S(1)} %bitcast.225), channel_id=1, replica_groups=mesh['ep'=8,'es'=4] {'ep','es'}, dimensions={0}, use_global_device_ids=true | all-gather | bytes 4224 | tf_op jit(solution)/shard_map/all_gather | solution.py:198
  462.3 84.3 %reduce-scatter.12.cloned.1.call-done = f32[1024,1024]{1,0:T(8,128)} async-done(((f32[4096,1024]{1,0:T(8,128)}), f32[1024,1024]{1,0:T(8,128)}) %reduce-scatter.12.cloned.1.call-update) | async-done | bytes 4194320 | tf_op jit(solution)/shard_map/reduce_scatter | solution.py:246
  556.2 93.5 %all-gather.18.cloned.1.call-done = bf16[1024,4096]{1,0:T(8,128)(2,1)} async-done(((bf16[32,4096]{1,0:T(8,128)(2,1)}), bf16[1024,4096]{1,0:T(8,128)(2,1)}) %all-gather.18.cloned.1.call-update) | async-done | bytes 8388624 | tf_op jit(solution)/shard_map/all_gather | solution.py:192
  649.8 26.8 %multiply_convert_fusion.2 = (bf16[512,4096]{1,0:T(8,128)(2,1)}, f32[512,4096]{1,0:T(8,128)}, f32[512,4096]{1,0:T(8,128)}) fusion(bf16[1024,4096]{1,0:T(8,128)(2,1)} %all-gather.18.cloned.1.call-done, f32[512,1024]{1,0:T(8,128)} %copy-done.2, f32[1024]{0:T(1024)S(1)} %copy-done.35, f32[1024]{0:T(1024)S(1)} %copy-done.22, f32[512]{0:T(512)S(1)} %copy-done.28, ...), kind=kOutput, calls=%fused_computation.103 | convolution fusion | flops 4433903616 | bytes 31469568 | tf_op jit(solution)/shard_map/dot_general | solution.py:27
  683.9 45.2 %all-gather.20.cloned.1.call-done = bf16[4096,1024]{1,0:T(8,128)(2,1)} async-done(((bf16[128,1024]{1,0:T(8,128)(2,1)}), bf16[4096,1024]{1,0:T(8,128)(2,1)}) %all-gather.20.cloned.1.call-update) | async-done | bytes 8388624 | tf_op jit(solution)/shard_map/all_gather | solution.py:193
  744.2 53.2 %all_to_all.21 = bf16[8,128,1024]{2,1,0:T(8,128)(2,1)} all-to-all(bf16[8,128,1024]{2,1,0:T(8,128)(2,1)} %bitcast.204), channel_id=1, replica_groups=mesh['ep'=8,'es'=4] {'ep'}, dimensions={0} | all-to-all | bytes 4194304 | tf_op jit(solution)/shard_map/all_to_all | solution.py:283
  797.5 57.4 %all-gather.24.cloned.1.call-done = bf16[4096,1024]{1,0:T(8,128)(2,1)} async-done(((bf16[1024,1024]{1,0:T(8,128)(2,1)}), bf16[4096,1024]{1,0:T(8,128)(2,1)}) %all-gather.24.cloned.1.call-update) | async-done | bytes 8388624 | tf_op jit(solution)/shard_map/all_gather | solution.py:290
  892.9 126.2 %reduce-scatter.14.cloned.1.call-done = f32[1024,1024]{1,0:T(8,128)} async-done(((f32[4096,1024]{1,0:T(8,128)}), f32[1024,1024]{1,0:T(8,128)}) %reduce-scatter.14.cloned.1.call-update) | async-done | bytes 4194320 | tf_op jit(solution)/shard_map/reduce_scatter | solution.py:296
  1094.8 315.9 %while.27 = (s32[]{:T(128)}, f32[4,2048,4,64]{1,3,2,0:T(8,128)}, f32[4,2048,4,64]{1,3,2,0:T(8,128)}, bf16[4,1,512,4,64]{2,4,3,1,0:T(8,128)(2,1)}, bf16[4,512,4,6...) while((s32[]{:T(128)}, f32[4,2048,4,64]{1,3,2,0:T(8,128)}, ...), condition=%wide.region_24.25_spmd, body=%wide.region_22.24_spmd.sunk | while | flops 2794463744 | bytes 199820400 | solution.py:147
  1446.0 34.9 %reduce-scatter.16.cloned.1.call-done = f32[512,1024]{0,1:T(8,128)} async-done(((f32[2048,1024]{0,1:T(8,128)}), f32[512,1024]{0,1:T(8,128)}) %reduce-scatter.16.cloned.1.call-update) | async-done | bytes 2097168 | tf_op jit(solution)/shard_map/reduce_scatter | solution.py:316
  1482.6 72.6 %reduce-scatter.18.cloned.1.call-done = f32[512,1024]{0,1:T(8,128)} async-done(((f32[2048,1024]{0,1:T(8,128)}), f32[512,1024]{0,1:T(8,128)}) %reduce-scatter.18.cloned.1.call-update) | async-done | bytes 2097168 | tf_op jit(solution)/shard_map/reduce_scatter | solution.py:317
  1566.9 125.0 %reduce-scatter.28.cloned.1.call-done = f32[32,2]{1,0:T(8,128)} async-done(((f32[1024,2]{1,0:T(8,128)}), f32[32,2]{1,0:T(8,128)}) %reduce-scatter.28.cloned.1.call-update) | async-done | bytes 272
  1730.5 40.4 %all-reduce.8 = (f32[1024]{0:T(1024)S(1)}, f32[1024]{0:T(1024)S(1)}, f32[1024]{0:T(1024)S(1)}, f32[1024]{0:T(1024)S(1)}) all-reduce(f32[1024]{0:T(1024)S(1)} %get-tuple-element.163, f32[1024]{0:T(1024)S(1)} %get-tuple-element.166, f32[1024]{0:T(1024)S(1)} %copy-done.48, ...), channel_id=10, replica_groups=mesh['ep'=8,'es'=4] {'ep','es'}, use_global_device_ids=true, to_apply=%region_34.35.clone | all-reduce | flops 4096 | bytes 32768
  1778.1 97.5 %reduce-scatter.24.cloned.1.call-done = f32[32,4096]{1,0:T(8,128)} async-done(((f32[1024,4096]{1,0:T(8,128)}), f32[32,4096]{1,0:T(8,128)}) %reduce-scatter.24.cloned.1.call-update) | async-done | bytes 524304 | tf_op jit(solution)/shard_map/reduce_scatter | solution.py:330
  1875.5 187.4 %reduce-scatter.26.cloned.1.call-done = f32[128,1024]{1,0:T(8,128)} async-done(((f32[4096,1024]{1,0:T(8,128)}), f32[128,1024]{1,0:T(8,128)}) %reduce-scatter.26.cloned.1.call-update) | async-done | bytes 524304 | tf_op jit(solution)/shard_map/reduce_scatter | solution.py:331
  2062.9 145.3 %reduce-scatter.22.cloned.1.call-done = f32[32,1024]{1,0:T(8,128)} async-done(((f32[1024,1024]{1,0:T(8,128)}), f32[32,1024]{1,0:T(8,128)}) %reduce-scatter.22.cloned.1.call-update) | async-done | bytes 131088 | tf_op jit(solution)/shard_map/reduce_scatter | solution.py:329
  2208.2 158.8 %reduce-scatter.20.cloned.1.call-done = f32[32,3072]{1,0:T(8,128)} async-done(((f32[1024,3072]{1,0:T(8,128)}), f32[32,3072]{1,0:T(8,128)}) %reduce-scatter.20.cloned.1.call-update) | async-done | bytes 393232 | tf_op jit(solution)/shard_map/reduce_scatter | solution.py:328
  (318 shorter events, 711.5 us)
Async XLA Ops:
  7.2 350.9 %copy-start = (bf16[1,1024,1024]{2,1,0:T(8,128)(2,1)S(1)}, bf16[1,1024,1024]{2,1,0:T(8,128)(2,1)}, u32[]{:S(2)}) copy-start(bf16[1,1024,1024]{2,1,0:T(8,128)(2,1)} %param.30) | copy-start | bytes 6291460
  7.2 76.1 %all-gather.10.cloned.1.call-start = ((), (), s32[]{:S(2)}) async-start(), calls=%async_computation.13 | async-start | bytes 6488064 | tf_op jit(solution)/shard_map/all_gather | solution.py:190
  7.9 116.9 %all-gather.12.cloned.1.call-start = ((), (), s32[]{:S(2)}) async-start(), calls=%async_computation.14 | async-start | bytes 5242880 | tf_op jit(solution)/shard_map/all_gather | solution.py:216
  91.6 69.9 %all-gather.14.cloned.1.call-start = ((), (), s32[]{:S(2)}) async-start(), calls=%async_computation.15 | async-start | bytes 5242880 | tf_op jit(solution)/shard_map/all_gather | solution.py:215
  92.4 144.4 %all-gather.16.cloned.1.call-start = ((), (), s32[]{:S(2)}) async-start(), calls=%async_computation.16 | async-start | bytes 2162688 | tf_op jit(solution)/shard_map/all_gather | solution.py:191
  92.9 265.1 %all-gather.22.cloned.1.call-start = ((), (), s32[]{:S(2)}) async-start(), calls=%async_computation.19 | async-start | bytes 10485760 | tf_op jit(solution)/shard_map/all_gather | solution.py:242
  301.5 245.1 %reduce-scatter.12.cloned.1.call-start = ((), (), s32[]{:S(2)}) async-start(), calls=%async_computation.20 | async-start | bytes 20971520 | tf_op jit(solution)/shard_map/reduce_scatter | solution.py:246
  420.3 229.4 %all-gather.18.cloned.1.call-start = ((), (), s32[]{:S(2)}) async-start(), calls=%async_computation.17 | async-start | bytes 8650752 | tf_op jit(solution)/shard_map/all_gather | solution.py:192
  421.1 308.0 %all-gather.20.cloned.1.call-start = ((), (), s32[]{:S(2)}) async-start(), calls=%async_computation.18 | async-start | bytes 8650752 | tf_op jit(solution)/shard_map/all_gather | solution.py:193
  550.4 127.7 %all-to-all-start.1 = ((bf16[8,128,1024]{2,1,0:T(8,128)(2,1)}), bf16[8,128,1024]{2,1,0:T(8,128)(2,1)}, u32[]{:S(2)}, u32[]{:S(2)}) async-start(bf16[8,128,1024]{2,1,0:T(8,128)(2,1)} %bitcast.198), calls=%async_computation.2 | async-start | bytes 4194304 | tf_op jit(solution)/shard_map/all_to_all | solution.py:249
  555.9 299.0 %all-gather.24.cloned.1.call-start = ((), (), s32[]{:S(2)}) async-start(), calls=%async_computation.21 | async-start | bytes 10485760 | tf_op jit(solution)/shard_map/all_gather | solution.py:290
  739.9 342.3 %copy-start.50 = (f32[512]{0:T(512)}, f32[512]{0:T(512)S(1)}, u32[]{:S(2)}) copy-start(f32[512]{0:T(512)S(1)} %get-tuple-element.168) | copy-start | bytes 6148
  739.9 342.3 %copy-start.52 = (f32[512]{0:T(512)}, f32[512]{0:T(512)S(1)}, u32[]{:S(2)}) copy-start(f32[512]{0:T(512)S(1)} %get-tuple-element.169) | copy-start | bytes 6148
  740.0 346.9 %copy-start.57 = (f32[512,1]{0,1:T(1,128)}, f32[512,1]{0,1:T(1,128)S(1)}, u32[]{:S(2)}) copy-start(f32[512,1]{0,1:T(1,128)S(1)} %get-tuple-element.228) | copy-start | bytes 6148
  797.5 221.7 %reduce-scatter.14.cloned.1.call-start = ((), (), s32[]{:S(2)}) async-start(), calls=%async_computation.22 | async-start | bytes 20971520 | tf_op jit(solution)/shard_map/reduce_scatter | solution.py:296
  1023.0 53.9 %all-to-all-start.3 = ((bf16[8,128,1024]{2,1,0:T(8,128)(2,1)}), bf16[8,128,1024]{2,1,0:T(8,128)(2,1)}, u32[]{:S(2)}, u32[]{:S(2)}) async-start(bf16[8,128,1024]{2,1,0:T(8,128)(2,1)} %bitcast.49), calls=%async_computation.5 | async-start | bytes 4194304 | tf_op jit(solution)/shard_map/all_to_all | solution.py:299
  1028.6 452.3 %reduce-scatter.16.cloned.1.call-start = ((), (), s32[]{:S(2)}) async-start(), calls=%async_computation.23 | async-start | bytes 10485760 | tf_op jit(solution)/shard_map/reduce_scatter | solution.py:316
  1410.8 144.4 %reduce-scatter.18.cloned.1.call-start = ((), (), s32[]{:S(2)}) async-start(), calls=%async_computation.24 | async-start | bytes 10485760 | tf_op jit(solution)/shard_map/reduce_scatter | solution.py:317
  1411.4 280.4 %reduce-scatter.28.cloned.1.call-start = ((), (), s32[]{:S(2)}) async-start(), calls=%async_computation.29 | async-start | bytes 540672
  1416.8 458.7 %reduce-scatter.24.cloned.1.call-start = ((), (), s32[]{:S(2)}) async-start(), calls=%async_computation.27 | async-start | bytes 17301504 | tf_op jit(solution)/shard_map/reduce_scatter | solution.py:330
  1428.5 634.4 %reduce-scatter.26.cloned.1.call-start = ((), (), s32[]{:S(2)}) async-start(), calls=%async_computation.28 | async-start | bytes 17301504 | tf_op jit(solution)/shard_map/reduce_scatter | solution.py:331
  1440.2 768.0 %reduce-scatter.22.cloned.1.call-start = ((), (), s32[]{:S(2)}) async-start(), calls=%async_computation.26 | async-start | bytes 4325376 | tf_op jit(solution)/shard_map/reduce_scatter | solution.py:329
  1445.9 921.1 %reduce-scatter.20.cloned.1.call-start = ((), (), s32[]{:S(2)}) async-start(), calls=%async_computation.25 | async-start | bytes 12976128 | tf_op jit(solution)/shard_map/reduce_scatter | solution.py:328
  1724.3 642.8 %copy-start.1 = (bf16[1,1024,1024]{2,1,0:T(8,128)(2,1)S(1)}, bf16[1,1024,1024]{2,1,0:T(8,128)(2,1)}, u32[]{:S(2)}) copy-start(bf16[1,1024,1024]{2,1,0:T(8,128)(2,1)} %param.30) | copy-start | bytes 6291460
  (64 other events, 3390.1 us)
Sparse Core Ops, SparseCore 0:
  10.9 72.3 all-gather.9
  91.7 33.0 all-gather.11
  127.0 34.5 all-gather.13
  164.3 56.3 all-gather.15
  301.6 56.4 all-gather.21
  420.4 126.1 reduce-scatter.11
  549.8 99.8 all-gather.17
  653.0 76.0 all-gather.19
  797.6 57.2 all-gather.23
  893.0 126.0 reduce-scatter.13
  1411.0 69.8 reduce-scatter.15
  1483.5 71.6 reduce-scatter.17
  1558.0 133.8 reduce-scatter.27
  1694.7 180.8 reduce-scatter.23
  1878.4 184.5 reduce-scatter.25
  2065.7 142.4 reduce-scatter.21
  2215.7 151.2 reduce-scatter.19
where the time goes:
time: 2380 us; the launch traced here: 2370 us
  waiting for transfers between devices  1400 us (59%)
  matrix products  605 us (25%)
  blocking collectives  231 us (10%)
  other arithmetic  62.4 us (3%)
  local copies, waits for them, and re-layouts  51.6 us (2%)
    reduce_scatter x1, waiting for transfers between devices, on_device(): lax.psum_scatter(grad_fc_out, ('ep', 'es'), scatter_dimension=0, tiled=True)  187 us
    reduce_scatter x1, waiting for transfers between devices, on_device(): lax.psum_scatter(grad_w_qkv, ('ep', 'es'), scatter_dimension=0, tiled=True)  159 us
    reduce_scatter x1, waiting for transfers between devices, on_device(): lax.psum_scatter(grad_w_out, ('ep', 'es'), scatter_dimension=0, tiled=True)  145 us
    unnamed x18, waiting for transfers between devices  129 us
    reduce_scatter x1, waiting for transfers between devices, on_device(): lax.psum_scatter(matrix_product(grad_expert_inner, expert_up[0]), 'es', s...  126 us
    dot_general x4, matrix products, one_block(): jnp.einsum('hqk,qhd->khd', grad_raw, query_block, preferred_element_type=...  100 us
    dot_general x6, matrix products, contract_columns(): lax.dot_general(left, right, (((1,), (1,)), ((), ())), preferred_element_...  97.7 us
    reduce_scatter x1, waiting for transfers between devices, on_device(): lax.psum_scatter(grad_fc_in, ('ep', 'es'), scatter_dimension=0, tiled=True)  97.5 us
  transfers between devices with their start and end apart: 19, of which 17 were waited for; matrix products, arithmetic and copies ran while one was open for 10% of the time, Pallas kernels for 0%

commit v1 on v0

v1 whole, which is shorter than its diff:
```python
import functools

import jax
import jax.numpy as jnp
import numpy as np
from jax import lax
from jax.experimental import pallas as pl
from jax.experimental.pallas import tpu as pltpu
from jax.sharding import PartitionSpec as P

HEADS = 16
HEAD_DIM = 64
EPSILON = 1e-05
MASKED = -1e30
HIGHEST = lax.Precision.HIGHEST
BOTH = ("ep", "es")
MIB = 1 << 20


def norm_forward(values, gain, offset):
    average = jnp.mean(values, axis=-1, keepdims=True)
    centred = values - average
    variance = jnp.mean(centred * centred, axis=-1, keepdims=True)
    inverse = lax.rsqrt(variance + EPSILON)
    unit = centred * inverse
    return unit * gain + offset, unit, inverse


def norm_backward(grad, unit, inverse, gain):
    scaled = grad * gain
    mean_scaled = jnp.mean(scaled, axis=-1, keepdims=True)
    mean_unit = jnp.mean(scaled * unit, axis=-1, keepdims=True)
    grad_in = (scaled - mean_scaled - unit * mean_unit) * inverse
    return grad_in, jnp.sum(grad * unit, axis=0), jnp.sum(grad, axis=0)


def gelu_and_slope(values):
    cdf = 0.5 * (1.0 + lax.erf(values * (2.0**-0.5)))
    density = jnp.exp(-0.5 * values * values) * ((2.0 * np.pi) ** -0.5)
    return values * cdf, cdf + values * density


def dot(left, right, contract=((1,), (0,)), out=jnp.float32):
    return lax.dot_general(left, right, (contract, ((), ())), preferred_element_type=out)


def softmax_pair(logits):
    largest = jnp.max(logits, axis=-1, keepdims=True)
    expanded = jnp.exp(logits - largest)
    return expanded / jnp.sum(expanded, axis=-1, keepdims=True)


def digits(axis):
    size = lax.axis_size(axis)
    return [(axis, 1 << b) for b in range(size.bit_length() - 1)]


def exchange(x, digit):
    axis, stride = digit
    size = lax.axis_size(axis)
    return lax.ppermute(x, axis, [(i, i ^ stride) for i in range(size)])


def weight_of(digit):
    axis, stride = digit
    return stride * (lax.axis_size("es") if axis == "ep" else 1)


def relative_numbers(order):
    numbers = [0]
    for digit in order:
        numbers = numbers + [n + weight_of(digit) for n in numbers]
    return numbers


def gather_relative(shard, order):
    held = shard[None]
    for digit in order[:-1]:
        held = jnp.concatenate([held, exchange(held, digit)], axis=0)
    return held, exchange(held, order[-1])


def place_kernel(plan, me_ref, *refs):
    out, held, sems_in, sems_out = refs[-4:]
    me = me_ref[0]
    arriving, leaving = [], []
    for number, (which, row, relative, rows, first, width) in enumerate(plan):
        at = (pl.ds(number * rows, rows), pl.ds(0, width))
        copy = pltpu.make_async_copy(refs[which].at[row], held.at[at], sems_in.at[number])
        copy.start()
        arriving.append(copy)
        start = pl.multiple_of((me ^ relative) * rows, rows)
        leaving.append(
            pltpu.make_async_copy(
                held.at[at], out.at[pl.ds(start, rows), pl.ds(first, width)], sems_out.at[number]
            )
        )
    for number in range(len(plan)):
        arriving[number].wait()
        leaving[number].start()
    for copy in leaving:
        copy.wait()


def gather_rows(shard, orders, me):
    rows, columns = shard.shape
    width = columns // len(orders)
    count = 1 << len(orders[0])
    if rows % 16 or width % 128:
        axes = tuple(a for a in BOTH if any(d[0] == a for d in orders[0]))
        return lax.all_gather(shard, axes, axis=0, tiled=True)
    parts, plan = [], []
    for index, order in enumerate(orders):
        numbers = relative_numbers(order)
        first = index * width
        held, received = gather_relative(shard[:, first : first + width], order)
        for half, part in enumerate((held, received)):
            for row in range(count // 2):
                plan.append((len(parts), row, numbers[half * (count // 2) + row], rows, first, width))
            parts.append(part)
    return pl.pallas_call(
        functools.partial(place_kernel, tuple(plan)),
        out_shape=jax.ShapeDtypeStruct((count * rows, columns), shard.dtype),
        in_specs=[pl.BlockSpec(memory_space=pltpu.SMEM)] + [pl.BlockSpec(memory_space=pl.ANY)] * len(parts),
        out_specs=pl.BlockSpec(memory_space=pl.ANY),
        scratch_shapes=[
            pltpu.VMEM((len(plan) * rows, width), shard.dtype),
            pltpu.SemaphoreType.DMA((len(plan),)),
            pltpu.SemaphoreType.DMA((len(plan),)),
        ],
        compiler_params=pltpu.CompilerParams(vmem_limit_bytes=16 * MIB),
        name="place_rows",
    )(me, *parts)


def gather_small(shard, order, me):
    held = shard[None]
    for digit in order:
        held = jnp.concatenate([held, exchange(held, digit)], axis=0)
    numbers = relative_numbers(order)
    count = len(numbers)
    place = np.zeros(count, np.int32)
    place[np.array(numbers)] = np.arange(count)
    index = jnp.asarray(place)[jnp.arange(count, dtype=jnp.int32) ^ me]
    return held[index]


def scatter_sum(partial, order, kept=jnp.bfloat16):
    count = 1 << len(order)
    rows = partial.shape[0] // count
    remaining = sorted(order, key=weight_of, reverse=True)
    held = partial.reshape((2,) * len(order) + (rows,) + partial.shape[1:])
    for number, digit in enumerate(order):
        axis, stride = digit
        place = remaining.index(digit)
        remaining.remove(digit)
        bit = (lax.axis_index(axis) // stride) % 2
        mine = lax.dynamic_index_in_dim(held, bit, place, keepdims=False)
        theirs = lax.dynamic_index_in_dim(held, 1 - bit, place, keepdims=False)
        held = mine.astype(jnp.float32) + exchange(theirs, digit).astype(jnp.float32)
        if number < len(order) - 1:
            held = held.astype(kept)
    return held


def head_mask(rows, width, head):
    lane = lax.broadcasted_iota(jnp.int32, (rows, width), 1)
    return (lane // HEAD_DIM) == head


def causal_tile(block):
    key = lax.broadcasted_iota(jnp.int32, (block, block), 0)
    query = lax.broadcasted_iota(jnp.int32, (block, block), 1)
    return key <= query


def attend_kernel(heads, block, q_ref, k_ref, vt_ref, low_ref, full_ref, log_ref, qh, acc, top, total):
    i = pl.program_id(0)
    width = heads * HEAD_DIM
    scaled = q_ref[...] * jnp.asarray(HEAD_DIM**-0.5, jnp.bfloat16)
    for h in range(heads):
        qh[h] = jnp.where(head_mask(block, width, h), scaled, jnp.zeros_like(scaled))
    acc[...] = jnp.zeros_like(acc)
    total[...] = jnp.zeros_like(total)
    top[...] = jnp.full_like(top, MASKED)
    nt = ((1,), (1,))

    def scores(j, h, diagonal):
        s = dot(k_ref[pl.ds(j * block, block), :], qh[h], nt)
        return jnp.where(causal_tile(block), s, MASKED) if diagonal else s

    def find_top(j, diagonal):
        for h in range(heads):
            s = scores(j, h, diagonal)
            folded = jnp.max(s.reshape(block // 8, 8, block), axis=0)
            top[h] = jnp.maximum(top[h], folded)

    def add_block(j, diagonal):
        for h in range(heads):
            s = scores(j, h, diagonal)
            p = jnp.exp(s - jnp.max(top[h], axis=0, keepdims=True))
            total[h] = total[h] + jnp.sum(p.reshape(block // 8, 8, block), axis=0)
            low = slice(h * HEAD_DIM, (h + 1) * HEAD_DIM)
            acc[low, :] = acc[low, :] + dot(
                vt_ref[low, pl.ds(j * block, block)], p.astype(jnp.bfloat16)
            )

    @pl.loop(0, i)
    def _(j):
        find_top(j, False)

    find_top(i, True)
    for h in range(heads):
        top[h] = jnp.broadcast_to(jnp.max(top[h], axis=0, keepdims=True), top.shape[1:])

    @pl.loop(0, i)
    def _(j):
        add_block(j, False)

    add_block(i, True)
    for h in range(heads):
        summed = jnp.sum(total[h], axis=0, keepdims=True)
        log_ref[pl.ds(h, 1), :] = jnp.max(top[h], axis=0, keepdims=True) + jnp.log(summed)
        low = slice(h * HEAD_DIM, (h + 1) * HEAD_DIM)
        acc[low, :] = acc[low, :] / summed
    out = acc[...].T
    full_ref[...] = out
    low_ref[...] = out.astype(jnp.bfloat16)


def attend(q, k, v):
    rows, width = q.shape
    heads = width // HEAD_DIM
    block = min(256, rows)
    whole = lambda shape: pl.BlockSpec(shape, lambda i: (0, 0))
    return pl.pallas_call(
        functools.partial(attend_kernel, heads, block),
        grid=(rows // block,),
        in_specs=[
            pl.BlockSpec((block, width), lambda i: (i, 0)),
            whole((rows, width)),
            whole((width, rows)),
        ],
        out_specs=[
            pl.BlockSpec((block, width), lambda i: (i, 0)),
            pl.BlockSpec((block, width), lambda i: (i, 0)),
            pl.BlockSpec((heads, block), lambda i: (0, i)),
        ],
        out_shape=[
            jax.ShapeDtypeStruct((rows, width), jnp.bfloat16),
            jax.ShapeDtypeStruct((rows, width), jnp.float32),
            jax.ShapeDtypeStruct((heads, rows), jnp.float32),
        ],
        scratch_shapes=[
            pltpu.VMEM((heads, block, width), jnp.bfloat16),
            pltpu.VMEM((width, block), jnp.float32),
            pltpu.VMEM((heads, 8, block), jnp.float32),
            pltpu.VMEM((heads, 8, block), jnp.float32),
        ],
        compiler_params=pltpu.CompilerParams(vmem_limit_bytes=32 * MIB),
        cost_estimate=pl.CostEstimate(
            flops=3 * rows * rows * width * heads,
            bytes_accessed=12 * rows * width,
            transcendentals=heads * rows * rows // 2,
        ),
        name="attend",
    )(q, k, v.T)


def attend_back_kernel(
    heads, block, q_ref, k_ref, kt_ref, v_ref, g_ref, log_ref, delta_ref,
    gq_ref, gk_ref, gv_ref, qh, gh, acc, acc_k, acc_v,
):
    i = pl.program_id(0)
    width = heads * HEAD_DIM
    scale = HEAD_DIM**-0.5
    scaled = q_ref[...] * jnp.asarray(scale, jnp.bfloat16)
    grads = g_ref[...]
    for h in range(heads):
        mask = head_mask(block, width, h)
        qh[pl.ds(h * block, block), :] = jnp.where(mask, scaled, jnp.zeros_like(scaled))
        gh[pl.ds(h * block, block), :] = jnp.where(mask, grads, jnp.zeros_like(grads))
    acc[...] = jnp.zeros_like(acc)

    @pl.when(i == 0)
    def _():
        acc_k[...] = jnp.zeros_like(acc_k)
        acc_v[...] = jnp.zeros_like(acc_v)

    nt = ((1,), (1,))

    def one(j, diagonal):
        at = pl.ds(j * block, block)
        keys, values = k_ref[at, :], v_ref[at, :]
        probs, raws = [], []
        for h in range(heads):
            s = dot(keys, qh[pl.ds(h * block, block), :], nt)
            p = jnp.exp(s - log_ref[pl.ds(h, 1), :])
            if diagonal:
                p = jnp.where(causal_tile(block), p, 0.0)
            dp = dot(values, gh[pl.ds(h * block, block), :], nt)
            raw = (p * (dp - delta_ref[pl.ds(h, 1), :])).astype(jnp.bfloat16)
            low = slice(h * HEAD_DIM, (h + 1) * HEAD_DIM)
            acc[low, :] = acc[low, :] + dot(kt_ref[low, at], raw)
            probs.append(p.astype(jnp.bfloat16))
            raws.append(raw)
        acc_v[at, :] = acc_v[at, :] + dot(jnp.concatenate(probs, axis=1), gh[...])
        acc_k[at, :] = acc_k[at, :] + dot(jnp.concatenate(raws, axis=1), qh[...])

    @pl.loop(0, i)
    def _(j):
        one(j, False)

    one(i, True)
    gq_ref[...] = (acc[...].T * scale).astype(jnp.bfloat16)

    @pl.when(i == pl.num_programs(0) - 1)
    def _():
        gk_ref[...] = acc_k[...].astype(jnp.bfloat16)
        gv_ref[...] = acc_v[...].astype(jnp.bfloat16)


def attend_back(q, k, v, grad, logs, delta):
    rows, width = q.shape
    heads = width // HEAD_DIM
    block = min(256, rows)
    whole = lambda shape: pl.BlockSpec(shape, lambda i: (0, 0))
    strip = pl.BlockSpec((block, width), lambda i: (i, 0))
    line = pl.BlockSpec((heads, block), lambda i: (0, i))
    low = jax.ShapeDtypeStruct((rows, width), jnp.bfloat16)
    return pl.pallas_call(
        functools.partial(attend_back_kernel, heads, block),
        grid=(rows // block,),
        in_specs=[strip, whole((rows, width)), whole((width, rows)), whole((rows, width)), strip, line, line],
        out_specs=[strip, whole((rows, width)), whole((rows, width))],
        out_shape=[low, low, low],
        scratch_shapes=[
            pltpu.VMEM((heads * block, width), jnp.bfloat16),
            pltpu.VMEM((heads * block, width), jnp.bfloat16),
            pltpu.VMEM((width, block), jnp.float32),
            pltpu.VMEM((rows, width), jnp.float32),
            pltpu.VMEM((rows, width), jnp.float32),
        ],
        compiler_params=pltpu.CompilerParams(vmem_limit_bytes=48 * MIB),
        cost_estimate=pl.CostEstimate(
            flops=5 * rows * rows * width * heads,
            bytes_accessed=14 * rows * width,
            transcendentals=heads * rows * rows // 2,
        ),
        name="attend_back",
    )(q, k, k.T, v, grad, logs, delta)


def swap_groups(x, axis):
    return lax.all_to_all(x, axis, split_axis=0, concat_axis=0, tiled=True)


def on_device(
    tokens,
    cotangent,
    w_qkv,
    w_out,
    w_fc_in,
    w_fc_out,
    norm1_gain,
    norm1_bias,
    norm2_gain,
    norm2_bias,
    coef_weight,
    expert_up,
    expert_down,
    routes,
    keep_mask,
):
    rows, width = tokens.shape
    n_es = lax.axis_size("es")
    experts = lax.axis_size("ep")
    me_scalar = lax.axis_index("ep") * n_es + lax.axis_index("es")
    me = me_scalar.astype(jnp.int32).reshape(1)
    me_es = lax.axis_index("es").astype(jnp.int32).reshape(1)
    ep_up, es_up = digits("ep"), digits("es")
    order_a = ep_up[:0:-1] + ep_up[:1] + es_up[:0:-1] + es_up[:1]
    order_b = es_up[:0:-1] + ep_up[:0:-1] + ep_up[:1] + es_up[:1]
    order_e = es_up[::-1]

    full_qkv = gather_rows(w_qkv, (order_a, order_b), me)
    packed = jnp.concatenate(
        [
            jnp.stack([norm1_gain, norm1_bias, norm2_gain, norm2_bias]),
            coef_weight.T,
        ],
        axis=0,
    )
    small = gather_small(packed, order_a, me_scalar).transpose(1, 0, 2).reshape(6, width)
    small = small.astype(jnp.float32)
    gain_one, bias_one, gain_two, bias_two = (small[i : i + 1] for i in range(4))
    coef_full = small[4:6]
    full_out = gather_rows(w_out, (order_a, order_b), me)
    full_fc_in = gather_rows(w_fc_in, (order_a, order_b), me)
    full_fc_out = gather_rows(w_fc_out, (order_a, order_b), me)
    full_up = gather_rows(expert_up[0], (order_e,), me_es)
    full_down = gather_rows(expert_down[0], (order_e,), me_es)

    group = width // n_es
    inputs = tokens.astype(jnp.float32)
    normed_one, unit_one, inverse_one = norm_forward(inputs, gain_one, bias_one)
    normed_one_low = normed_one.astype(jnp.bfloat16)
    qkv_low = dot(normed_one_low, full_qkv).astype(jnp.bfloat16)
    by_group = qkv_low.reshape(rows, 3, n_es, group).transpose(2, 0, 1, 3).reshape(n_es, rows, 3 * group)
    mine = swap_groups(by_group, "es").reshape(n_es * rows, 3 * group)
    q, k, v = mine[:, :group], mine[:, group : 2 * group], mine[:, 2 * group :]
    attended_mine, attended_full, logs = attend(q, k, v)
    attended = (
        swap_groups(attended_mine.reshape(n_es, rows, group), "es").transpose(1, 0, 2).reshape(rows, width)
    )
    hidden = inputs + dot(attended, full_out)
    normed_two, unit_two, inverse_two = norm_forward(hidden, gain_two, bias_two)
    normed_two_low = normed_two.astype(jnp.bfloat16)
    coefficients = softmax_pair(
        lax.dot_general(normed_two, coef_full, (((1,), (1,)), ((), ())), precision=HIGHEST)
    )
    keep = keep_mask.astype(jnp.float32)[:, None]
    grad_out = cotangent.astype(jnp.float32)
    grad_dense_low = (coefficients[:, 0:1] * grad_out).astype(jnp.bfloat16)
    grad_expert_low = (coefficients[:, 1:2] * keep * grad_out).astype(jnp.bfloat16)

    capacity = 2 * rows // experts
    expert_ids = routes[:, 0]
    chosen = (expert_ids[:, None] == lax.broadcasted_iota(jnp.int32, (1, experts), 1)).astype(jnp.float32)
    before = (
        lax.broadcasted_iota(jnp.int32, (rows, rows), 1) < lax.broadcasted_iota(jnp.int32, (rows, rows), 0)
    ).astype(jnp.float32)
    ranks = jnp.sum(dot(before, chosen) * chosen, axis=1).astype(jnp.int32)
    slots = expert_ids * capacity + ranks
    in_slot = (slots[None, :] == lax.broadcasted_iota(jnp.int32, (experts * capacity, 1), 0)).astype(
        jnp.bfloat16
    )
    outgoing = dot(in_slot, jnp.concatenate([normed_two_low, grad_expert_low], axis=1)).astype(jnp.bfloat16)
    received = swap_groups(outgoing.reshape(experts, capacity, 2 * width), "ep").reshape(
        experts * capacity, 2 * width
    )
    expert_in, expert_grad = received[:, :width], received[:, width:]

    inner = dot(normed_two_low, full_fc_in)
    activated, slope = gelu_and_slope(inner)
    activated_low = activated.astype(jnp.bfloat16)
    dense = dot(activated_low, full_fc_out)
    grad_fc_out = dot(activated_low, grad_dense_low, ((0,), (0,))).astype(jnp.bfloat16)
    grad_inner_low = (dot(grad_dense_low, full_fc_out, ((1,), (1,))) * slope).astype(jnp.bfloat16)
    grad_fc_in = dot(normed_two_low, grad_inner_low, ((0,), (0,))).astype(jnp.bfloat16)
    grad_normed_dense = dot(grad_inner_low, full_fc_in, ((1,), (1,)))

    expert_inner = dot(expert_in, full_up, ((1,), (1,)))
    expert_act, expert_slope = gelu_and_slope(expert_inner)
    expert_act_low = expert_act.astype(jnp.bfloat16)
    expert_out = dot(expert_act_low, full_down).astype(jnp.bfloat16)
    grad_expert_inner = (dot(expert_grad, full_down, ((1,), (1,))) * expert_slope).astype(jnp.bfloat16)
    grad_expert_in = dot(grad_expert_inner, full_up).astype(jnp.bfloat16)
    returned = swap_groups(
        jnp.concatenate([expert_out, grad_expert_in], axis=1).reshape(experts, capacity, 2 * width), "ep"
    ).reshape(experts * capacity, 2 * width)
    grad_down = dot(expert_act_low, expert_grad, ((0,), (0,))).astype(jnp.bfloat16)
    grad_up = dot(grad_expert_inner, expert_in, ((0,), (0,))).astype(jnp.bfloat16)
    at_home = dot(in_slot, returned, ((0,), (0,)))
    expert_tokens = at_home[:, :width] * keep
    grad_expert_home = at_home[:, width:]

    mixed = hidden + coefficients[:, 0:1] * dense + coefficients[:, 1:2] * expert_tokens
    out_tokens = mixed.astype(jnp.bfloat16)
    grad_pair = jnp.concatenate(
        [
            jnp.sum(grad_out * dense, axis=1, keepdims=True),
            jnp.sum(grad_out * expert_tokens, axis=1, keepdims=True),
        ],
        axis=1,
    )
    grad_logits = coefficients * (
        grad_pair - jnp.sum(coefficients * grad_pair, axis=1, keepdims=True)
    )
    grad_coef = lax.dot_general(grad_logits, normed_two, (((0,), (0,)), ((), ())), precision=HIGHEST)
    grad_normed_two = (
        grad_normed_dense
        + grad_expert_home
        + grad_logits[:, 0:1] * coef_full[0:1]
        + grad_logits[:, 1:2] * coef_full[1:2]
    )
    grad_hidden_norm, grad_gain_two, grad_bias_two = norm_backward(
        grad_normed_two, unit_two, inverse_two, gain_two
    )
    grad_hidden = grad_out + grad_hidden_norm
    grad_att_low = grad_hidden.astype(jnp.bfloat16)
    grad_w_out = dot(attended, grad_att_low, ((0,), (0,))).astype(jnp.bfloat16)
    grad_attended = dot(grad_att_low, full_out, ((1,), (1,))).astype(jnp.bfloat16)

    grad_mine = swap_groups(grad_attended.reshape(rows, n_es, group).transpose(1, 0, 2), "es").reshape(
        n_es * rows, group
    )
    per_head = (
        lax.broadcasted_iota(jnp.int32, (group // HEAD_DIM, group), 1) // HEAD_DIM
        == lax.broadcasted_iota(jnp.int32, (group // HEAD_DIM, group), 0)
    ).astype(jnp.float32)
    delta = lax.dot_general(
        per_head,
        grad_mine.astype(jnp.float32) * attended_full,
        (((1,), (1,)), ((), ())),
        precision=HIGHEST,
    )
    grad_q, grad_k, grad_v = attend_back(q, k, v, grad_mine, logs, delta)
    grad_qkv_low = (
        swap_groups(
            jnp.concatenate([grad_q, grad_k, grad_v], axis=1).reshape(n_es, rows, 3 * group), "es"
        )
        .reshape(n_es, rows, 3, group)
        .transpose(1, 2, 0, 3)
        .reshape(rows, 3 * width)
    )
    grad_w_qkv = dot(normed_one_low, grad_qkv_low, ((0,), (0,))).astype(jnp.bfloat16)
    grad_inputs_norm, grad_gain_one, grad_bias_one = norm_backward(
        dot(grad_qkv_low, full_qkv, ((1,), (1,))), unit_one, inverse_one, gain_one
    )
    grad_tokens = grad_hidden + grad_inputs_norm

    back_a, back_b, back_e = order_a[::-1], order_b[::-1], order_e[::-1]

    def sum_halves(partial):
        half = partial.shape[1] // 2
        return jnp.concatenate(
            [scatter_sum(partial[:, :half], back_a), scatter_sum(partial[:, half:], back_b)], axis=1
        )

    small_grads = jnp.stack(
        [grad_gain_one, grad_bias_one, grad_gain_two, grad_bias_two, grad_coef[0], grad_coef[1]]
    )
    count = experts * n_es
    small_sum = scatter_sum(
        small_grads.reshape(6, count, width // count).transpose(1, 0, 2).reshape(count * 6, width // count),
        back_a,
        jnp.float32,
    )
    return (
        out_tokens,
        grad_tokens,
        sum_halves(grad_w_qkv),
        sum_halves(grad_w_out),
        sum_halves(grad_fc_in),
        sum_halves(grad_fc_out),
        small_sum[0],
        small_sum[1],
        small_sum[2],
        small_sum[3],
        small_sum[4:6].T,
        scatter_sum(grad_up, back_e)[None],
        scatter_sum(grad_down, back_e)[None],
    )


def solution(mesh):
    both = P(BOTH)
    table = P(BOTH, None)
    stack = P("ep", "es", None)
    return jax.shard_map(
        on_device,
        mesh=mesh,
        in_specs=(table,) * 6 + (both,) * 4 + (table, stack, stack, table, both),
        out_specs=(table,) * 6 + (both,) * 4 + (table, stack, stack),
        check_vma=False,
    )
```

time: 2380 us -> 1130 us (0.47)
  waiting for transfers between devices: 1400 us -> 418 us
  matrix products: 605 us -> 176 us
  blocking collectives: 231 us -> 0 us
  Pallas kernels: 0 us -> 138 us
  starting transfers between devices: 12.3 us -> 140 us
  local copies, waits for them, and re-layouts: 51.6 us -> 175 us
    reduce_scatter x8 -> x0, waiting for transfers between devices: 907 us -> none  [the longest x1 187 us: on_device(): lax.psum_scatter(grad_fc_out, ('ep', 'es'), scatter_dimension=0, tiled=True)]
    dot_general x48 -> x24, matrix products: 601 us -> 176 us  [the longest x21 171 us: dot(): lax.dot_general(left, right, (contract, ((), ())), preferred_element_type...]
    ppermute x0 -> x98, waiting for transfers between devices: none -> 418 us  [exchange(): return lax.ppermute(x, axis, [(i, i ^ stride) for i in range(size)])]
    all_gather x8 -> x0, waiting for transfers between devices: 336 us -> none  [the longest x1 93.5 us: on_device(): lax.all_gather(w_fc_in, ('ep', 'es'), axis=0, tiled=True)]
    pallas_call x0 -> x8, Pallas kernels: none -> 138 us  [the longest x1 57.7 us: attend_back(): pl.pallas_call(functools.partial(attend_back_kernel, heads, block), grid=...]
    unnamed x18 -> x0, waiting for transfers between devices: 129 us -> none
    all_to_all x2 -> x0, blocking collectives: 107 us -> none  [the longest x1 54.2 us: on_device(): lax.all_to_all(outgoing.reshape(experts, capacity, width), 'ep', split_ax...]
    ppermute x0 -> x98, starting transfers between devices: none -> 102 us  [exchange(): return lax.ppermute(x, axis, [(i, i ^ stride) for i in range(size)])]
  transfers between devices with their start and end apart: 19 -> 104, of which waited for: 17 -> 38; matrix products, arithmetic and copies ran while one was open for 10% -> 30% of each run, Pallas kernels for 0% -> 12%
where the time goes in v1:
time: 1130 us
  waiting for transfers between devices  418 us (37%)
  matrix products  176 us (16%)
  local copies, waits for them, and re-layouts  175 us (15%)
  starting transfers between devices  140 us (12%)
  Pallas kernels  138 us (12%)
  other arithmetic  76.2 us (7%)
    ppermute x98, waiting for transfers between devices, exchange(): return lax.ppermute(x, axis, [(i, i ^ stride) for i in range(size)])  418 us
    dot_general x21, matrix products, dot(): lax.dot_general(left, right, (contract, ((), ())), preferred_element_type...  171 us
    ppermute x98, starting transfers between devices, exchange(): return lax.ppermute(x, axis, [(i, i ^ stride) for i in range(size)])  102 us
    unnamed x314, local copies, waits for them, and re-layouts  64.5 us
    pallas_call x1, Pallas kernels, attend_back(): pl.pallas_call(functools.partial(attend_back_kernel, heads, block), grid=...  57.7 us
    pallas_call x1, Pallas kernels, attend(): pl.pallas_call(functools.partial(attend_kernel, heads, block), grid=(rows...  46.2 us
    all_to_all x6, starting transfers between devices, swap_groups(): return lax.all_to_all(x, axis, split_axis=0, concat_axis=0, tiled=True)  37.7 us
    pallas_call x6, Pallas kernels, gather_rows(): pl.pallas_call(functools.partial(place_kernel, tuple(plan)), out_shape=ja...  34 us
  transfers between devices with their start and end apart: 104, of which 38 were waited for; matrix products, arithmetic and copies ran while one was open for 30% of the time, Pallas kernels for 12%

profile of v1, /device:TPU:0, one launch (start us, length us, event | category | flops | bytes accessed | tf_op | source)
XLA Modules:
  0.0 1126.6 jit_solution(5704028472857688920)
XLA Ops:
  36.9 15.1 %collective-permute-done.3 = bf16[8,6,32]{2,1,0:T(8,128)(2,1)S(1)} collective-permute-done((bf16[8,6,32]{2,1,0:T(8,128)(2,1)S(1)}, bf16[8,6,32]{2,1,0:T(8,128)(2,1)S(1)}, u32[]{:S(2)}, u32[]{:S(2)}) %collective-permute-start.3) | collective-permute-done | bytes 3104 | tf_op jit(solution)/shard_map/ppermute | solution.py:61
  128.7 8.4 collective-permute-done.13
  161.3 11.7 %place_rows.6 = bf16[1024,3072]{1,0:T(8,128)(2,1)S(1)} custom-call(s32[1]{0:T(128)} %bitcast.10.me_ref, bf16[16,32,1536]{2,1,0:T(8,128)(2,1)S(1)} %constant_dynamic-update-slice_fusion.11.refs_0_, bf16[16,32,1536]{2,1,0:T(8,128)(2,1)S(1)} %collective-permute-done.9.refs_1_, bf16[16,32,1536]{2,1,0:T(8,128)(2,1)S(1)} %constant_dynamic-update-slice_fusion.16.refs_2_, ...), custom_call_target="tpu_custom_call" | custom-call | tf_op jit(solution)/shard_map/place_rows/pallas_call | solution.py:121
  190.5 15.4 %all-to-all-start = ((bf16[4,512,768]{1,2,0:T(8,128)(2,1)}), bf16[4,512,768]{1,2,0:T(8,128)(2,1)}, u32[]{:S(2)}, u32[]{:S(2)}) async-start(bf16[4,512,768]{1,2,0:T(8,128)(2,1)} %bitcast.435), calls=%async_computation | async-start | bytes 6291456 | tf_op jit(solution)/shard_map/all_to_all | solution.py:355
  227.5 60.0 %collective-permute-done.38 = bf16[8,128,512]{2,1,0:T(8,128)(2,1)S(1)} collective-permute-done((bf16[8,128,512]{2,1,0:T(8,128)(2,1)S(1)}, bf16[8,128,512]{2,1,0:T(8,128)(2,1)S(1)}, u32[]{:S(2)}, u32[]{:S(2)}) %collective-permute-start.38) | collective-permute-done | bytes 1048608 | tf_op jit(solution)/shard_map/ppermute | solution.py:61
  305.0 46.2 %attend.1 = (bf16[2048,256]{1,0:T(8,128)(2,1)S(1)}, f32[2048,256]{1,0:T(8,128)S(1)}, f32[4,2048]{1,0:T(4,128)S(1)}) custom-call(bf16[2048,256]{1,0:T(8,128)(2,1)S(1)} %copy-done.9, bf16[2048,256]{1,0:T(8,128)(2,1)S(1)} %get-tuple-element.63.k_ref, bf16[256,2048]{1,0:T(8,128)(2,1)S(1)} %copy.180.vt_ref), custom_call_target="tpu_custom_call" | custom-call | flops 12884901888 | bytes 6291456 | tf_op jit(solution)/shard_map/attend/pallas_call | solution.py:236
  411.5 9.0 multiply_convert_fusion.1
  420.5 10.4 fusion.11
  497.5 18.2 %collective-permute-done.75 = bf16[2,2,2,32,2048]{4,3,2,0,1:T(8,128)(2,1)S(1)} collective-permute-done((bf16[2,2,2,32,2048]{4,3,2,0,1:T(8,128)(2,1)S(1)}, bf16[2,2,2,32,2048]{4,3,2,0,1:T(8,128)(2,1)S(1)}, u32[]{:S(2)}, u32[]{:S(2)}) %collective-permute-start.75) | collective-permute-done | bytes 1048608 | tf_op jit(solution)/shard_map/ppermute | solution.py:61
  520.2 18.1 %collective-permute-done.85 = bf16[2,2,2,128,512]{4,3,2,0,1:T(8,128)(2,1)S(1)} collective-permute-done((bf16[2,2,2,128,512]{4,3,2,0,1:T(8,128)(2,1)S(1)}, bf16[2,2,2,128,512]{4,3,2,0,1:T(8,128)(2,1)S(1)}, u32[]{:S(2)}, u32[]{:S(2)}) %collective-permute-start.85) | collective-permute-done | bytes 1048608 | tf_op jit(solution)/shard_map/ppermute | solution.py:61
  545.1 14.3 %multiply_convert_fusion = (bf16[1024,4096]{1,0:T(8,128)(2,1)}, f32[1024,4096]{1,0:T(8,128)S(1)}) fusion(bf16[4096,1024]{1,0:T(8,128)(2,1)} %copy-done.3, bf16[1024,2048]{1,0:T(8,128)(2,1)} %bitcast.32), kind=kOutput, calls=%fused_computation.9 | convolution fusion | flops 8610906112 | bytes 35651584 | tf_op jit(solution)/shard_map/dot_general | solution.py:44
  559.4 17.1 %fusion.5 = bf16[1024,4096]{1,0:T(8,128)(2,1)} fusion(f32[1024,4096]{1,0:T(8,128)S(1)} %get-tuple-element.121, bf16[4096,1024]{1,0:T(8,128)(2,1)} %copy-done.2, bf16[1024,2048]{1,0:T(8,128)(2,1)} %bitcast.32), kind=kOutput, calls=%fused_computation.8 | convolution fusion | flops 8631877632 | bytes 35651584 | tf_op jit(solution)/shard_map/dot_general | solution.py:44
  576.5 12.6 %convolution_convert_fusion.7 = bf16[1024,1024]{0,1:T(8,128)(2,1)} fusion(bf16[1024,4096]{1,0:T(8,128)(2,1)} %fusion.5, bf16[4096,1024]{1,0:T(8,128)(2,1)S(1)} %bitcast.429), kind=kOutput, calls=%fused_computation.114 | convolution fusion | flops 8590983168 | bytes 18874368 | tf_op jit(solution)/shard_map/dot_general | solution.py:44
  589.0 12.9 %convolution_convert_fusion.1 = bf16[4096,1024]{1,0:T(8,128)(2,1)S(1)} fusion(bf16[1024,4096]{1,0:T(8,128)(2,1)} %fusion.5, bf16[1024,2048]{1,0:T(8,128)(2,1)} %bitcast.32), kind=kOutput, calls=%fused_computation.25 | convolution fusion | flops 8594128896 | bytes 18874368 | tf_op jit(solution)/shard_map/dot_general | solution.py:44
  607.5 15.7 %convolution_convert_fusion = bf16[4096,1024]{1,0:T(8,128)(2,1)} fusion(bf16[1024,4096]{1,0:T(8,128)(2,1)} %get-tuple-element.120, bf16[1024,2048]{1,0:T(8,128)(2,1)} %bitcast.32), kind=kOutput, calls=%fused_computation.24 | convolution fusion | flops 8594128896 | bytes 18874368 | tf_op jit(solution)/shard_map/dot_general | solution.py:44
  623.2 12.4 %convolution_convert_fusion.8 = bf16[1024,1024]{0,1:T(8,128)(2,1)} fusion(bf16[1024,4096]{1,0:T(8,128)(2,1)} %get-tuple-element.120, bf16[4096,1024]{1,0:T(8,128)(2,1)S(1)} %bitcast.427), kind=kOutput, calls=%fused_computation.115 | convolution fusion | flops 8590983168 | bytes 18874368 | tf_op jit(solution)/shard_map/dot_general | solution.py:44
  657.1 102.6 %collective-permute-done.77 = bf16[2,32,2048]{2,1,0:T(8,128)(2,1)S(1)} collective-permute-done((bf16[2,32,2048]{2,1,0:T(8,128)(2,1)S(1)}, bf16[2,32,2048]{2,1,0:T(8,128)(2,1)S(1)}, u32[]{:S(2)}, u32[]{:S(2)}) %collective-permute-start.77) | collective-permute-done | bytes 262176 | tf_op jit(solution)/shard_map/ppermute | solution.py:61
  793.3 37.5 %collective-permute-done.95 = bf16[1024,1024]{1,0:T(8,128)(2,1)} collective-permute-done((bf16[1024,1024]{1,0:T(8,128)(2,1)S(1)}, bf16[1024,1024]{1,0:T(8,128)(2,1)}, u32[]{:S(2)}, u32[]{:S(2)}) %collective-permute-start.95) | collective-permute-done | bytes 2097184 | tf_op jit(solution)/shard_map/ppermute | solution.py:61
  835.3 36.5 %collective-permute-done.97 = bf16[1024,1024]{1,0:T(8,128)(2,1)S(1)} collective-permute-done((bf16[1024,1024]{1,0:T(8,128)(2,1)S(1)}, bf16[1024,1024]{1,0:T(8,128)(2,1)S(1)}, u32[]{:S(2)}, u32[]{:S(2)}) %collective-permute-start.97) | collective-permute-done | bytes 2097184 | tf_op jit(solution)/shard_map/ppermute | solution.py:61
  886.5 10.8 fusion.38
  897.5 8.5 multiply_reduce_fusion
  938.5 57.7 %attend_back.1 = (bf16[2048,256]{1,0:T(8,128)(2,1)S(1)}, bf16[2048,256]{1,0:T(8,128)(2,1)S(1)}, bf16[2048,256]{1,0:T(8,128)(2,1)S(1)}) custom-call(bf16[2048,256]{1,0:T(8,128)(2,1)S(1)} %copy-done.10, bf16[2048,256]{1,0:T(8,128)(2,1)S(1)} %get-tuple-element.63.k_ref, bf16[256,2048]{1,0:T(8,128)(2,1)} %copy.186.kt_ref, ...), custom_call_target="tpu_custom_call" | custom-call | flops 21474836480 | bytes 7340032 | tf_op jit(solution)/shard_map/attend_back/pallas_call | solution.py:331
  1020.3 20.4 %collective-permute-done.68 = bf16[32,512]{1,0:T(8,128)(2,1)S(1)} collective-permute-done((bf16[32,512]{1,0:T(8,128)(2,1)S(1)}, bf16[32,512]{1,0:T(8,128)(2,1)S(1)}, u32[]{:S(2)}, u32[]{:S(2)}) %collective-permute-start.68) | collective-permute-done | bytes 32800 | tf_op jit(solution)/shard_map/ppermute | solution.py:61
  1084.3 14.8 %collective-permute-done.55 = bf16[2,2,2,32,1536]{4,3,2,0,1:T(8,128)(2,1)S(1)} collective-permute-done((bf16[2,2,2,32,1536]{4,3,2,0,1:T(8,128)(2,1)S(1)}, bf16[2,2,2,32,1536]{4,3,2,0,1:T(8,128)(2,1)S(1)}, u32[]{:S(2)}, u32[]{:S(2)}) %collective-permute-start.55) | collective-permute-done | bytes 786464 | tf_op jit(solution)/shard_map/ppermute | solution.py:61
  (754 shorter events, 537.3 us)
Async XLA Ops:
  0.7 297.1 %collective-permute-start.45 = (bf16[1,1024,1024]{2,1,0:T(8,128)(2,1)}, bf16[1,1024,1024]{2,1,0:T(8,128)(2,1)}, u32[]{:S(2)}, u32[]{:S(2)}) collective-permute-start(bf16[1,1024,1024]{2,1,0:T(8,128)(2,1)} %param.27), channel_id=1, source_target_pairs={{0,2},{1,3},{2,0},{3,1},{4,6},{5,7},{6,4},{7,5},{8,10},{9,11},{10,... | collective-permute-start | bytes 6291464 | tf_op jit(solution)/shard_map/ppermute | solution.py:61
  9.0 74.8 %collective-permute-start.10 = (bf16[1,32,1536]{2,1,0:T(8,128)(2,1)S(1)}, bf16[1,32,1536]{2,1,0:T(8,128)(2,1)}, u32[]{:S(2)}, u32[]{:S(2)}) collective-permute-start(bf16[1,32,1536]{2,1,0:T(8,128)(2,1)S(1)} %get-tuple-element.79), channel_id=1, source_target_pairs={{0,2},{1,3},{2,0},{3,1},{4,6},{5,7},{6,4},{7,5},{8,10},{9,11},{10,... | collective-permute-start | bytes 294920 | tf_op jit(solution)/shard_map/ppermute | solution.py:61
  190.5 102.0 %all-to-all-start = ((bf16[4,512,768]{1,2,0:T(8,128)(2,1)}), bf16[4,512,768]{1,2,0:T(8,128)(2,1)}, u32[]{:S(2)}, u32[]{:S(2)}) async-start(bf16[4,512,768]{1,2,0:T(8,128)(2,1)} %bitcast.435), calls=%async_computation | async-start | bytes 6291456 | tf_op jit(solution)/shard_map/all_to_all | solution.py:355
  210.5 79.6 %collective-permute-start.28 = (bf16[8,32,2048]{2,1,0:T(8,128)(2,1)S(1)}, bf16[8,32,2048]{2,1,0:T(8,128)(2,1)S(1)}, u32[]{:S(2)}, u32[]{:S(2)}) collective-permute-start(bf16[8,32,2048]{2,1,0:T(8,128)(2,1)S(1)} %pad_maximum_fusion.1), channel_id=1, source_target_pairs={{0,2},{1,3},{2,0},{3,1},{4,6},{5,7},{6,4},{7,5},{8,10},{9,11},{10,... | collective-permute-start | bytes 3145736 | tf_op jit(solution)/shard_map/ppermute | solution.py:61
  213.4 74.0 %collective-permute-start.38 = (bf16[8,128,512]{2,1,0:T(8,128)(2,1)S(1)}, bf16[8,128,512]{2,1,0:T(8,128)(2,1)S(1)}, u32[]{:S(2)}, u32[]{:S(2)}) collective-permute-start(bf16[8,128,512]{2,1,0:T(8,128)(2,1)S(1)} %pad_maximum_fusion.3), channel_id=1, source_target_pairs={{0,2},{1,3},{2,0},{3,1},{4,6},{5,7},{6,4},{7,5},{8,10},{9,11},{10,... | collective-permute-start | bytes 3145736 | tf_op jit(solution)/shard_map/ppermute | solution.py:61
  290.1 85.4 %collective-permute-start.47 = (bf16[1,1024,1024]{2,1,0:T(8,128)(2,1)}, bf16[1,1024,1024]{2,1,0:T(8,128)(2,1)}, u32[]{:S(2)}, u32[]{:S(2)}) collective-permute-start(bf16[1,1024,1024]{2,1,0:T(8,128)(2,1)} %param.28), channel_id=1, source_target_pairs={{0,2},{1,3},{2,0},{3,1},{4,6},{5,7},{6,4},{7,5},{8,10},{9,11},{10,... | collective-permute-start | bytes 6291464 | tf_op jit(solution)/shard_map/ppermute | solution.py:61
  291.5 87.4 %collective-permute-start.29 = (bf16[16,32,2048]{2,1,0:T(8,128)(2,1)}, bf16[16,32,2048]{2,1,0:T(8,128)(2,1)}, u32[]{:S(2)}, u32[]{:S(2)}) collective-permute-start(bf16[16,32,2048]{2,1,0:T(8,128)(2,1)} %constant_dynamic-update-slice_fusion.31.refs_0_), channel_id=1, source_target_pairs={{0,1},{1,0},{2,3},{3,2},{4,5},{5,4},{6,7},{7,6},{8,9},{9,8},{10,11... | collective-permute-start | bytes 6291464 | tf_op jit(solution)/shard_map/ppermute | solution.py:61
  297.2 81.8 %collective-permute-start.34 = (bf16[16,32,2048]{2,1,0:T(8,128)(2,1)}, bf16[16,32,2048]{2,1,0:T(8,128)(2,1)}, u32[]{:S(2)}, u32[]{:S(2)}) collective-permute-start(bf16[16,32,2048]{2,1,0:T(8,128)(2,1)} %constant_dynamic-update-slice_fusion.36.refs_2_), channel_id=1, source_target_pairs={{0,1},{1,0},{2,3},{3,2},{4,5},{5,4},{6,7},{7,6},{8,9},{9,8},{10,11... | collective-permute-start | bytes 6291464 | tf_op jit(solution)/shard_map/ppermute | solution.py:61
  297.7 89.8 %collective-permute-start.39 = (bf16[16,128,512]{2,1,0:T(8,128)(2,1)}, bf16[16,128,512]{2,1,0:T(8,128)(2,1)}, u32[]{:S(2)}, u32[]{:S(2)}) collective-permute-start(bf16[16,128,512]{2,1,0:T(8,128)(2,1)} %constant_dynamic-update-slice_fusion.41.refs_0_), channel_id=1, source_target_pairs={{0,1},{1,0},{2,3},{3,2},{4,5},{5,4},{6,7},{7,6},{8,9},{9,8},{10,11... | collective-permute-start | bytes 6291464 | tf_op jit(solution)/shard_map/ppermute | solution.py:61
  297.8 89.7 %collective-permute-start.44 = (bf16[16,128,512]{2,1,0:T(8,128)(2,1)}, bf16[16,128,512]{2,1,0:T(8,128)(2,1)}, u32[]{:S(2)}, u32[]{:S(2)}) collective-permute-start(bf16[16,128,512]{2,1,0:T(8,128)(2,1)} %constant_dynamic-update-slice_fusion.46.refs_2_), channel_id=1, source_target_pairs={{0,1},{1,0},{2,3},{3,2},{4,5},{5,4},{6,7},{7,6},{8,9},{9,8},{10,11... | collective-permute-start | bytes 6291464 | tf_op jit(solution)/shard_map/ppermute | solution.py:61
  375.4 92.8 %collective-permute-start.46 = (bf16[2,1024,1024]{2,1,0:T(8,128)(2,1)}, bf16[2,1024,1024]{2,1,0:T(8,128)(2,1)}, u32[]{:S(2)}, u32[]{:S(2)}) collective-permute-start(bf16[2,1024,1024]{2,1,0:T(8,128)(2,1)} %constant_dynamic-update-slice_fusion.51.refs_0_), channel_id=1, source_target_pairs={{0,1},{1,0},{2,3},{3,2},{4,5},{5,4},{6,7},{7,6},{8,9},{9,8},{10,11... | collective-permute-start | bytes 12582920 | tf_op jit(solution)/shard_map/ppermute | solution.py:61
  378.9 96.4 %collective-permute-start.48 = (bf16[2,1024,1024]{2,1,0:T(8,128)(2,1)}, bf16[2,1024,1024]{2,1,0:T(8,128)(2,1)}, u32[]{:S(2)}, u32[]{:S(2)}) collective-permute-start(bf16[2,1024,1024]{2,1,0:T(8,128)(2,1)} %constant_dynamic-update-slice_fusion.53.refs_0_), channel_id=1, source_target_pairs={{0,1},{1,0},{2,3},{3,2},{4,5},{5,4},{6,7},{7,6},{8,9},{9,8},{10,11... | collective-permute-start | bytes 12582920 | tf_op jit(solution)/shard_map/ppermute | solution.py:61
  406.4 138.7 %all-to-all-start.2 = ((bf16[8,128,2048]{2,1,0:T(8,128)(2,1)}), bf16[8,128,2048]{2,1,0:T(8,128)(2,1)}, u32[]{:S(2)}, u32[]{:S(2)}) async-start(bf16[8,128,2048]{2,1,0:T(8,128)(2,1)} %bitcast.447), calls=%async_computation.2 | async-start | bytes 8388608 | tf_op jit(solution)/shard_map/all_to_all | solution.py:355
  520.1 128.1 %collective-permute-start.71 = (bf16[2,2,32,2048]{3,2,0,1:T(8,128)(2,1)}, bf16[2,2,32,2048]{3,2,0,1:T(8,128)(2,1)}, u32[]{:S(2)}, u32[]{:S(2)}) collective-permute-start(bf16[2,2,32,2048]{3,2,0,1:T(8,128)(2,1)} %dynamic-slice_bitcast_fusion.13), channel_id=1, source_target_pairs={{0,4},{4,0},{8,12},{12,8},{16,20},{20,16},{24,28},{28,24},{1,5},{5... | collective-permute-start | bytes 1572872 | tf_op jit(solution)/shard_map/ppermute | solution.py:61
  539.4 113.0 %collective-permute-start.86 = (bf16[2,2,128,512]{3,2,1,0:T(8,128)(2,1)}, bf16[2,2,128,512]{3,2,1,0:T(8,128)(2,1)}, u32[]{:S(2)}, u32[]{:S(2)}) collective-permute-start(bf16[2,2,128,512]{3,2,1,0:T(8,128)(2,1)} %dynamic-slice_bitcast_fusion.10), channel_id=1, source_target_pairs={{0,8},{4,12},{8,0},{12,4},{16,24},{20,28},{24,16},{28,20},{1,9},{5... | collective-permute-start | bytes 1572872 | tf_op jit(solution)/shard_map/ppermute | solution.py:61
  543.4 111.8 %collective-permute-start.81 = (bf16[2,2,128,512]{3,2,0,1:T(8,128)(2,1)}, bf16[2,2,128,512]{3,2,0,1:T(8,128)(2,1)}, u32[]{:S(2)}, u32[]{:S(2)}) collective-permute-start(bf16[2,2,128,512]{3,2,0,1:T(8,128)(2,1)} %dynamic-slice_bitcast_fusion.11), channel_id=1, source_target_pairs={{0,4},{4,0},{8,12},{12,8},{16,20},{20,16},{24,28},{28,24},{1,5},{5... | collective-permute-start | bytes 1572872 | tf_op jit(solution)/shard_map/ppermute | solution.py:61
  607.5 166.0 %collective-permute-start.94 = (bf16[2,1024,1024]{2,1,0:T(8,128)(2,1)}, bf16[2,1024,1024]{2,1,0:T(8,128)(2,1)}, u32[]{:S(2)}, u32[]{:S(2)}) collective-permute-start(bf16[2,1024,1024]{2,1,0:T(8,128)(2,1)} %dynamic-slice_bitcast_fusion.1), channel_id=1, source_target_pairs={{0,1},{1,0},{2,3},{3,2},{4,5},{5,4},{6,7},{7,6},{8,9},{9,8},{10,11... | collective-permute-start | bytes 12582920 | tf_op jit(solution)/shard_map/ppermute | solution.py:61
  640.5 141.6 %collective-permute-start.96 = (bf16[2,1024,1024]{2,1,0:T(8,128)(2,1)}, bf16[2,1024,1024]{2,1,0:T(8,128)(2,1)}, u32[]{:S(2)}, u32[]{:S(2)}) collective-permute-start(bf16[2,1024,1024]{2,1,0:T(8,128)(2,1)} %dynamic-slice_bitcast_fusion), channel_id=1, source_target_pairs={{0,1},{1,0},{2,3},{3,2},{4,5},{5,4},{6,7},{7,6},{8,9},{9,8},{10,11... | collective-permute-start | bytes 12582920 | tf_op jit(solution)/shard_map/ppermute | solution.py:61
  643.3 231.4 %all-to-all-start.3 = ((bf16[8,128,2048]{1,2,0:T(8,128)(2,1)}), bf16[8,128,2048]{1,2,0:T(8,128)(2,1)}, u32[]{:S(2)}, u32[]{:S(2)}) async-start(bf16[8,128,2048]{1,2,0:T(8,128)(2,1)} %copy_bitcast_fusion), calls=%async_computation.3 | async-start | bytes 8388608 | tf_op jit(solution)/shard_map/all_to_all | solution.py:355
  648.2 111.4 %collective-permute-start.77 = (bf16[2,32,2048]{2,1,0:T(8,128)(2,1)S(1)}, bf16[2,32,2048]{2,1,0:T(8,128)(2,1)S(1)}, u32[]{:S(2)}, u32[]{:S(2)}) collective-permute-start(bf16[2,32,2048]{2,1,0:T(8,128)(2,1)S(1)} %copy-done.85), channel_id=1, source_target_pairs={{0,16},{4,20},{8,24},{12,28},{16,0},{20,4},{24,8},{28,12},{1,17},{... | collective-permute-start | bytes 786440 | tf_op jit(solution)/shard_map/ppermute | solution.py:61
  652.4 108.1 %collective-permute-start.72 = (bf16[2,32,2048]{2,1,0:T(8,128)(2,1)S(1)}, bf16[2,32,2048]{2,1,0:T(8,128)(2,1)S(1)}, u32[]{:S(2)}, u32[]{:S(2)}) collective-permute-start(bf16[2,32,2048]{2,1,0:T(8,128)(2,1)S(1)} %dynamic-slice_bitcast_fusion.19), channel_id=1, source_target_pairs={{0,8},{4,12},{8,0},{12,4},{16,24},{20,28},{24,16},{28,20},{1,9},{5... | collective-permute-start | bytes 786440 | tf_op jit(solution)/shard_map/ppermute | solution.py:61
  655.2 109.6 %collective-permute-start.87 = (bf16[2,128,512]{2,1,0:T(8,128)(2,1)S(1)}, bf16[2,128,512]{2,1,0:T(8,128)(2,1)S(1)}, u32[]{:S(2)}, u32[]{:S(2)}) collective-permute-start(bf16[2,128,512]{2,1,0:T(8,128)(2,1)S(1)} %dynamic-slice_bitcast_fusion.16), channel_id=1, source_target_pairs={{0,16},{4,20},{8,24},{12,28},{16,0},{20,4},{24,8},{28,12},{1,17},{... | collective-permute-start | bytes 786440 | tf_op jit(solution)/shard_map/ppermute | solution.py:61
  787.0 84.8 %collective-permute-start.97 = (bf16[1024,1024]{1,0:T(8,128)(2,1)S(1)}, bf16[1024,1024]{1,0:T(8,128)(2,1)S(1)}, u32[]{:S(2)}, u32[]{:S(2)}) collective-permute-start(bf16[1024,1024]{1,0:T(8,128)(2,1)S(1)} %dynamic-slice_bitcast_fusion.2), channel_id=1, source_target_pairs={{0,2},{1,3},{2,0},{3,1},{4,6},{5,7},{6,4},{7,5},{8,10},{9,11},{10,... | collective-permute-start | bytes 6291464 | tf_op jit(solution)/shard_map/ppermute | solution.py:61
  927.6 75.6 %collective-permute-start.65 = (bf16[2,2,2,32,512]{4,3,2,0,1:T(8,128)(2,1)S(1)}, bf16[2,2,2,32,512]{4,3,2,0,1:T(8,128)(2,1)}, u32[]{:S(2)}, u32[]{:S(2)}) collective-permute-start(bf16[2,2,2,32,512]{4,3,2,0,1:T(8,128)(2,1)S(1)} %dynamic-slice_bitcast_fusion.20), channel_id=1, source_target_pairs={{0,4},{4,0},{8,12},{12,8},{16,20},{20,16},{24,28},{28,24},{1,5},{5... | collective-permute-start | bytes 786440 | tf_op jit(solution)/shard_map/ppermute | solution.py:61
  (217 other events, 3566.2 us)

commit v2 on v1

v2 whole, which is shorter than its diff:
```python
import functools

import jax
import jax.numpy as jnp
import numpy as np
from jax import lax
from jax.experimental import pallas as pl
from jax.experimental.pallas import tpu as pltpu
from jax.sharding import PartitionSpec as P

HEADS = 16
HEAD_DIM = 64
EPSILON = 1e-05
MASKED = -1e30
HIGHEST = lax.Precision.HIGHEST
BOTH = ("ep", "es")
MIB = 1 << 20


def norm_forward(values, gain, offset):
    average = jnp.mean(values, axis=-1, keepdims=True)
    centred = values - average
    variance = jnp.mean(centred * centred, axis=-1, keepdims=True)
    inverse = lax.rsqrt(variance + EPSILON)
    unit = centred * inverse
    return unit * gain + offset, unit, inverse


def norm_backward(grad, unit, inverse, gain):
    scaled = grad * gain
    mean_scaled = jnp.mean(scaled, axis=-1, keepdims=True)
    mean_unit = jnp.mean(scaled * unit, axis=-1, keepdims=True)
    grad_in = (scaled - mean_scaled - unit * mean_unit) * inverse
    return grad_in, jnp.sum(grad * unit, axis=0), jnp.sum(grad, axis=0)


def gelu_and_slope(values):
    cdf = 0.5 * (1.0 + lax.erf(values * (2.0**-0.5)))
    density = jnp.exp(-0.5 * values * values) * ((2.0 * np.pi) ** -0.5)
    return values * cdf, cdf + values * density


def dot(left, right, contract=((1,), (0,)), out=jnp.float32):
    return lax.dot_general(left, right, (contract, ((), ())), preferred_element_type=out)


def softmax_pair(logits):
    largest = jnp.max(logits, axis=-1, keepdims=True)
    expanded = jnp.exp(logits - largest)
    return expanded / jnp.sum(expanded, axis=-1, keepdims=True)


def digits(axis):
    size = lax.axis_size(axis)
    return [(axis, 1 << b) for b in range(size.bit_length() - 1)]


def exchange(x, digit):
    axis, stride = digit
    size = lax.axis_size(axis)
    return lax.ppermute(x, axis, [(i, i ^ stride) for i in range(size)])


def after(x, *others):
    return lax.optimization_barrier((x, *others))[0]


def weights_of(order):
    inner = 1 << sum(axis == "es" for axis, _ in order)
    return {(axis, stride): stride * (inner if axis == "ep" else 1) for axis, stride in order}


def relative_numbers(order):
    numbers, weights = [0], weights_of(order)
    for digit in order:
        numbers = numbers + [n + weights[digit] for n in numbers]
    return numbers


def gather_pieces(shard, order, hold=None):
    pieces = [shard]
    for number, digit in enumerate(order):
        if number == len(order) - 1 and hold is not None:
            pieces = [after(piece, hold) for piece in pieces]
        pieces = pieces + [exchange(piece, digit) for piece in pieces]
    return pieces


def gather_relative(shard, order, hold=None):
    held = shard[None]
    for number, digit in enumerate(order[:-1]):
        held = jnp.concatenate([held, exchange(held, digit)], axis=0)
        if number == len(order) - 2 and hold is not None:
            held = after(held, hold)
    return held, exchange(held, order[-1])


def place_kernel(plan, outputs, me_ref, *refs):
    sems_in, sems_out = refs[-2:]
    inputs = len(refs) - 2 - outputs - len({step[2] for step in plan})
    outs, held = refs[inputs : inputs + outputs], refs[inputs + outputs : -2]
    me = me_ref[0]
    arriving, leaving = [], []
    for which, row, chain, slot, relative, rows, segments in plan:
        here = held[chain].at[pl.ds(slot * rows, rows), :]
        copy = pltpu.make_async_copy(refs[which].at[row], here, sems_in.at[len(arriving)])
        copy.start()
        arriving.append(copy)
        start = pl.multiple_of((me ^ relative) * rows, rows)
        group = []
        for place, out, first, width in segments:
            group.append(
                pltpu.make_async_copy(
                    held[chain].at[pl.ds(slot * rows, rows), pl.ds(place, width)],
                    outs[out].at[pl.ds(start, rows), pl.ds(first, width)],
                    sems_out.at[sum(map(len, leaving)) + len(group)],
                )
            )
        leaving.append(group)
    for copy, group in zip(arriving, leaving):
        copy.wait()
        for out in group:
            out.start()
    for group in leaving:
        for out in group:
            out.wait()


def gather_rows(shards, chains, me, hold=None):
    rows = shards[0].shape[0]
    count = 1 << len(chains[0][0])
    if rows % 16 or any(w % 128 or f % 128 for _, ranges in chains for _, f, w in ranges):
        axes = tuple(a for a in BOTH if any(d[0] == a for d in chains[0][0]))
        return [lax.all_gather(shard, axes, axis=0, tiled=True) for shard in shards]
    parts, plan, widths = [], [], []
    for chain, (order, ranges) in enumerate(chains):
        numbers = relative_numbers(order)
        segments, place = [], 0
        for index, first, width in ranges:
            segments.append((place, index, first, width))
            place += width
        widths.append(place)
        cut = [shards[index][:, first : first + width] for index, first, width in ranges]
        joined = cut[0] if len(cut) == 1 else jnp.concatenate(cut, axis=1)
        for half, part in enumerate(gather_relative(joined, order, None if chain else hold)):
            for row in range(count // 2):
                slot = half * (count // 2) + row
                plan.append((len(parts), row, chain, slot, numbers[slot], rows, tuple(segments)))
            parts.append(part)
    return pl.pallas_call(
        functools.partial(place_kernel, tuple(plan), len(shards)),
        out_shape=[jax.ShapeDtypeStruct((count * rows, s.shape[1]), s.dtype) for s in shards],
        in_specs=[pl.BlockSpec(memory_space=pltpu.SMEM)] + [pl.BlockSpec(memory_space=pl.ANY)] * len(parts),
        out_specs=[pl.BlockSpec(memory_space=pl.ANY)] * len(shards),
        scratch_shapes=[pltpu.VMEM((count * rows, w), shards[0].dtype) for w in widths]
        + [
            pltpu.SemaphoreType.DMA((len(plan),)),
            pltpu.SemaphoreType.DMA((sum(len(step[-1]) for step in plan),)),
        ],
        compiler_params=pltpu.CompilerParams(vmem_limit_bytes=16 * MIB),
        name="place_rows",
    )(me, *parts)


def fold_pieces(pieces, digit):
    half = len(pieces) // 2
    return [
        kept.astype(jnp.float32) + exchange(sent.astype(jnp.bfloat16), digit).astype(jnp.float32)
        for kept, sent in zip(pieces[:half], pieces[half:])
    ]


def fold_all_but_last(pieces, order):
    for digit in order[:0:-1]:
        pieces = [piece.astype(jnp.bfloat16) for piece in fold_pieces(pieces, digit)]
    return pieces


def sum_pieces(pieces, order):
    for digit in order[::-1]:
        pieces = fold_pieces(pieces, digit)
    return pieces[0]


def scatter_sum(partial, order, hold=None, taps=None):
    count = 1 << len(order)
    rows = partial.shape[0] // count
    remaining = sorted(order, key=weights_of(order).get, reverse=True)
    held = partial.reshape((2,) * len(order) + (rows,) + partial.shape[1:])
    for number, digit in enumerate(order):
        axis, stride = digit
        place = remaining.index(digit)
        remaining.remove(digit)
        bit = (lax.axis_index(axis) // stride) % 2
        mine = lax.dynamic_index_in_dim(held, bit, place, keepdims=False)
        theirs = lax.dynamic_index_in_dim(held, 1 - bit, place, keepdims=False)
        held = mine.astype(jnp.float32) + exchange(theirs, digit).astype(jnp.float32)
        if number < len(order) - 1:
            held = held.astype(jnp.bfloat16)
        if taps is not None:
            taps.append(held)
        if number == 0 and hold is not None:
            held = after(held, *hold)
    return held


def norm_place_kernel(per, me_ref, *refs):
    gain_ref, bias_ref, out_ref = refs[-3:]
    for number, ref in enumerate(refs[:-3]):

        @pl.when(pl.program_id(0) // per == number)
        def _():
            values = ref[...].astype(jnp.float32)
            out_ref[...] = norm_forward(values, gain_ref[...], bias_ref[...])[0].astype(jnp.bfloat16)


def place_normed(pieces, order, me, gain, bias):
    rows, width = pieces[0].shape
    step = min(256, rows)
    per = rows // step
    weights = weights_of(order)

    def target(i, me_ref):
        block = me_ref[0]
        for bit, digit in enumerate(order):
            block = block ^ ((((i // per) >> bit) & 1) * weights[digit])
        return (block * per + i % per, 0)

    def source(number):
        return lambda i, me_ref: (jnp.clip(i - number * per, 0, per - 1), 0)

    line = pl.BlockSpec((1, width), lambda i, me_ref: (0, 0))
    return pl.pallas_call(
        functools.partial(norm_place_kernel, per),
        grid_spec=pltpu.PrefetchScalarGridSpec(
            num_scalar_prefetch=1,
            grid=(len(pieces) * per,),
            in_specs=[pl.BlockSpec((step, width), source(n)) for n in range(len(pieces))] + [line, line],
            out_specs=pl.BlockSpec((step, width), target),
        ),
        out_shape=jax.ShapeDtypeStruct((len(pieces) * rows, width), jnp.bfloat16),
        compiler_params=pltpu.CompilerParams(vmem_limit_bytes=24 * MIB),
        name="norm_place",
    )(me, *pieces, gain, bias)


def head_mask(rows, width, head):
    lane = lax.broadcasted_iota(jnp.int32, (rows, width), 1)
    return (lane // HEAD_DIM) == head


def causal_tile(block):
    key = lax.broadcasted_iota(jnp.int32, (block, block), 0)
    query = lax.broadcasted_iota(jnp.int32, (block, block), 1)
    return key <= query


def flip(dst, src, block):
    for start in range(0, src.shape[0], block):
        dst[:, start : start + block] = src[start : start + block, :].T


def attend_kernel(heads, block, q_ref, k_ref, v_ref, low_ref, full_ref, log_ref, vt, qh, acc, top, total):
    i = pl.program_id(0)
    width = heads * HEAD_DIM

    @pl.when(i == 0)
    def _():
        flip(vt, v_ref, block)

    scaled = q_ref[...] * jnp.asarray(HEAD_DIM**-0.5, jnp.bfloat16)
    for h in range(heads):
        qh[h] = jnp.where(head_mask(block, width, h), scaled, jnp.zeros_like(scaled))
    acc[...] = jnp.zeros_like(acc)
    total[...] = jnp.zeros_like(total)
    top[...] = jnp.full_like(top, MASKED)
    nt = ((1,), (1,))

    def scores(j, h, diagonal):
        s = dot(k_ref[pl.ds(j * block, block), :], qh[h], nt)
        return jnp.where(causal_tile(block), s, MASKED) if diagonal else s

    def find_top(j, diagonal):
        for h in range(heads):
            s = scores(j, h, diagonal)
            folded = jnp.max(s.reshape(block // 8, 8, block), axis=0)
            top[h] = jnp.maximum(top[h], folded)

    def add_block(j, diagonal):
        for h in range(heads):
            s = scores(j, h, diagonal)
            p = jnp.exp(s - top[h, pl.ds(0, 1), :])
            total[h] = total[h] + jnp.sum(p.reshape(block // 8, 8, block), axis=0)
            low = slice(h * HEAD_DIM, (h + 1) * HEAD_DIM)
            acc[low, :] = acc[low, :] + dot(vt[low, pl.ds(j * block, block)], p.astype(jnp.bfloat16))

    @pl.loop(0, i)
    def _(j):
        find_top(j, False)

    find_top(i, True)
    for h in range(heads):
        top[h] = jnp.broadcast_to(jnp.max(top[h], axis=0, keepdims=True), top.shape[1:])

    @pl.loop(0, i)
    def _(j):
        add_block(j, False)

    add_block(i, True)
    for h in range(heads):
        summed = jnp.sum(total[h], axis=0, keepdims=True)
        log_ref[pl.ds(h, 1), :] = top[h, pl.ds(0, 1), :] + jnp.log(summed)
        low = slice(h * HEAD_DIM, (h + 1) * HEAD_DIM)
        acc[low, :] = acc[low, :] / summed
    out = acc[...].T
    full_ref[...] = out
    low_ref[...] = out.astype(jnp.bfloat16)


def column(rows, width, place):
    return pl.BlockSpec((rows, width), lambda i: (0, place))


def attend(qkv):
    rows = qkv.shape[0]
    width = qkv.shape[1] // 3
    heads = width // HEAD_DIM
    block = min(256, rows)
    strip = pl.BlockSpec((block, width), lambda i: (i, 0))
    return pl.pallas_call(
        functools.partial(attend_kernel, heads, block),
        grid=(rows // block,),
        in_specs=[strip, column(rows, width, 1), column(rows, width, 2)],
        out_specs=[strip, strip, pl.BlockSpec((heads, block), lambda i: (0, i))],
        out_shape=[
            jax.ShapeDtypeStruct((rows, width), jnp.bfloat16),
            jax.ShapeDtypeStruct((rows, width), jnp.float32),
            jax.ShapeDtypeStruct((heads, rows), jnp.float32),
        ],
        scratch_shapes=[
            pltpu.VMEM((width, rows), jnp.bfloat16),
            pltpu.VMEM((heads, block, width), jnp.bfloat16),
            pltpu.VMEM((width, block), jnp.float32),
            pltpu.VMEM((heads, 8, block), jnp.float32),
            pltpu.VMEM((heads, 8, block), jnp.float32),
        ],
        compiler_params=pltpu.CompilerParams(vmem_limit_bytes=32 * MIB),
        cost_estimate=pl.CostEstimate(flops=MIB, bytes_accessed=MIB, transcendentals=0),
        name="attend",
    )(qkv, qkv, qkv)


def attend_back_kernel(
    heads, block, q_ref, k_ref, v_ref, g_ref, o_ref, log_ref, out_ref,
    kt, qh, gh, delta, acc, acc_k, acc_v,
):
    i = pl.program_id(0)
    width = heads * HEAD_DIM
    scale = HEAD_DIM**-0.5
    nt = ((1,), (1,))

    @pl.when(i == 0)
    def _():
        flip(kt, k_ref, block)
        acc_k[...] = jnp.zeros_like(acc_k)
        acc_v[...] = jnp.zeros_like(acc_v)

    scaled = q_ref[...] * jnp.asarray(scale, jnp.bfloat16)
    grads = g_ref[...]
    for h in range(heads):
        mask = head_mask(block, width, h)
        qh[pl.ds(h * block, block), :] = jnp.where(mask, scaled, jnp.zeros_like(scaled))
        gh[pl.ds(h * block, block), :] = jnp.where(mask, grads, jnp.zeros_like(grads))
    per_head = (
        lax.broadcasted_iota(jnp.int32, (8, width), 1) // HEAD_DIM
        == lax.broadcasted_iota(jnp.int32, (8, width), 0)
    ).astype(jnp.float32)
    delta[...] = lax.dot_general(
        per_head, grads.astype(jnp.float32) * o_ref[...], (nt, ((), ())), precision=HIGHEST,
        preferred_element_type=jnp.float32,
    )
    acc[...] = jnp.zeros_like(acc)

    def one(j, diagonal):
        at = pl.ds(j * block, block)
        keys, values = k_ref[at, :], v_ref[at, :]
        probs, raws = [], []
        for h in range(heads):
            s = dot(keys, qh[pl.ds(h * block, block), :], nt)
            p = jnp.exp(s - log_ref[pl.ds(h, 1), :])
            if diagonal:
                p = jnp.where(causal_tile(block), p, 0.0)
            dp = dot(values, gh[pl.ds(h * block, block), :], nt)
            raw = (p * (dp - delta[pl.ds(h, 1), :])).astype(jnp.bfloat16)
            low = slice(h * HEAD_DIM, (h + 1) * HEAD_DIM)
            acc[low, :] = acc[low, :] + dot(kt[low, at], raw)
            probs.append(p.astype(jnp.bfloat16))
            raws.append(raw)
        acc_v[at, :] = acc_v[at, :] + dot(jnp.concatenate(probs, axis=1), gh[...])
        acc_k[at, :] = acc_k[at, :] + dot(jnp.concatenate(raws, axis=1), qh[...])

    @pl.loop(0, i)
    def _(j):
        one(j, False)

    one(i, True)
    out_ref[pl.ds(pl.multiple_of(i * block, block), block), :width] = (acc[...].T * scale).astype(jnp.bfloat16)

    @pl.when(i == pl.num_programs(0) - 1)
    def _():
        out_ref[:, width : 2 * width] = acc_k[...].astype(jnp.bfloat16)
        out_ref[:, 2 * width :] = acc_v[...].astype(jnp.bfloat16)


def attend_back(qkv, grad, full, logs):
    rows, width = grad.shape
    heads = width // HEAD_DIM
    block = min(256, rows)
    strip = pl.BlockSpec((block, width), lambda i: (i, 0))
    return pl.pallas_call(
        functools.partial(attend_back_kernel, heads, block),
        grid=(rows // block,),
        in_specs=[
            strip,
            column(rows, width, 1),
            column(rows, width, 2),
            strip,
            strip,
            pl.BlockSpec((heads, block), lambda i: (0, i)),
        ],
        out_specs=pl.BlockSpec((rows, 3 * width), lambda i: (0, 0)),
        out_shape=jax.ShapeDtypeStruct((rows, 3 * width), jnp.bfloat16),
        scratch_shapes=[
            pltpu.VMEM((width, rows), jnp.bfloat16),
            pltpu.VMEM((heads * block, width), jnp.bfloat16),
            pltpu.VMEM((heads * block, width), jnp.bfloat16),
            pltpu.VMEM((8, block), jnp.float32),
            pltpu.VMEM((width, block), jnp.float32),
            pltpu.VMEM((rows, width), jnp.float32),
            pltpu.VMEM((rows, width), jnp.float32),
        ],
        compiler_params=pltpu.CompilerParams(vmem_limit_bytes=48 * MIB),
        cost_estimate=pl.CostEstimate(flops=32 * rows * rows * width * heads // 2, bytes_accessed=14 * rows * width, transcendentals=0),
        name="attend_back",
    )(qkv, qkv, qkv, grad, full, logs)


def swap_groups(x, axis):
    return lax.all_to_all(x, axis, split_axis=0, concat_axis=0, tiled=True)


def on_device(
    tokens,
    cotangent,
    w_qkv,
    w_out,
    w_fc_in,
    w_fc_out,
    norm1_gain,
    norm1_bias,
    norm2_gain,
    norm2_bias,
    coef_weight,
    expert_up,
    expert_down,
    routes,
    keep_mask,
):
    rows, width = tokens.shape
    n_es = lax.axis_size("es")
    n_ep = lax.axis_size("ep")
    me_es = lax.axis_index("es").astype(jnp.int32).reshape(1)
    me_ep = lax.axis_index("ep").astype(jnp.int32).reshape(1)
    ep_up, es_up = digits("ep"), digits("es")
    order_e = es_up[::-1]
    order_z = ep_up[::-1]
    order_y = ep_up[:1] + ep_up[:0:-1]
    group = width // n_es
    stripe = w_qkv.shape[0]
    block = w_fc_out.shape[0]
    units = n_ep * block
    tile = 128

    packed = jnp.concatenate(
        [jnp.stack([norm1_gain, norm1_bias, norm2_gain, norm2_bias]), coef_weight.T], axis=0
    )
    packed = jnp.pad(packed, ((0, stripe - packed.shape[0]), (0, tile - stripe)))
    shared = swap_groups(
        jnp.concatenate(
            [
                w_qkv.reshape(stripe, 3, n_es, group).transpose(2, 0, 1, 3).reshape(n_es, stripe, 3 * group),
                jnp.broadcast_to(packed, (n_es, stripe, tile)),
            ],
            axis=2,
        ),
        "es",
    ).reshape(n_es * stripe, 3 * group + tile)
    own_heads, own_small = shared[:, : 3 * group], shared[:, 3 * group :]
    token_pieces = gather_pieces(after(tokens, shared), order_e)
    by_units = w_fc_in.reshape(stripe, n_ep, n_es, block).transpose(2, 0, 1, 3).reshape(n_es, stripe, units)
    more = swap_groups(
        after(jnp.concatenate([by_units, jnp.broadcast_to(w_out, (n_es, *w_out.shape))], axis=2), shared), "es"
    ).reshape(n_es * stripe, units + width)
    cut = 2 * group
    w_heads, small = gather_rows(
        [own_heads, own_small],
        [(order_z, ((0, 0, cut),)), (order_y, ((0, cut, 3 * group - cut), (1, 0, tile)))],
        me_ep,
        token_pieces[1],
    )
    small = small.reshape(n_ep * n_es, stripe, tile)[:, :6, :stripe].transpose(1, 0, 2).reshape(6, width)
    small = small.astype(jnp.float32)
    gain_one, bias_one, gain_two, bias_two = (small[i : i + 1] for i in range(4))
    coef_full = small[4:6]
    normed_all = place_normed(token_pieces, order_e, me_es, gain_one, bias_one)
    dense_weights = lax.all_gather(
        after(jnp.concatenate([more, w_fc_out], axis=1), w_heads), "ep", axis=0, tiled=True
    )
    w_in, full_out, w_back = (
        dense_weights[:, :units],
        dense_weights[:, units : units + width],
        dense_weights[:, units + width :],
    )
    ups = gather_pieces(after(expert_up[0], token_pieces[1]), order_e)

    inputs = tokens.astype(jnp.float32)
    qkv = after(dot(normed_all, w_heads).astype(jnp.bfloat16), ups[2])
    attended_mine, attended_full, logs = attend(qkv)
    attended_mine = after(attended_mine, ups[1])
    attended = (
        swap_groups(attended_mine.reshape(n_es, rows, group), "es").transpose(1, 0, 2).reshape(rows, width)
    )
    hidden = inputs + dot(attended, full_out)
    normed_two, unit_two, inverse_two = norm_forward(hidden, gain_two, bias_two)
    normed_two_low = normed_two.astype(jnp.bfloat16)
    coefficients = softmax_pair(
        lax.dot_general(normed_two, coef_full, (((1,), (1,)), ((), ())), precision=HIGHEST)
    )
    keep = keep_mask.astype(jnp.float32)[:, None]
    grad_out = cotangent.astype(jnp.float32)
    grad_dense_low = (coefficients[:, 0:1] * grad_out).astype(jnp.bfloat16)
    grad_expert_low = (coefficients[:, 1:2] * keep * grad_out).astype(jnp.bfloat16)

    capacity = 2 * rows // n_ep
    expert_ids = routes[:, 0]
    chosen = (expert_ids[:, None] == lax.broadcasted_iota(jnp.int32, (1, n_ep), 1)).astype(jnp.float32)
    before = (
        lax.broadcasted_iota(jnp.int32, (rows, rows), 1) < lax.broadcasted_iota(jnp.int32, (rows, rows), 0)
    ).astype(jnp.float32)
    ranks = jnp.sum(dot(before, chosen) * chosen, axis=1).astype(jnp.int32)
    slots = expert_ids * capacity + ranks
    in_slot = (slots[None, :] == lax.broadcasted_iota(jnp.int32, (n_ep * capacity, 1), 0)).astype(
        jnp.bfloat16
    )

    def to_experts(values):
        return swap_groups(values.reshape(n_ep, capacity, width), "ep").reshape(n_ep * capacity, width)

    outgoing = dot(in_slot, normed_two_low).astype(jnp.bfloat16)
    downs = gather_pieces(after(expert_down[0], attended), order_e, outgoing)
    full_up, full_down = jnp.concatenate(ups, axis=0), jnp.concatenate(downs, axis=0)
    expert_in = to_experts(outgoing)
    expert_grad = to_experts(
        after(dot(in_slot, grad_expert_low).astype(jnp.bfloat16), expert_in, full_up, downs[1])
    )

    def split_pieces(values):
        return [values[i * rows : (i + 1) * rows] for i in range(n_es)]

    acts, expert_slope = gelu_and_slope(dot(expert_in, full_up, ((1,), (1,))))
    acts = acts.astype(jnp.bfloat16)
    expert_out = dot(acts, full_down).astype(jnp.bfloat16)
    dense_in = jnp.concatenate(gather_pieces(normed_two_low, order_e, acts), axis=0)
    grad_pieces = gather_pieces(grad_dense_low, order_e, expert_out)
    dense_grad = jnp.concatenate(grad_pieces, axis=0)
    inner = dot(after(dense_in, expert_out), w_in)
    activated, slope = gelu_and_slope(inner)
    activated_low = activated.astype(jnp.bfloat16)
    dense_part = dot(activated_low, w_back).astype(jnp.bfloat16)
    dense_folded = fold_all_but_last(split_pieces(dense_part), order_e)
    expert_grad = after(expert_grad, expert_out, dense_part)
    grad_inners = (dot(expert_grad, full_down, ((1,), (1,))) * expert_slope).astype(jnp.bfloat16)
    grad_expert_in = dot(after(grad_inners, dense_folded[1]), full_up).astype(jnp.bfloat16)
    home = swap_groups(
        jnp.stack([v.reshape(n_ep, capacity, width) for v in (expert_out, grad_expert_in)], axis=1), "ep"
    )
    out_home, grad_home = (home[:, i].reshape(n_ep * capacity, width) for i in range(2))

    dense = sum_pieces(dense_folded, order_e[:1])
    grad_inner_low = (dot(after(dense_grad, grad_expert_in), w_back, ((1,), (1,))) * slope).astype(jnp.bfloat16)
    grad_normed_part = dot(after(grad_inner_low, dense), w_in, ((1,), (1,))).astype(jnp.bfloat16)
    grad_normed_folded = fold_all_but_last(split_pieces(grad_normed_part), order_e)
    grad_normed_dense = sum_pieces(grad_normed_folded, order_e[:1])

    def outer_fold(left, right, hold):
        half = left.shape[1] // 2
        sent = exchange(dot(left[:, half:], right, ((0,), (0,))).astype(jnp.bfloat16), order_e[-1])
        kept = dot(left[:, :half], after(right, hold), ((0,), (0,))).astype(jnp.bfloat16)
        size = half // (n_es // 2)
        pieces = [
            (kept[i : i + size].astype(jnp.float32) + sent[i : i + size].astype(jnp.float32)).astype(jnp.bfloat16)
            for i in range(0, half, size)
        ]
        return fold_all_but_last(pieces, order_e[:-1])

    grad_ups = outer_fold(grad_inners, after(expert_in, grad_normed_part), grad_normed_folded[1])
    last_ups = exchange(after(grad_ups[1], grad_normed_dense), order_e[0])
    late_in, late_grad = after(dense_in, *grad_ups), after(dense_grad, *grad_ups)
    grad_w_back = dot(activated_low, late_grad, ((0,), (0,))).astype(jnp.bfloat16)
    grad_w_in = dot(late_in, grad_inner_low, ((0,), (0,))).astype(jnp.bfloat16)
    out_home = after(out_home, last_ups, grad_w_back, grad_w_in)
    expert_tokens = dot(in_slot, out_home, ((0,), (0,))) * keep
    grad_expert_home = dot(in_slot, grad_home, ((0,), (0,)))

    mixed = hidden + coefficients[:, 0:1] * dense + coefficients[:, 1:2] * expert_tokens
    out_tokens = mixed.astype(jnp.bfloat16)
    grad_pair = jnp.concatenate(
        [
            jnp.sum(grad_out * dense, axis=1, keepdims=True),
            jnp.sum(grad_out * expert_tokens, axis=1, keepdims=True),
        ],
        axis=1,
    )
    grad_logits = coefficients * (
        grad_pair - jnp.sum(coefficients * grad_pair, axis=1, keepdims=True)
    )
    grad_coef = lax.dot_general(grad_logits, normed_two, (((0,), (0,)), ((), ())), precision=HIGHEST)
    grad_normed_two = (
        grad_normed_dense
        + grad_expert_home
        + grad_logits[:, 0:1] * coef_full[0:1]
        + grad_logits[:, 1:2] * coef_full[1:2]
    )
    grad_hidden_norm, grad_gain_two, grad_bias_two = norm_backward(
        grad_normed_two, unit_two, inverse_two, gain_two
    )
    grad_hidden = grad_out + grad_hidden_norm
    grad_att_low = grad_hidden.astype(jnp.bfloat16)
    grad_w_out = dot(attended, grad_att_low, ((0,), (0,))).astype(jnp.bfloat16)
    grad_attended = dot(after(grad_att_low, grad_w_out), full_out, ((1,), (1,))).astype(jnp.bfloat16)

    grad_mine = swap_groups(grad_attended.reshape(rows, n_es, group).transpose(1, 0, 2), "es").reshape(
        n_es * rows, group
    )
    grad_downs = outer_fold(acts, after(expert_grad, grad_attended), grad_attended)
    last_downs = exchange(after(grad_downs[1], grad_mine), order_e[0])
    by_es = grad_w_out.reshape(n_ep, n_es, stripe, width).transpose(1, 0, 2, 3)
    out_part = scatter_sum(by_es.reshape(n_es * n_ep * stripe, width), order_e[::-1]).astype(jnp.bfloat16)
    dense_sum = lax.psum_scatter(
        jnp.concatenate([g.reshape(n_ep, -1, width) for g in (out_part, grad_w_in, grad_w_back)], axis=1),
        "ep",
        scatter_dimension=0,
        tiled=True,
    )[0]
    grad_qkv = attend_back(qkv, after(grad_mine, out_part, grad_downs[1]), attended_full, logs)
    grad_ups, grad_downs = (
        pieces[0].astype(jnp.float32) + last.astype(jnp.float32)
        for pieces, last in ((grad_ups, last_ups), (grad_downs, last_downs))
    )
    grad_qkv = after(grad_qkv, last_downs)
    grad_w_heads = dot(normed_all, grad_qkv, ((0,), (0,)))
    column_sums = jnp.sum(grad_qkv.astype(jnp.float32), axis=0, keepdims=True)
    grad_w_heads_low = grad_w_heads.astype(jnp.bfloat16)
    heads_wide = w_heads.astype(jnp.float32)
    grad_bias_one = jnp.sum(heads_wide * column_sums, axis=1)
    grad_gain_one = (jnp.sum(heads_wide * grad_w_heads, axis=1) - bias_one[0] * grad_bias_one) / gain_one[0]
    back_e = order_e[::-1]
    taps = []
    grad_rows = scatter_sum(
        dot(after(grad_qkv, grad_w_heads_low), w_heads, ((1,), (1,))).astype(jnp.bfloat16),
        back_e,
        taps=taps,
    )
    _, unit_one, inverse_one = norm_forward(inputs, gain_one, bias_one)
    grad_inputs_norm, _, _ = norm_backward(grad_rows, unit_one, inverse_one, gain_one)
    grad_tokens = grad_hidden + grad_inputs_norm

    back_z = order_z[::-1]
    small_grads = jnp.stack(
        [grad_gain_one, grad_bias_one, grad_gain_two, grad_bias_two, grad_coef[0], grad_coef[1]]
    )
    small_grads = small_grads.astype(jnp.bfloat16).reshape(6, n_ep, n_es * stripe).transpose(1, 0, 2)
    extra = 16
    small_grads = jnp.pad(small_grads, ((0, 0), (0, extra - 6), (0, 3 * group - n_es * stripe)))
    joined = jnp.concatenate([grad_w_heads_low.reshape(n_ep, n_es * stripe, 3 * group), small_grads], axis=1)
    joined = scatter_sum(joined.reshape(-1, 3 * group), back_z, hold=taps[:1])
    joined = joined.astype(jnp.bfloat16)
    small_sum = joined[n_es * stripe :][:6, : n_es * stripe].reshape(6, n_es, stripe).transpose(1, 0, 2)
    small_sum = jnp.pad(small_sum, ((0, 0), (0, stripe - 6), (0, tile - stripe)))
    cuts = (stripe, stripe + n_es * stripe)
    last = swap_groups(
        jnp.concatenate(
            [
                joined[: n_es * stripe].reshape(n_es, stripe, 3 * group),
                small_sum,
                dense_sum[cuts[0] : cuts[1]].reshape(n_es, stripe, units),
            ],
            axis=2,
        ),
        "es",
    ).astype(jnp.float32)
    cut = 3 * group
    grad_w_qkv = last[:, :, :cut].reshape(n_es, stripe, 3, group).transpose(1, 2, 0, 3).reshape(stripe, 3 * width)
    small_sum = jnp.sum(last[:, :6, cut : cut + stripe], axis=0)
    grad_fc_in = (
        last[:, :, cut + tile :]
        .reshape(n_es, stripe, n_ep, block)
        .transpose(1, 2, 0, 3)
        .reshape(stripe, n_ep * n_es * block)
    )
    return (
        out_tokens,
        grad_tokens,
        grad_w_qkv,
        dense_sum[: cuts[0]].astype(jnp.float32),
        grad_fc_in,
        dense_sum[cuts[1] :].astype(jnp.float32),
        small_sum[0],
        small_sum[1],
        small_sum[2],
        small_sum[3],
        small_sum[4:6].T,
        grad_ups[None],
        grad_downs[None],
    )


def solution(mesh):
    both = P(BOTH)
    table = P(BOTH, None)
    stack = P("ep", "es", None)
    return jax.shard_map(
        on_device,
        mesh=mesh,
        in_specs=(table,) * 6 + (both,) * 4 + (table, stack, stack, table, both),
        out_specs=(table,) * 6 + (both,) * 4 + (table, stack, stack),
        check_vma=False,
    )
```

time: 1130 us -> 729 us (0.65)
  waiting for transfers between devices: 418 us -> 209 us
  local copies, waits for them, and re-layouts: 175 us -> 58.7 us
  starting transfers between devices: 140 us -> 71.1 us
  Pallas kernels: 138 us -> 119 us
  between operations: 3.36 us -> 16 us
    ppermute x98 -> x38, waiting for transfers between devices: 418 us -> 169 us  [exchange(): return lax.ppermute(x, axis, [(i, i ^ stride) for i in range(size)])]
    ppermute x98 -> x38, starting transfers between devices: 102 us -> 36.2 us  [exchange(): return lax.ppermute(x, axis, [(i, i ^ stride) for i in range(size)])]
    unnamed x314 -> x180, local copies, waits for them, and re-layouts: 64.5 us -> 30.2 us
    all_to_all x6 -> x8, waiting for transfers between devices: 0.02 us -> 26.9 us  [swap_groups(): return lax.all_to_all(x, axis, split_axis=0, concat_axis=0, tiled=True)]
    pallas_call x6 -> x2, Pallas kernels: 34 us -> 9.31 us  [the longest x1 6.03 us: place_normed(): pl.pallas_call(functools.partial(norm_place_kernel, per), grid_spec=pltpu...]
    dynamic_slice x20 -> x0, local copies, waits for them, and re-layouts: 19.3 us -> none  [the longest x10 11 us: scatter_sum(): mine = lax.dynamic_index_in_dim(held, bit, place, keepdims=False)]
    concatenate x24 -> x4, other arithmetic: 19.5 us -> 2.05 us  [gather_relative(): held = jnp.concatenate([held, exchange(held, digit)], axis=0)]
    all_gather x0 -> x1, waiting for transfers between devices: none -> 12.6 us  [on_device(): lax.all_gather(after(jnp.concatenate([more, w_fc_out], axis=1), w_heads),...]
  transfers between devices with their start and end apart: 104 -> 48, of which waited for: 38 -> 23; matrix products, arithmetic and copies ran while one was open for 30% -> 28% of each run, Pallas kernels for 12% -> 16%
where the time goes in v2:
time: 729 us; the launch traced here: 719 us
  waiting for transfers between devices  209 us (29%)
  matrix products  179 us (25%)
  Pallas kernels  119 us (16%)
  starting transfers between devices  71.1 us (10%)
  other arithmetic  66.9 us (9%)
  local copies, waits for them, and re-layouts  58.7 us (8%)
  between operations  16 us (2%)
    dot_general x25, matrix products, dot(): lax.dot_general(left, right, (contract, ((), ())), preferred_element_type...  176 us
    ppermute x38, waiting for transfers between devices, exchange(): return lax.ppermute(x, axis, [(i, i ^ stride) for i in range(size)])  169 us
    pallas_call x1, Pallas kernels, attend_back(): pl.pallas_call(functools.partial(attend_back_kernel, heads, block), grid=...  62.5 us
    pallas_call x1, Pallas kernels, attend(): pl.pallas_call(functools.partial(attend_kernel, heads, block), grid=(rows...  47 us
    ppermute x38, starting transfers between devices, exchange(): return lax.ppermute(x, axis, [(i, i ^ stride) for i in range(size)])  36.2 us
    all_to_all x8, starting transfers between devices, swap_groups(): return lax.all_to_all(x, axis, split_axis=0, concat_axis=0, tiled=True)  34.8 us
    unnamed x180, local copies, waits for them, and re-layouts  30.2 us
    all_to_all x8, waiting for transfers between devices, swap_groups(): return lax.all_to_all(x, axis, split_axis=0, concat_axis=0, tiled=True)  26.9 us
  transfers between devices with their start and end apart: 48, of which 23 were waited for; matrix products, arithmetic and copies ran while one was open for 28% of the time, Pallas kernels for 16%

profile of v2, /device:TPU:0, one launch (start us, length us, event | category | flops | bytes accessed | tf_op | source)
XLA Modules:
  0.0 718.7 jit_solution(7333195132079641661)
XLA Ops:
  53.0 8.1 %collective-permute-done.8.refs_3_ = bf16[4,128,384]{2,1,0:T(8,128)(2,1)} collective-permute-done((bf16[4,128,384]{2,1,0:T(8,128)(2,1)S(1)}, bf16[4,128,384]{2,1,0:T(8,128)(2,1)}, u32[]{:S(2)}, u32[]{:S(2)}) %collective-permute-start.8) | collective-permute-done | bytes 393248 | tf_op jit(solution)/shard_map/ppermute | solution.py:61
  83.4 47.0 %attend.1 = (bf16[2048,256]{1,0:T(8,128)(2,1)S(1)}, f32[2048,256]{1,0:T(8,128)S(1)}, f32[4,2048]{1,0:T(4,128)S(1)}) custom-call(bf16[2048,768]{1,0:T(8,128)(2,1)S(1)} %convolution_convert_fusion.3.q_ref.k_ref.v_ref, bf16[2048,768]{1,0:T(8,128)(2,1)S(1)} %convolution_convert_fusion.3.q_ref.k_ref.v_ref, ...), custom_call_target="tpu_custom_call" | custom-call | flops 1048576 | bytes 1048576 | tf_op jit(solution)/shard_map/attend/pallas_call | solution.py:330
  137.5 13.5 %all-to-all-done.1 = bf16[4,512,256]{1,2,0:T(8,128)(2,1)S(1)} async-done(((bf16[4,512,256]{1,2,0:T(8,128)(2,1)}), bf16[4,512,256]{1,2,0:T(8,128)(2,1)S(1)}, u32[]{:S(2)}, u32[]{:S(2)}) %all-to-all-start.1) | async-done | bytes 1048608 | tf_op jit(solution)/shard_map/all_to_all | solution.py:449
  152.0 12.6 %all-gather.2.cloned.1.call-done = bf16[1024,3072]{1,0:T(8,128)(2,1)} async-done(((bf16[128,3072]{1,0:T(8,128)(2,1)}), bf16[1024,3072]{1,0:T(8,128)(2,1)}) %all-gather.2.cloned.1.call-update) | async-done | bytes 6291472 | tf_op jit(solution)/shard_map/all_gather | solution.py:516
  184.7 13.9 %collective-permute-done.15 = bf16[1024,1024]{1,0:T(8,128)(2,1)} collective-permute-done((bf16[1024,1024]{1,0:T(8,128)(2,1)}, bf16[1024,1024]{1,0:T(8,128)(2,1)}, u32[]{:S(2)}, u32[]{:S(2)}) %collective-permute-start.15) | collective-permute-done | bytes 2097184 | tf_op jit(solution)/shard_map/ppermute | solution.py:61
  226.2 15.3 %multiply_convert_fusion = (bf16[1024,4096]{1,0:T(8,128)(2,1)S(1)}, f32[1024,4096]{1,0:T(8,128)}) fusion(bf16[1024,1024]{1,0:T(8,128)(2,1)} %bitcast.22, bf16[4096,1024]{1,0:T(8,128)(2,1)} %constant_dynamic-update-slice_fusion), kind=kOutput, calls=%fused_computation.7 | convolution fusion | flops 8610906112 | bytes 35651584 | tf_op jit(solution)/shard_map/dot_general | solution.py:44
  242.0 14.7 %convolution_convert_fusion.5 = bf16[1024,1024]{1,0:T(8,128)(2,1)} fusion(bf16[1024,4096]{1,0:T(8,128)(2,1)S(1)} %get-tuple-element.134, bf16[4096,1024]{1,0:T(8,128)(2,1)} %constant_dynamic-update-slice_fusion.8), kind=kOutput, calls=%fused_computation.96 | convolution fusion | flops 8590983168 | bytes 18874368 | tf_op jit(solution)/shard_map/dot_general | solution.py:44
  265.6 9.8 %multiply_convert_fusion.1 = (bf16[2048,1024]{1,0:T(8,128)(2,1)S(1)}, f32[2048,1024]{1,0:T(8,128)}) fusion(bf16[2048,1024]{1,0:T(8,128)(2,1)S(1)} %constant_dynamic-update-slice_fusion.4, bf16[1024,3072]{1,0:T(8,128)(2,1)} %all-gather.2.cloned.1.call-done), kind=kOutput, calls=%fused_computation.16 | convolution fusion | flops 4305453056 | bytes 18874368 | tf_op jit(solution)/shard_map/dot_general | solution.py:44
  275.5 7.8 %convolution_convert_fusion.2 = bf16[2048,1024]{1,0:T(8,128)(2,1)S(1)} fusion(bf16[2048,1024]{1,0:T(8,128)(2,1)S(1)} %get-tuple-element.136, bf16[1024,3072]{1,0:T(8,128)(2,1)} %all-gather.2.cloned.1.call-done), kind=kOutput, calls=%fused_computation.50 | convolution fusion | flops 4297064448 | bytes 10485760 | tf_op jit(solution)/shard_map/dot_general | solution.py:44
  290.7 21.5 %collective-permute-done.20 = bf16[512,1024]{1,0:T(8,128)(2,1)S(1)} collective-permute-done((bf16[512,1024]{1,0:T(8,128)(2,1)S(1)}, bf16[512,1024]{1,0:T(8,128)(2,1)S(1)}, u32[]{:S(2)}, u32[]{:S(2)}) %collective-permute-start.20) | collective-permute-done | bytes 1048608 | tf_op jit(solution)/shard_map/ppermute | solution.py:61
  314.1 17.0 %fusion.5 = bf16[1024,4096]{1,0:T(8,128)(2,1)S(1)} fusion(f32[1024,4096]{1,0:T(8,128)} %get-tuple-element.135, bf16[1024,1024]{1,0:T(8,128)(2,1)S(1)} %bitcast.210, bf16[4096,1024]{1,0:T(8,128)(2,1)} %constant_dynamic-update-slice_fusion.8), kind=kOutput, calls=%fused_computation.6 | convolution fusion | flops 8631877632 | bytes 35651584 | tf_op jit(solution)/shard_map/dot_general | solution.py:44
  331.2 14.5 %convolution_convert_fusion.4 = bf16[1024,1024]{1,0:T(8,128)(2,1)S(1)} fusion(bf16[1024,4096]{1,0:T(8,128)(2,1)S(1)} %fusion.5, bf16[4096,1024]{1,0:T(8,128)(2,1)} %constant_dynamic-update-slice_fusion), kind=kOutput, calls=%fused_computation.95 | convolution fusion | flops 8590983168 | bytes 18874368 | tf_op jit(solution)/shard_map/dot_general | solution.py:44
  345.7 10.0 %fusion.11 = bf16[2048,1024]{1,0:T(8,128)(2,1)S(1)} fusion(f32[2048,1024]{1,0:T(8,128)} %get-tuple-element.137, bf16[2048,1024]{1,0:T(8,128)(2,1)S(1)} %copy-done.43, bf16[1024,3072]{1,0:T(8,128)(2,1)} %all-gather.2.cloned.1.call-done), kind=kOutput, calls=%fused_computation.15 | convolution fusion | flops 4315938816 | bytes 18874368 | tf_op jit(solution)/shard_map/dot_general | solution.py:44
  355.8 7.9 %convolution_convert_fusion.1 = bf16[2048,1024]{1,0:T(8,128)(2,1)S(1)} fusion(bf16[2048,1024]{1,0:T(8,128)(2,1)S(1)} %fusion.11, bf16[1024,3072]{1,0:T(8,128)(2,1)} %all-gather.2.cloned.1.call-done), kind=kOutput, calls=%fused_computation.49 | convolution fusion | flops 4297064448 | bytes 10485760 | tf_op jit(solution)/shard_map/dot_general | solution.py:44
  363.7 9.4 %fusion.24 = bf16[2048,1024]{1,0:T(8,128)(2,1)} fusion(bf16[1024,1024]{1,0:T(8,128)(2,1)} %bitcast.22, bf16[1024,4096]{1,0:T(8,128)(2,1)S(1)} %fusion.5), kind=kOutput, calls=%fused_computation.46 | convolution fusion | flops 4297064448 | bytes 10485760 | tf_op jit(solution)/shard_map/dot_general | solution.py:44
  387.0 7.4 %fusion.21 = bf16[2048,1024]{1,0:T(8,128)(2,1)S(1)} fusion(bf16[1024,1024]{1,0:T(8,128)(2,1)} %bitcast.22, bf16[1024,4096]{1,0:T(8,128)(2,1)} %copy-done.79), kind=kOutput, calls=%fused_computation.45 | convolution fusion | flops 4297064448 | bytes 10485760 | tf_op jit(solution)/shard_map/dot_general | solution.py:44
  394.5 16.4 %collective-permute-done.27 = bf16[512,1024]{1,0:T(8,128)(2,1)S(1)} collective-permute-done((bf16[512,1024]{1,0:T(8,128)(2,1)S(1)}, bf16[512,1024]{1,0:T(8,128)(2,1)S(1)}, u32[]{:S(2)}, u32[]{:S(2)}) %collective-permute-start.27) | collective-permute-done | bytes 1048608 | tf_op jit(solution)/shard_map/ppermute | solution.py:61
  419.8 45.7 %collective-permute-done.28 = bf16[1024,1024]{1,0:T(8,128)(2,1)S(1)} collective-permute-done((bf16[1024,1024]{1,0:T(8,128)(2,1)}, bf16[1024,1024]{1,0:T(8,128)(2,1)S(1)}, u32[]{:S(2)}, u32[]{:S(2)}) %collective-permute-start.28) | collective-permute-done | bytes 2097184 | tf_op jit(solution)/shard_map/ppermute | solution.py:61
  518.8 8.7 %fusion.27 = bf16[2048,1024]{1,0:T(8,128)(2,1)} fusion(bf16[1024,1024]{1,0:T(8,128)(2,1)S(1)} %bitcast.212, bf16[1024,4096]{1,0:T(8,128)(2,1)} %copy-done.78), kind=kOutput, calls=%fused_computation.47 | convolution fusion | flops 4297064448 | bytes 10485760 | tf_op jit(solution)/shard_map/dot_general | solution.py:44
  527.5 12.5 %collective-permute-done.30 = bf16[256,1024]{1,0:T(8,128)(2,1)S(1)} collective-permute-done((bf16[256,1024]{1,0:T(8,128)(2,1)S(1)}, bf16[256,1024]{1,0:T(8,128)(2,1)S(1)}, u32[]{:S(2)}, u32[]{:S(2)}) %collective-permute-start.30) | collective-permute-done | bytes 524320 | tf_op jit(solution)/shard_map/ppermute | solution.py:61
  547.8 62.5 %attend_back.1 = bf16[2048,768]{1,0:T(8,128)(2,1)} custom-call(bf16[2048,768]{1,0:T(8,128)(2,1)} %copy-done, bf16[2048,768]{1,0:T(8,128)(2,1)} %copy-done, bf16[2048,768]{1,0:T(8,128)(2,1)} %copy-done, bf16[2048,256]{1,0:T(8,128)(2,1)S(1)} %bitcast.197, f32[2048,256]{1,0:T(8,128)S(1)} %copy-done.11, f32[4,2048]{1,0:T(4,128)S(1)} %get-tuple-element.86.log_ref), custom_call_target="tpu_custom_call" | custom-call | flops 68719476736 | bytes 7340032 | tf_op jit(solution)/shard_map/attend_back/pallas_call | solution.py:420
  613.5 7.0 fusion.34
  633.3 20.0 %collective-permute-done.35 = bf16[2,2,144,768]{3,2,0,1:T(8,128)(2,1)} collective-permute-done((bf16[2,2,144,768]{3,2,0,1:T(8,128)(2,1)S(1)}, bf16[2,2,144,768]{3,2,0,1:T(8,128)(2,1)}, u32[]{:S(2)}, u32[]{:S(2)}) %collective-permute-start.35) | collective-permute-done | bytes 884768 | tf_op jit(solution)/shard_map/ppermute | solution.py:61
  664.0 7.1 collective-permute-done.36
  (397 shorter events, 292.6 us)
Async XLA Ops:
  20.1 26.1 %collective-permute-start = (bf16[512,1024]{1,0:T(8,128)(2,1)S(1)}, bf16[512,1024]{1,0:T(8,128)(2,1)S(1)}, u32[]{:S(2)}, u32[]{:S(2)}) collective-permute-start(bf16[512,1024]{1,0:T(8,128)(2,1)S(1)} %copy-done.1), channel_id=1, source_target_pairs={{0,2},{1,3},{2,0},{3,1},{4,6},{5,7},{6,4},{7,5},{8,10},{9,11},{10,... | collective-permute-start | bytes 3145736 | tf_op jit(solution)/shard_map/ppermute | solution.py:61
  35.6 129.0 %all-gather.2.cloned.1.call-start = ((), (), s32[]{:S(2)}) async-start(), calls=%async_computation.9 | async-start | bytes 7077888 | tf_op jit(solution)/shard_map/all_gather | solution.py:516
  66.3 65.4 %collective-permute-start.10 = (bf16[1024,1024]{1,0:T(8,128)(2,1)}, bf16[1024,1024]{1,0:T(8,128)(2,1)}, u32[]{:S(2)}, u32[]{:S(2)}) collective-permute-start(bf16[1024,1024]{1,0:T(8,128)(2,1)} %bitcast.208), channel_id=1, source_target_pairs={{0,2},{1,3},{2,0},{3,1},{4,6},{5,7},{6,4},{7,5},{8,10},{9,11},{10,... | collective-permute-start | bytes 6291464 | tf_op jit(solution)/shard_map/ppermute | solution.py:61
  137.0 64.6 %collective-permute-start.11 = (bf16[1024,1024]{1,0:T(8,128)(2,1)}, bf16[1024,1024]{1,0:T(8,128)(2,1)}, u32[]{:S(2)}, u32[]{:S(2)}) collective-permute-start(bf16[1024,1024]{1,0:T(8,128)(2,1)} %collective-permute-done.10), channel_id=1, source_target_pairs={{0,1},{1,0},{2,3},{3,2},{4,5},{5,4},{6,7},{7,6},{8,9},{9,8},{10,11... | collective-permute-start | bytes 6291464 | tf_op jit(solution)/shard_map/ppermute | solution.py:61
  151.0 47.6 %collective-permute-start.15 = (bf16[1024,1024]{1,0:T(8,128)(2,1)}, bf16[1024,1024]{1,0:T(8,128)(2,1)}, u32[]{:S(2)}, u32[]{:S(2)}) collective-permute-start(bf16[1024,1024]{1,0:T(8,128)(2,1)} %bitcast.23), channel_id=1, source_target_pairs={{0,2},{1,3},{2,0},{3,1},{4,6},{5,7},{6,4},{7,5},{8,10},{9,11},{10,... | collective-permute-start | bytes 6291464 | tf_op jit(solution)/shard_map/ppermute | solution.py:61
  173.5 52.7 %all-to-all-start.3 = ((bf16[8,128,1024]{2,1,0:T(8,128)(2,1)}), bf16[8,128,1024]{2,1,0:T(8,128)(2,1)}, u32[]{:S(2)}, u32[]{:S(2)}) async-start(bf16[8,128,1024]{2,1,0:T(8,128)(2,1)} %bitcast.214), calls=%async_computation.3 | async-start | bytes 4194304 | tf_op jit(solution)/shard_map/all_to_all | solution.py:449
  181.6 36.5 %collective-permute-start.16 = (bf16[1024,1024]{1,0:T(8,128)(2,1)}, bf16[1024,1024]{1,0:T(8,128)(2,1)S(1)}, u32[]{:S(2)}, u32[]{:S(2)}) collective-permute-start(bf16[1024,1024]{1,0:T(8,128)(2,1)} %bitcast.23), channel_id=1, source_target_pairs={{0,1},{1,0},{2,3},{3,2},{4,5},{5,4},{6,7},{7,6},{8,9},{9,8},{10,11... | collective-permute-start | bytes 6291464 | tf_op jit(solution)/shard_map/ppermute | solution.py:61
  204.8 36.7 %collective-permute-start.12 = (bf16[512,1024]{1,0:T(8,128)(2,1)}, bf16[512,1024]{1,0:T(8,128)(2,1)}, u32[]{:S(2)}, u32[]{:S(2)}) collective-permute-start(bf16[512,1024]{1,0:T(8,128)(2,1)} %fusion.67), channel_id=1, source_target_pairs={{0,2},{1,3},{2,0},{3,1},{4,6},{5,7},{6,4},{7,5},{8,10},{9,11},{10,... | collective-permute-start | bytes 3145736 | tf_op jit(solution)/shard_map/ppermute | solution.py:61
  207.8 75.8 %collective-permute-start.21 = (bf16[512,1024]{1,0:T(8,128)(2,1)S(1)}, bf16[512,1024]{1,0:T(8,128)(2,1)}, u32[]{:S(2)}, u32[]{:S(2)}) collective-permute-start(bf16[512,1024]{1,0:T(8,128)(2,1)S(1)} %fusion.45), channel_id=1, source_target_pairs={{0,2},{1,3},{2,0},{3,1},{4,6},{5,7},{6,4},{7,5},{8,10},{9,11},{10,... | collective-permute-start | bytes 3145736 | tf_op jit(solution)/shard_map/ppermute | solution.py:61
  241.5 22.9 %collective-permute-start.14 = (bf16[512,1024]{1,0:T(8,128)(2,1)}, bf16[512,1024]{1,0:T(8,128)(2,1)}, u32[]{:S(2)}, u32[]{:S(2)}) collective-permute-start(bf16[512,1024]{1,0:T(8,128)(2,1)} %collective-permute-done.12), channel_id=1, source_target_pairs={{0,1},{1,0},{2,3},{3,2},{4,5},{5,4},{6,7},{7,6},{8,9},{9,8},{10,11... | collective-permute-start | bytes 3145736 | tf_op jit(solution)/shard_map/ppermute | solution.py:61
  256.6 57.5 %all-to-all-start.4 = ((bf16[8,128,1024]{2,1,0:T(8,128)(2,1)}), bf16[8,128,1024]{2,1,0:T(8,128)(2,1)S(1)}, u32[]{:S(2)}, u32[]{:S(2)}) async-start(bf16[8,128,1024]{2,1,0:T(8,128)(2,1)} %bitcast.213), calls=%async_computation.4 | async-start | bytes 4194304 | tf_op jit(solution)/shard_map/all_to_all | solution.py:449
  286.6 25.6 %collective-permute-start.20 = (bf16[512,1024]{1,0:T(8,128)(2,1)S(1)}, bf16[512,1024]{1,0:T(8,128)(2,1)S(1)}, u32[]{:S(2)}, u32[]{:S(2)}) collective-permute-start(bf16[512,1024]{1,0:T(8,128)(2,1)S(1)} %add_convert_fusion.7), channel_id=1, source_target_pairs={{0,2},{1,3},{2,0},{3,1},{4,6},{5,7},{6,4},{7,5},{8,10},{9,11},{10,... | collective-permute-start | bytes 3145736 | tf_op jit(solution)/shard_map/ppermute | solution.py:61
  373.0 41.0 %collective-permute-start.25 = (bf16[2048,1024]{1,0:T(8,128)(2,1)}, bf16[2048,1024]{1,0:T(8,128)(2,1)}, u32[]{:S(2)}, u32[]{:S(2)}) collective-permute-start(bf16[2048,1024]{1,0:T(8,128)(2,1)} %fusion.24), channel_id=1, source_target_pairs={{0,1},{1,0},{2,3},{3,2},{4,5},{5,4},{6,7},{7,6},{8,9},{9,8},{10,11... | collective-permute-start | bytes 12582920 | tf_op jit(solution)/shard_map/ppermute | solution.py:61
  377.0 105.9 %all-to-all-start.5 = ((bf16[8,2,128,1024]{3,2,1,0:T(8,128)(2,1)}), bf16[8,2,128,1024]{3,2,1,0:T(8,128)(2,1)}, u32[]{:S(2)}, u32[]{:S(2)}) async-start(bf16[8,2,128,1024]{3,2,1,0:T(8,128)(2,1)} %pad_maximum_fusion.1), calls=%async_computation.5 | async-start | bytes 8388608 | tf_op jit(solution)/shard_map/all_to_all | solution.py:449
  385.3 25.6 %collective-permute-start.27 = (bf16[512,1024]{1,0:T(8,128)(2,1)S(1)}, bf16[512,1024]{1,0:T(8,128)(2,1)S(1)}, u32[]{:S(2)}, u32[]{:S(2)}) collective-permute-start(bf16[512,1024]{1,0:T(8,128)(2,1)S(1)} %add_convert_fusion.6), channel_id=1, source_target_pairs={{0,2},{1,3},{2,0},{3,1},{4,6},{5,7},{6,4},{7,5},{8,10},{9,11},{10,... | collective-permute-start | bytes 3145736 | tf_op jit(solution)/shard_map/ppermute | solution.py:61
  417.9 47.6 %collective-permute-start.28 = (bf16[1024,1024]{1,0:T(8,128)(2,1)}, bf16[1024,1024]{1,0:T(8,128)(2,1)S(1)}, u32[]{:S(2)}, u32[]{:S(2)}) collective-permute-start(bf16[1024,1024]{1,0:T(8,128)(2,1)} %add_convert_fusion.3), channel_id=1, source_target_pairs={{0,2},{1,3},{2,0},{3,1},{4,6},{5,7},{6,4},{7,5},{8,10},{9,11},{10,... | collective-permute-start | bytes 6291464 | tf_op jit(solution)/shard_map/ppermute | solution.py:61
  506.4 36.3 %collective-permute-start.31 = (bf16[2048,1024]{1,0:T(8,128)(2,1)}, bf16[2048,1024]{1,0:T(8,128)(2,1)}, u32[]{:S(2)}, u32[]{:S(2)}) collective-permute-start(bf16[2048,1024]{1,0:T(8,128)(2,1)} %fusion.30), channel_id=1, source_target_pairs={{0,1},{1,0},{2,3},{3,2},{4,5},{5,4},{6,7},{7,6},{8,9},{9,8},{10,11... | collective-permute-start | bytes 12582920 | tf_op jit(solution)/shard_map/ppermute | solution.py:61
  510.8 36.6 %all-to-all-start.6 = ((bf16[4,512,256]{2,1,0:T(8,128)(2,1)}), bf16[4,512,256]{2,1,0:T(8,128)(2,1)S(1)}, u32[]{:S(2)}, u32[]{:S(2)}) async-start(bf16[4,512,256]{2,1,0:T(8,128)(2,1)} %bitcast.204), calls=%async_computation.6 | async-start | bytes 2097152 | tf_op jit(solution)/shard_map/all_to_all | solution.py:449
  514.3 174.6 %reduce-scatter.2.cloned.1.call-start = ((), (), s32[]{:S(2)}) async-start(), calls=%async_computation.10 | async-start | bytes 5308416 | tf_op jit(solution)/shard_map/reduce_scatter | solution.py:649
  517.1 22.9 %collective-permute-start.30 = (bf16[256,1024]{1,0:T(8,128)(2,1)S(1)}, bf16[256,1024]{1,0:T(8,128)(2,1)S(1)}, u32[]{:S(2)}, u32[]{:S(2)}) collective-permute-start(bf16[256,1024]{1,0:T(8,128)(2,1)S(1)} %dynamic-slice_bitcast_fusion.3), channel_id=1, source_target_pairs={{0,2},{1,3},{2,0},{3,1},{4,6},{5,7},{6,4},{7,5},{8,10},{9,11},{10,... | collective-permute-start | bytes 1572872 | tf_op jit(solution)/shard_map/ppermute | solution.py:61
  547.4 62.8 %collective-permute-start.32 = (bf16[1024,1024]{1,0:T(8,128)(2,1)}, bf16[1024,1024]{1,0:T(8,128)(2,1)S(1)}, u32[]{:S(2)}, u32[]{:S(2)}) collective-permute-start(bf16[1024,1024]{1,0:T(8,128)(2,1)} %add_convert_fusion.1), channel_id=1, source_target_pairs={{0,2},{1,3},{2,0},{3,1},{4,6},{5,7},{6,4},{7,5},{8,10},{9,11},{10,... | collective-permute-start | bytes 6291464 | tf_op jit(solution)/shard_map/ppermute | solution.py:61
  627.4 27.2 %collective-permute-start.33 = (bf16[2,512,1024]{2,1,0:T(8,128)(2,1)}, bf16[2,512,1024]{2,1,0:T(8,128)(2,1)}, u32[]{:S(2)}, u32[]{:S(2)}) collective-permute-start(bf16[2,512,1024]{2,1,0:T(8,128)(2,1)} %dynamic-slice_bitcast_fusion), channel_id=1, source_target_pairs={{0,1},{1,0},{2,3},{3,2},{4,5},{5,4},{6,7},{7,6},{8,9},{9,8},{10,11... | collective-permute-start | bytes 6291464 | tf_op jit(solution)/shard_map/ppermute | solution.py:61
  631.0 22.3 %collective-permute-start.35 = (bf16[2,2,144,768]{3,2,0,1:T(8,128)(2,1)S(1)}, bf16[2,2,144,768]{3,2,0,1:T(8,128)(2,1)}, u32[]{:S(2)}, u32[]{:S(2)}) collective-permute-start(bf16[2,2,144,768]{3,2,0,1:T(8,128)(2,1)S(1)} %bitcast.234), channel_id=1, source_target_pairs={{0,4},{4,0},{8,12},{12,8},{16,20},{20,16},{24,28},{28,24},{1,5},{5... | collective-permute-start | bytes 2654216 | tf_op jit(solution)/shard_map/ppermute | solution.py:61
  662.3 24.5 %collective-permute-start.34 = (bf16[512,1024]{1,0:T(8,128)(2,1)}, bf16[512,1024]{1,0:T(8,128)(2,1)}, u32[]{:S(2)}, u32[]{:S(2)}) collective-permute-start(bf16[512,1024]{1,0:T(8,128)(2,1)} %dynamic-slice_bitcast_fusion.1), channel_id=1, source_target_pairs={{0,2},{1,3},{2,0},{3,1},{4,6},{5,7},{6,4},{7,5},{8,10},{9,11},{10,... | collective-permute-start | bytes 3145736 | tf_op jit(solution)/shard_map/ppermute | solution.py:61
  (106 other events, 1335.8 us)
Sparse Core Ops, SparseCore 0:
  66.4 98.2 all-gather.1
  542.8 95.8 reduce-scatter.1

commit v3 on v2

--- a/solution.py
+++ b/solution.py
@@ -249,69 +249,66 @@
     return (lane // HEAD_DIM) == head
 
 
-def causal_tile(block):
-    key = lax.broadcasted_iota(jnp.int32, (block, block), 0)
-    query = lax.broadcasted_iota(jnp.int32, (block, block), 1)
+def causal_tile(keys, queries):
+    key = lax.broadcasted_iota(jnp.int32, (keys, queries), 0)
+    query = lax.broadcasted_iota(jnp.int32, (keys, queries), 1)
     return key <= query
 
 
-def flip(dst, src, block):
+def flip(dst, src):
+    block = min(256, src.shape[0])
     for start in range(0, src.shape[0], block):
         dst[:, start : start + block] = src[start : start + block, :].T
 
 
-def attend_kernel(heads, block, q_ref, k_ref, v_ref, low_ref, full_ref, log_ref, vt, qh, acc, top, total):
+def over_keys(step, query_block, key_block):
     i = pl.program_id(0)
+    per = query_block // key_block
+
+    @pl.loop(0, i * per)
+    def _(j):
+        step(j, 0, False)
+
+    for r in range(per):
+        step(i * per + r, r * key_block, True)
+
+
+def attend_kernel(heads, bq, bk, q_ref, k_ref, v_ref, low_ref, full_ref, log_ref, vt, qh, acc, top, total):
     width = heads * HEAD_DIM
 
-    @pl.when(i == 0)
+    @pl.when(pl.program_id(0) == 0)
     def _():
-        flip(vt, v_ref, block)
+        flip(vt, v_ref)
 
     scaled = q_ref[...] * jnp.asarray(HEAD_DIM**-0.5, jnp.bfloat16)
     for h in range(heads):
-        qh[h] = jnp.where(head_mask(block, width, h), scaled, jnp.zeros_like(scaled))
+        qh[h] = jnp.where(head_mask(bq, width, h), scaled, jnp.zeros_like(scaled))
     acc[...] = jnp.zeros_like(acc)
     total[...] = jnp.zeros_like(total)
     top[...] = jnp.full_like(top, MASKED)
-    nt = ((1,), (1,))
-
-    def scores(j, h, diagonal):
-        s = dot(k_ref[pl.ds(j * block, block), :], qh[h], nt)
-        return jnp.where(causal_tile(block), s, MASKED) if diagonal else s
-
-    def find_top(j, diagonal):
+    one = pl.ds(0, 1)
+
+    def step(j, lo, diagonal):
+        at = pl.ds(j * bk, bk)
+        keys = k_ref[at, :]
         for h in range(heads):
-            s = scores(j, h, diagonal)
-            folded = jnp.max(s.reshape(block // 8, 8, block), axis=0)
-            top[h] = jnp.maximum(top[h], folded)
-
-    def add_block(j, diagonal):
-        for h in range(heads):
-            s = scores(j, h, diagonal)
-            p = jnp.exp(s - top[h, pl.ds(0, 1), :])
-            total[h] = total[h] + jnp.sum(p.reshape(block // 8, 8, block), axis=0)
+            s = dot(keys, qh[h, lo:, :], ((1,), (1,)))
+            if diagonal:
+                s = jnp.where(causal_tile(bk, bq - lo), s, MASKED)
+            old = top[h, one, lo:]
+            new = jnp.maximum(old, jnp.max(s, axis=0, keepdims=True))
+            p = jnp.exp(s - new)
+            shrink = jnp.exp(old - new)
+            top[h, one, lo:] = new
+            total[h, one, lo:] = total[h, one, lo:] * shrink + jnp.sum(p, axis=0, keepdims=True)
             low = slice(h * HEAD_DIM, (h + 1) * HEAD_DIM)
-            acc[low, :] = acc[low, :] + dot(vt[low, pl.ds(j * block, block)], p.astype(jnp.bfloat16))
-
-    @pl.loop(0, i)
-    def _(j):
-        find_top(j, False)
-
-    find_top(i, True)
+            acc[low, lo:] = acc[low, lo:] * shrink + dot(vt[low, at], p.astype(jnp.bfloat16))
+
+    over_keys(step, bq, bk)
     for h in range(heads):
-        top[h] = jnp.broadcast_to(jnp.max(top[h], axis=0, keepdims=True), top.shape[1:])
-
-    @pl.loop(0, i)
-    def _(j):
-        add_block(j, False)
-
-    add_block(i, True)
-    for h in range(heads):
-        summed = jnp.sum(total[h], axis=0, keepdims=True)
-        log_ref[pl.ds(h, 1), :] = top[h, pl.ds(0, 1), :] + jnp.log(summed)
+        log_ref[pl.ds(h, 1), :] = top[h, one, :] + jnp.log(total[h, one, :])
         low = slice(h * HEAD_DIM, (h + 1) * HEAD_DIM)
-        acc[low, :] = acc[low, :] / summed
+        acc[low, :] = acc[low, :] / total[h, one, :]
     out = acc[...].T
     full_ref[...] = out
     low_ref[...] = out.astype(jnp.bfloat16)
@@ -325,13 +322,13 @@
     rows = qkv.shape[0]
     width = qkv.shape[1] // 3
     heads = width // HEAD_DIM
-    block = min(256, rows)
-    strip = pl.BlockSpec((block, width), lambda i: (i, 0))
-    return pl.pallas_call(
-        functools.partial(attend_kernel, heads, block),
-        grid=(rows // block,),
+    bq = bk = min(512, rows)
+    strip = pl.BlockSpec((bq, width), lambda i: (i, 0))
+    return pl.pallas_call(
+        functools.partial(attend_kernel, heads, bq, bk),
+        grid=(rows // bq,),
         in_specs=[strip, column(rows, width, 1), column(rows, width, 2)],
-        out_specs=[strip, strip, pl.BlockSpec((heads, block), lambda i: (0, i))],
+        out_specs=[strip, strip, pl.BlockSpec((heads, bq), lambda i: (0, i))],
         out_shape=[
             jax.ShapeDtypeStruct((rows, width), jnp.bfloat16),
             jax.ShapeDtypeStruct((rows, width), jnp.float32),
@@ -339,19 +336,19 @@
         ],
         scratch_shapes=[
             pltpu.VMEM((width, rows), jnp.bfloat16),
-            pltpu.VMEM((heads, block, width), jnp.bfloat16),
-            pltpu.VMEM((width, block), jnp.float32),
-            pltpu.VMEM((heads, 8, block), jnp.float32),
-            pltpu.VMEM((heads, 8, block), jnp.float32),
-        ],
-        compiler_params=pltpu.CompilerParams(vmem_limit_bytes=32 * MIB),
+            pltpu.VMEM((heads, bq, width), jnp.bfloat16),
+            pltpu.VMEM((width, bq), jnp.float32),
+            pltpu.VMEM((heads, 8, bq), jnp.float32),
+            pltpu.VMEM((heads, 8, bq), jnp.float32),
+        ],
+        compiler_params=pltpu.CompilerParams(vmem_limit_bytes=40 * MIB),
         cost_estimate=pl.CostEstimate(flops=MIB, bytes_accessed=MIB, transcendentals=0),
         name="attend",
     )(qkv, qkv, qkv)
 
 
 def attend_back_kernel(
-    heads, block, q_ref, k_ref, v_ref, g_ref, o_ref, log_ref, out_ref,
+    heads, bq, bk, q_ref, k_ref, v_ref, g_ref, o_ref, log_ref, out_ref,
     kt, qh, gh, delta, acc, acc_k, acc_v,
 ):
     i = pl.program_id(0)
@@ -361,16 +358,16 @@
 
     @pl.when(i == 0)
     def _():
-        flip(kt, k_ref, block)
+        flip(kt, k_ref)
         acc_k[...] = jnp.zeros_like(acc_k)
         acc_v[...] = jnp.zeros_like(acc_v)
 
     scaled = q_ref[...] * jnp.asarray(scale, jnp.bfloat16)
     grads = g_ref[...]
     for h in range(heads):
-        mask = head_mask(block, width, h)
-        qh[pl.ds(h * block, block), :] = jnp.where(mask, scaled, jnp.zeros_like(scaled))
-        gh[pl.ds(h * block, block), :] = jnp.where(mask, grads, jnp.zeros_like(grads))
+        mask = head_mask(bq, width, h)
+        qh[h] = jnp.where(mask, scaled, jnp.zeros_like(scaled))
+        gh[h] = jnp.where(mask, grads, jnp.zeros_like(grads))
     per_head = (
         lax.broadcasted_iota(jnp.int32, (8, width), 1) // HEAD_DIM
         == lax.broadcasted_iota(jnp.int32, (8, width), 0)
@@ -381,30 +378,27 @@
     )
     acc[...] = jnp.zeros_like(acc)
 
-    def one(j, diagonal):
-        at = pl.ds(j * block, block)
+    def step(j, lo, diagonal):
+        at = pl.ds(j * bk, bk)
         keys, values = k_ref[at, :], v_ref[at, :]
-        probs, raws = [], []
+        sum_k = sum_v = 0.0
         for h in range(heads):
-            s = dot(keys, qh[pl.ds(h * block, block), :], nt)
-            p = jnp.exp(s - log_ref[pl.ds(h, 1), :])
+            queries, outer_grads = qh[h, lo:, :], gh[h, lo:, :]
+            s = dot(keys, queries, nt)
+            p = jnp.exp(s - log_ref[pl.ds(h, 1), lo:])
             if diagonal:
-                p = jnp.where(causal_tile(block), p, 0.0)
-            dp = dot(values, gh[pl.ds(h * block, block), :], nt)
-            raw = (p * (dp - delta[pl.ds(h, 1), :])).astype(jnp.bfloat16)
+                p = jnp.where(causal_tile(bk, bq - lo), p, 0.0)
+            dp = dot(values, outer_grads, nt)
+            raw = (p * (dp - delta[pl.ds(h, 1), lo:])).astype(jnp.bfloat16)
             low = slice(h * HEAD_DIM, (h + 1) * HEAD_DIM)
-            acc[low, :] = acc[low, :] + dot(kt[low, at], raw)
-            probs.append(p.astype(jnp.bfloat16))
-            raws.append(raw)
-        acc_v[at, :] = acc_v[at, :] + dot(jnp.concatenate(probs, axis=1), gh[...])
-        acc_k[at, :] = acc_k[at, :] + dot(jnp.concatenate(raws, axis=1), qh[...])
-
-    @pl.loop(0, i)
-    def _(j):
-        one(j, False)
-
-    one(i, True)
-    out_ref[pl.ds(pl.multiple_of(i * block, block), block), :width] = (acc[...].T * scale).astype(jnp.bfloat16)
+            acc[low, lo:] = acc[low, lo:] + dot(kt[low, at], raw)
+            sum_v = sum_v + dot(p.astype(jnp.bfloat16), outer_grads)
+            sum_k = sum_k + dot(raw, queries)
+        acc_v[at, :] = acc_v[at, :] + sum_v
+        acc_k[at, :] = acc_k[at, :] + sum_k
+
+    over_keys(step, bq, bk)
+    out_ref[pl.ds(pl.multiple_of(i * bq, bq), bq), :width] = (acc[...].T * scale).astype(jnp.bfloat16)
 
     @pl.when(i == pl.num_programs(0) - 1)
     def _():
@@ -415,34 +409,221 @@
 def attend_back(qkv, grad, full, logs):
     rows, width = grad.shape
     heads = width // HEAD_DIM
-    block = min(256, rows)
-    strip = pl.BlockSpec((block, width), lambda i: (i, 0))
-    return pl.pallas_call(
-        functools.partial(attend_back_kernel, heads, block),
-        grid=(rows // block,),
+    bq, bk = min(1024, rows), min(256, rows)
+    strip = pl.BlockSpec((bq, width), lambda i: (i, 0))
+    return pl.pallas_call(
+        functools.partial(attend_back_kernel, heads, bq, bk),
+        grid=(rows // bq,),
         in_specs=[
             strip,
             column(rows, width, 1),
             column(rows, width, 2),
             strip,
             strip,
-            pl.BlockSpec((heads, block), lambda i: (0, i)),
+            pl.BlockSpec((heads, bq), lambda i: (0, i)),
         ],
         out_specs=pl.BlockSpec((rows, 3 * width), lambda i: (0, 0)),
         out_shape=jax.ShapeDtypeStruct((rows, 3 * width), jnp.bfloat16),
         scratch_shapes=[
             pltpu.VMEM((width, rows), jnp.bfloat16),
-            pltpu.VMEM((heads * block, width), jnp.bfloat16),
-            pltpu.VMEM((heads * block, width), jnp.bfloat16),
-            pltpu.VMEM((8, block), jnp.float32),
-            pltpu.VMEM((width, block), jnp.float32),
+            pltpu.VMEM((heads, bq, width), jnp.bfloat16),
+            pltpu.VMEM((heads, bq, width), jnp.bfloat16),
+            pltpu.VMEM((8, bq), jnp.float32),
+            pltpu.VMEM((width, bq), jnp.float32),
             pltpu.VMEM((rows, width), jnp.float32),
             pltpu.VMEM((rows, width), jnp.float32),
         ],
-        compiler_params=pltpu.CompilerParams(vmem_limit_bytes=48 * MIB),
-        cost_estimate=pl.CostEstimate(flops=32 * rows * rows * width * heads // 2, bytes_accessed=14 * rows * width, transcendentals=0),
+        compiler_params=pltpu.CompilerParams(vmem_limit_bytes=56 * MIB),
+        cost_estimate=pl.CostEstimate(
+            flops=16 * rows * rows * width * heads, bytes_accessed=14 * rows * width, transcendentals=0
+        ),
         name="attend_back",
     )(qkv, qkv, qkv, grad, full, logs)
+
+
+def product_kernel(contract, left_ref, right_ref, out_ref):
+    out_ref[...] = dot(left_ref[...], right_ref[...], contract).astype(out_ref.dtype)
+
+
+LITTLE = pl.CostEstimate(flops=MIB, bytes_accessed=MIB, transcendentals=0)
+ROOM = pltpu.CompilerParams(vmem_limit_bytes=40 * MIB)
+
+
+def product(left, right, wide, contract=((1,), (0,)), place=0):
+    rows, depth = left.shape
+    tile = min(rows, 256 if depth > 2048 else 512)
+    columns = wide if contract[1] == (0,) else right.shape[0]
+    return pl.pallas_call(
+        functools.partial(product_kernel, contract),
+        grid=(rows // tile,),
+        in_specs=[
+            pl.BlockSpec((tile, depth), lambda i: (i, 0)),
+            pl.BlockSpec((right.shape[0], wide), lambda i: (0, place)),
+        ],
+        out_specs=pl.BlockSpec((tile, columns), lambda i: (i, 0)),
+        out_shape=jax.ShapeDtypeStruct((rows, columns), jnp.bfloat16),
+        compiler_params=ROOM,
+        cost_estimate=LITTLE,
+        name="product",
+    )(left, right)
+
+
+def gelu_product_kernel(left_ref, right_ref, act_ref, slope_ref):
+    act, slope = gelu_and_slope(dot(left_ref[...], right_ref[...]))
+    act_ref[...] = act.astype(jnp.bfloat16)
+    slope_ref[...] = slope
+
+
+def gelu_product(left, right, wide):
+    rows, depth = left.shape
+    tile = min(rows, 256)
+    strip = pl.BlockSpec((tile, wide), lambda i: (i, 0))
+    return pl.pallas_call(
+        gelu_product_kernel,
+        grid=(rows // tile,),
+        in_specs=[pl.BlockSpec((tile, depth), lambda i: (i, 0)), pl.BlockSpec((depth, wide), lambda i: (0, 0))],
+        out_specs=[strip, strip],
+        out_shape=[
+            jax.ShapeDtypeStruct((rows, wide), jnp.bfloat16),
+            jax.ShapeDtypeStruct((rows, wide), jnp.float32),
+        ],
+        compiler_params=ROOM,
+        cost_estimate=LITTLE,
+        name="gelu_product",
+    )(left, right)
+
+
+def slope_product_kernel(left_ref, right_ref, slope_ref, out_ref):
+    out_ref[...] = (dot(left_ref[...], right_ref[...], ((1,), (1,))) * slope_ref[...]).astype(jnp.bfloat16)
+
+
+def slope_product(left, right, slope, wide, place):
+    rows = left.shape[0]
+    tall = right.shape[0]
+    tile = min(rows, 256)
+    return pl.pallas_call(
+        slope_product_kernel,
+        grid=(rows // tile,),
+        in_specs=[
+            pl.BlockSpec((tile, wide), lambda i: (i, 0)),
+            pl.BlockSpec((tall, wide), lambda i: (0, place)),
+            pl.BlockSpec((tile, tall), lambda i: (i, 0)),
+        ],
+        out_specs=pl.BlockSpec((tile, tall), lambda i: (i, 0)),
+        out_shape=jax.ShapeDtypeStruct((rows, tall), jnp.bfloat16),
+        compiler_params=ROOM,
+        cost_estimate=LITTLE,
+        name="slope_product",
+    )(left, right, slope)
+
+
+def pieces_product_kernel(left_ref, *refs):
+    *pieces, out_ref = refs
+    tall = pieces[0].shape[0]
+    total = 0.0
+    for number, piece in enumerate(pieces):
+        total = total + dot(left_ref[:, number * tall : (number + 1) * tall], piece[...])
+    out_ref[...] = total.astype(jnp.bfloat16)
+
+
+def pieces_product(left, pieces):
+    rows, depth = left.shape
+    tall, width = pieces[0].shape
+    tile = min(rows, 256)
+    return pl.pallas_call(
+        pieces_product_kernel,
+        grid=(rows // tile,),
+        in_specs=[pl.BlockSpec((tile, depth), lambda i: (i, 0))]
+        + [pl.BlockSpec((tall, width), lambda i: (0, 0))] * len(pieces),
+        out_specs=pl.BlockSpec((tile, width), lambda i: (i, 0)),
+        out_shape=jax.ShapeDtypeStruct((rows, width), jnp.bfloat16),
+        compiler_params=ROOM,
+        cost_estimate=LITTLE,
+        name="pieces_product",
+    )(left, *pieces)
+
+
+def pieces_slope_kernel(left_ref, slope_ref, *refs):
+    *pieces, out_ref = refs
+    tall = pieces[0].shape[0]
+    for number, piece in enumerate(pieces):
+        place = slice(number * tall, (number + 1) * tall)
+        value = dot(left_ref[...], piece[...], ((1,), (1,))) * slope_ref[:, place]
+        out_ref[:, place] = value.astype(jnp.bfloat16)
+
+
+def pieces_slope_product(left, pieces, slope):
+    rows, width = left.shape
+    tall = pieces[0].shape[0]
+    depth = tall * len(pieces)
+    tile = min(rows, 256)
+    strip = pl.BlockSpec((tile, depth), lambda i: (i, 0))
+    return pl.pallas_call(
+        pieces_slope_kernel,
+        grid=(rows // tile,),
+        in_specs=[pl.BlockSpec((tile, width), lambda i: (i, 0)), strip]
+        + [pl.BlockSpec((tall, width), lambda i: (0, 0))] * len(pieces),
+        out_specs=strip,
+        out_shape=jax.ShapeDtypeStruct((rows, depth), jnp.bfloat16),
+        compiler_params=pltpu.CompilerParams(vmem_limit_bytes=48 * MIB),
+        cost_estimate=LITTLE,
+        name="pieces_slope_product",
+    )(left, slope, *pieces)
+
+
+def outer_kernel(half, left_ref, right_ref, later_ref, first_ref):
+    value = dot(left_ref[...], right_ref[...], ((0,), (0,))).astype(later_ref.dtype)
+
+    @pl.when(pl.program_id(0) < half)
+    def _():
+        later_ref[...] = value
+
+    @pl.when(pl.program_id(0) >= half)
+    def _():
+        first_ref[...] = value
+
+
+def outer_halves(left, right):
+    rows, tall = left.shape
+    width = right.shape[1]
+    tile = min(512, tall // 2)
+    half = tall // 2 // tile
+    shape = jax.ShapeDtypeStruct((tall // 2, width), jnp.bfloat16)
+    return pl.pallas_call(
+        functools.partial(outer_kernel, half),
+        grid=(2 * half,),
+        in_specs=[
+            pl.BlockSpec((rows, tile), lambda i: (0, jnp.where(i < half, i + half, i - half))),
+            pl.BlockSpec((rows, width), lambda i: (0, 0)),
+        ],
+        out_specs=[
+            pl.BlockSpec((tile, width), lambda i: (jnp.minimum(i, half - 1), 0)),
+            pl.BlockSpec((tile, width), lambda i: (jnp.maximum(i - half, 0), 0)),
+        ],
+        out_shape=[shape, shape],
+        compiler_params=ROOM,
+        cost_estimate=LITTLE,
+        name="outer_halves",
+    )(left, right)
+
+
+def outer(left, right):
+    rows, tall = left.shape
+    width = right.shape[1]
+    tile = min(512, tall)
+    return pl.pallas_call(
+        functools.partial(product_kernel, ((0,), (0,))),
+        grid=(tall // tile,),
+        in_specs=[
+            pl.BlockSpec((rows, tile), lambda i: (0, i)),
+            pl.BlockSpec((rows, width), lambda i: (0, 0)),
+        ],
+        out_specs=pl.BlockSpec((tile, width), lambda i: (i, 0)),
+        out_shape=jax.ShapeDtypeStruct((tall, width), jnp.bfloat16),
+        compiler_params=ROOM,
+        cost_estimate=LITTLE,
+        name="outer",
+    )(left, right)
 
 
 def swap_groups(x, axis):
@@ -516,11 +697,7 @@
     dense_weights = lax.all_gather(
         after(jnp.concatenate([more, w_fc_out], axis=1), w_heads), "ep", axis=0, tiled=True
     )
-    w_in, full_out, w_back = (
-        dense_weights[:, :units],
-        dense_weights[:, units : units + width],
-        dense_weights[:, units + width :],
-    )
+    full_out = dense_weights[:, units : units + width]
     ups = gather_pieces(after(expert_up[0], token_pieces[1]), order_e)
 
     inputs = tokens.astype(jnp.float32)
@@ -558,7 +735,7 @@
 
     outgoing = dot(in_slot, normed_two_low).astype(jnp.bfloat16)
     downs = gather_pieces(after(expert_down[0], attended), order_e, outgoing)
-    full_up, full_down = jnp.concatenate(ups, axis=0), jnp.concatenate(downs, axis=0)
+    full_up = jnp.concatenate(ups, axis=0)
     expert_in = to_experts(outgoing)
     expert_grad = to_experts(
         after(dot(in_slot, grad_expert_low).astype(jnp.bfloat16), expert_in, full_up, downs[1])
@@ -569,46 +746,52 @@
 
     acts, expert_slope = gelu_and_slope(dot(expert_in, full_up, ((1,), (1,))))
     acts = acts.astype(jnp.bfloat16)
-    expert_out = dot(acts, full_down).astype(jnp.bfloat16)
+    expert_out = pieces_product(acts, downs)
     dense_in = jnp.concatenate(gather_pieces(normed_two_low, order_e, acts), axis=0)
-    grad_pieces = gather_pieces(grad_dense_low, order_e, expert_out)
-    dense_grad = jnp.concatenate(grad_pieces, axis=0)
-    inner = dot(after(dense_in, expert_out), w_in)
-    activated, slope = gelu_and_slope(inner)
-    activated_low = activated.astype(jnp.bfloat16)
-    dense_part = dot(activated_low, w_back).astype(jnp.bfloat16)
+    dense_grad = jnp.concatenate(gather_pieces(grad_dense_low, order_e, acts), axis=0)
+    expert_grad = after(expert_grad, expert_out, dense_in, dense_grad)
+    grad_inners = pieces_slope_product(expert_grad, downs, expert_slope)
+    grad_expert_in = product(grad_inners, full_up, width)
+    out_home = to_experts(after(expert_out, expert_grad))
+
+    activated_low, slope = gelu_product(after(dense_in, grad_expert_in), dense_weights, units)
+    dense_part = product(activated_low, dense_weights, width, place=2)
+    grad_home = to_experts(after(grad_expert_in, out_home, dense_part))
     dense_folded = fold_all_but_last(split_pieces(dense_part), order_e)
-    expert_grad = after(expert_grad, expert_out, dense_part)
-    grad_inners = (dot(expert_grad, full_down, ((1,), (1,))) * expert_slope).astype(jnp.bfloat16)
-    grad_expert_in = dot(after(grad_inners, dense_folded[1]), full_up).astype(jnp.bfloat16)
-    home = swap_groups(
-        jnp.stack([v.reshape(n_ep, capacity, width) for v in (expert_out, grad_expert_in)], axis=1), "ep"
-    )
-    out_home, grad_home = (home[:, i].reshape(n_ep * capacity, width) for i in range(2))
-
     dense = sum_pieces(dense_folded, order_e[:1])
-    grad_inner_low = (dot(after(dense_grad, grad_expert_in), w_back, ((1,), (1,))) * slope).astype(jnp.bfloat16)
-    grad_normed_part = dot(after(grad_inner_low, dense), w_in, ((1,), (1,))).astype(jnp.bfloat16)
+    grad_inner_low = slope_product(after(dense_grad, dense_part), dense_weights, slope, width, 2)
+    grad_normed_part = product(grad_inner_low, dense_weights, units, ((1,), (1,)))
     grad_normed_folded = fold_all_but_last(split_pieces(grad_normed_part), order_e)
     grad_normed_dense = sum_pieces(grad_normed_folded, order_e[:1])
 
-    def outer_fold(left, right, hold):
-        half = left.shape[1] // 2
-        sent = exchange(dot(left[:, half:], right, ((0,), (0,))).astype(jnp.bfloat16), order_e[-1])
-        kept = dot(left[:, :half], after(right, hold), ((0,), (0,))).astype(jnp.bfloat16)
+    def outer_fold(later, kept):
+        half = later.shape[0]
         size = half // (n_es // 2)
         pieces = [
-            (kept[i : i + size].astype(jnp.float32) + sent[i : i + size].astype(jnp.float32)).astype(jnp.bfloat16)
+            (
+                kept[i : i + size].astype(jnp.float32)
+                + exchange(later[i : i + size], order_e[-1]).astype(jnp.float32)
+            ).astype(jnp.bfloat16)
             for i in range(0, half, size)
         ]
         return fold_all_but_last(pieces, order_e[:-1])
 
-    grad_ups = outer_fold(grad_inners, after(expert_in, grad_normed_part), grad_normed_folded[1])
-    last_ups = exchange(after(grad_ups[1], grad_normed_dense), order_e[0])
-    late_in, late_grad = after(dense_in, *grad_ups), after(dense_grad, *grad_ups)
-    grad_w_back = dot(activated_low, late_grad, ((0,), (0,))).astype(jnp.bfloat16)
-    grad_w_in = dot(late_in, grad_inner_low, ((0,), (0,))).astype(jnp.bfloat16)
-    out_home = after(out_home, last_ups, grad_w_back, grad_w_in)
+    later_ups, kept_ups = outer_halves(grad_inners, after(expert_in, grad_normed_part, dense_folded[1]))
+    later_downs, kept_downs = outer_halves(acts, after(expert_grad, later_ups))
+    grad_w_back = outer(activated_low, after(dense_grad, later_downs, grad_normed_folded[1]))
+    grad_w_in = outer(after(dense_in, later_downs), grad_inner_low)
+    grad_home = after(grad_home, later_downs, grad_w_back, grad_w_in, dense, grad_normed_dense)
+    out_home = after(out_home, grad_home)
+    grad_ups = outer_fold(later_ups, after(kept_ups, grad_home))
+    grad_downs = outer_fold(later_downs, after(kept_downs, grad_home))
+    dense_sum = lax.psum_scatter(
+        after(
+            jnp.concatenate([g.reshape(n_ep, -1, width) for g in (grad_w_in, grad_w_back)], axis=1), grad_home
+        ),
+        "ep",
+        scatter_dimension=0,
+        tiled=True,
+    )[0]
     expert_tokens = dot(in_slot, out_home, ((0,), (0,))) * keep
     grad_expert_home = dot(in_slot, grad_home, ((0,), (0,)))
 
@@ -636,46 +819,40 @@
     )
     grad_hidden = grad_out + grad_hidden_norm
     grad_att_low = grad_hidden.astype(jnp.bfloat16)
-    grad_w_out = dot(attended, grad_att_low, ((0,), (0,))).astype(jnp.bfloat16)
-    grad_attended = dot(after(grad_att_low, grad_w_out), full_out, ((1,), (1,))).astype(jnp.bfloat16)
+    grad_attended = dot(grad_att_low, full_out, ((1,), (1,))).astype(jnp.bfloat16)
 
     grad_mine = swap_groups(grad_attended.reshape(rows, n_es, group).transpose(1, 0, 2), "es").reshape(
         n_es * rows, group
     )
-    grad_downs = outer_fold(acts, after(expert_grad, grad_attended), grad_attended)
+    grad_w_out = dot(attended, after(grad_att_low, grad_attended), ((0,), (0,))).astype(jnp.bfloat16)
+    by_es = grad_w_out.reshape(n_ep, n_es, stripe, width).transpose(1, 0, 2, 3)
+    taps = []
+    out_part = scatter_sum(by_es.reshape(n_es * n_ep * stripe, width), order_e[::-1], taps=taps).astype(jnp.bfloat16)
+    grad_mine = after(grad_mine, grad_downs[1], taps[0])
     last_downs = exchange(after(grad_downs[1], grad_mine), order_e[0])
-    by_es = grad_w_out.reshape(n_ep, n_es, stripe, width).transpose(1, 0, 2, 3)
-    out_part = scatter_sum(by_es.reshape(n_es * n_ep * stripe, width), order_e[::-1]).astype(jnp.bfloat16)
-    dense_sum = lax.psum_scatter(
-        jnp.concatenate([g.reshape(n_ep, -1, width) for g in (out_part, grad_w_in, grad_w_back)], axis=1),
-        "ep",
-        scatter_dimension=0,
-        tiled=True,
-    )[0]
-    grad_qkv = attend_back(qkv, after(grad_mine, out_part, grad_downs[1]), attended_full, logs)
+    grad_qkv = attend_back(qkv, after(grad_mine, grad_downs[1]), attended_full, logs)
+    last_ups = exchange(after(grad_ups[1], grad_qkv), order_e[0])
     grad_ups, grad_downs = (
         pieces[0].astype(jnp.float32) + last.astype(jnp.float32)
         for pieces, last in ((grad_ups, last_ups), (grad_downs, last_downs))
     )
     grad_qkv = after(grad_qkv, last_downs)
-    grad_w_heads = dot(normed_all, grad_qkv, ((0,), (0,)))
+    taps = []
+    back_e = order_e[::-1]
+    grad_rows_part = dot(grad_qkv, w_heads, ((1,), (1,))).astype(jnp.bfloat16)
+    grad_rows = scatter_sum(grad_rows_part, back_e, taps=taps)
+    grad_w_heads = dot(normed_all, after(grad_qkv, grad_rows_part), ((0,), (0,)))
     column_sums = jnp.sum(grad_qkv.astype(jnp.float32), axis=0, keepdims=True)
     grad_w_heads_low = grad_w_heads.astype(jnp.bfloat16)
     heads_wide = w_heads.astype(jnp.float32)
     grad_bias_one = jnp.sum(heads_wide * column_sums, axis=1)
     grad_gain_one = (jnp.sum(heads_wide * grad_w_heads, axis=1) - bias_one[0] * grad_bias_one) / gain_one[0]
-    back_e = order_e[::-1]
-    taps = []
-    grad_rows = scatter_sum(
-        dot(after(grad_qkv, grad_w_heads_low), w_heads, ((1,), (1,))).astype(jnp.bfloat16),
-        back_e,
-        taps=taps,
-    )
     _, unit_one, inverse_one = norm_forward(inputs, gain_one, bias_one)
     grad_inputs_norm, _, _ = norm_backward(grad_rows, unit_one, inverse_one, gain_one)
     grad_tokens = grad_hidden + grad_inputs_norm
 
     back_z = order_z[::-1]
+    back_y = [order_z[1], order_z[-1], *order_z[2:-1], order_z[0]] if len(order_z) > 2 else back_z
     small_grads = jnp.stack(
         [grad_gain_one, grad_bias_one, grad_gain_two, grad_bias_two, grad_coef[0], grad_coef[1]]
     )
@@ -683,17 +860,25 @@
     extra = 16
     small_grads = jnp.pad(small_grads, ((0, 0), (0, extra - 6), (0, 3 * group - n_es * stripe)))
     joined = jnp.concatenate([grad_w_heads_low.reshape(n_ep, n_es * stripe, 3 * group), small_grads], axis=1)
-    joined = scatter_sum(joined.reshape(-1, 3 * group), back_z, hold=taps[:1])
+    by_columns = out_part.reshape(n_ep, stripe, n_es, group).transpose(0, 2, 1, 3).reshape(n_ep, -1, group)
+    by_columns = jnp.pad(by_columns, ((0, 0), (0, extra), (0, 0)))
+    joined = jnp.concatenate([joined, by_columns], axis=2).reshape(-1, 4 * group)
+    cut = 2 * group
+    joined = jnp.concatenate(
+        [scatter_sum(joined[:, :cut], back_z, hold=taps[:1]), scatter_sum(joined[:, cut:], back_y)], axis=1
+    )
+    grad_w_out = (
+        joined[: n_es * stripe, 3 * group :].reshape(n_es, stripe, group).transpose(1, 0, 2).reshape(stripe, width)
+    )
     joined = joined.astype(jnp.bfloat16)
     small_sum = joined[n_es * stripe :][:6, : n_es * stripe].reshape(6, n_es, stripe).transpose(1, 0, 2)
     small_sum = jnp.pad(small_sum, ((0, 0), (0, stripe - 6), (0, tile - stripe)))
-    cuts = (stripe, stripe + n_es * stripe)
     last = swap_groups(
         jnp.concatenate(
             [
-                joined[: n_es * stripe].reshape(n_es, stripe, 3 * group),
+                joined[: n_es * stripe, : 3 * group].reshape(n_es, stripe, 3 * group),
                 small_sum,
-                dense_sum[cuts[0] : cuts[1]].reshape(n_es, stripe, units),
+                dense_sum[: n_es * stripe].reshape(n_es, stripe, units),
             ],
             axis=2,
         ),
@@ -712,9 +897,9 @@
         out_tokens,
         grad_tokens,
         grad_w_qkv,
-        dense_sum[: cuts[0]].astype(jnp.float32),
+        grad_w_out,
         grad_fc_in,
-        dense_sum[cuts[1] :].astype(jnp.float32),
+        dense_sum[n_es * stripe :].astype(jnp.float32),
         small_sum[0],
         small_sum[1],
         small_sum[2],

time: 729 us -> 681 us (0.934)
  matrix products: 179 us -> 60.9 us
  Pallas kernels: 119 us -> 184 us
  waiting for transfers between devices: 209 us -> 183 us
  local copies, waits for them, and re-layouts: 58.7 us -> 80 us
  starting transfers between devices: 71.1 us -> 81.3 us
    dot_general x25 -> x12, matrix products: 176 us -> 58 us  [dot(): lax.dot_general(left, right, (contract, ((), ())), preferred_element_type...]
    pallas_call x2 -> x13, Pallas kernels: 109 us -> 175 us  [the longest x1 38 us: attend_back(): pl.pallas_call(functools.partial(attend_back_kernel, heads, bq, bk), grid...]
    ppermute x38 -> x43, waiting for transfers between devices: 169 us -> 127 us  [exchange(): return lax.ppermute(x, axis, [(i, i ^ stride) for i in range(size)])]
    all_gather x1, waiting for transfers between devices: 12.6 us -> 30.5 us  [on_device(): lax.all_gather(after(jnp.concatenate([more, w_fc_out], axis=1), w_heads),...]
    unnamed x180 -> x142, local copies, waits for them, and re-layouts: 30.2 us -> 45.6 us
    all_to_all x8 -> x9, starting transfers between devices: 34.8 us -> 41.8 us  [swap_groups(): return lax.all_to_all(x, axis, split_axis=0, concat_axis=0, tiled=True)]
    ppermute x38 -> x43, starting transfers between devices: 36.2 us -> 39.5 us  [exchange(): return lax.ppermute(x, axis, [(i, i ^ stride) for i in range(size)])]
    all_to_all x8 -> x9, waiting for transfers between devices: 26.9 us -> 25.2 us  [swap_groups(): return lax.all_to_all(x, axis, split_axis=0, concat_axis=0, tiled=True)]
  transfers between devices with their start and end apart: 48 -> 54, of which waited for: 23 -> 22; matrix products, arithmetic and copies ran while one was open for 28% -> 24% of each run, Pallas kernels for 16% -> 27%
where the time goes in v3:
time: 681 us; the launch traced here: 671 us
  Pallas kernels  184 us (27%)
  waiting for transfers between devices  183 us (27%)
  starting transfers between devices  81.3 us (12%)
  local copies, waits for them, and re-layouts  80 us (12%)
  other arithmetic  65.5 us (10%)
  matrix products  60.9 us (9%)
  between operations  15.6 us (2%)
    ppermute x43, waiting for transfers between devices, exchange(): return lax.ppermute(x, axis, [(i, i ^ stride) for i in range(size)])  127 us
    dot_general x12, matrix products, dot(): lax.dot_general(left, right, (contract, ((), ())), preferred_element_type...  58 us
    unnamed x142, local copies, waits for them, and re-layouts  45.6 us
    all_to_all x9, starting transfers between devices, swap_groups(): return lax.all_to_all(x, axis, split_axis=0, concat_axis=0, tiled=True)  41.8 us
    ppermute x43, starting transfers between devices, exchange(): return lax.ppermute(x, axis, [(i, i ^ stride) for i in range(size)])  39.5 us
    pallas_call x1, Pallas kernels, attend_back(): pl.pallas_call(functools.partial(attend_back_kernel, heads, bq, bk), grid...  38 us
    all_gather x1, waiting for transfers between devices, on_device(): lax.all_gather(after(jnp.concatenate([more, w_fc_out], axis=1), w_heads),...  30.5 us
    pallas_call x3, Pallas kernels, product(): pl.pallas_call(functools.partial(product_kernel, contract), grid=(rows //...  27.8 us
  transfers between devices with their start and end apart: 54, of which 22 were waited for; matrix products, arithmetic and copies ran while one was open for 24% of the time, Pallas kernels for 27%

profile of v3, /device:TPU:0, one launch (start us, length us, event | category | flops | bytes accessed | tf_op | source)
XLA Modules:
  0.0 671.0 jit_solution(1884090373061931359)
XLA Ops:
  53.0 8.0 %collective-permute-done.8.refs_3_ = bf16[4,128,384]{2,1,0:T(8,128)(2,1)} collective-permute-done((bf16[4,128,384]{2,1,0:T(8,128)(2,1)S(1)}, bf16[4,128,384]{2,1,0:T(8,128)(2,1)}, u32[]{:S(2)}, u32[]{:S(2)}) %collective-permute-start.8) | collective-permute-done | bytes 393248 | tf_op jit(solution)/shard_map/ppermute | solution.py:61
  83.3 24.0 %attend.1 = (bf16[2048,256]{1,0:T(8,128)(2,1)S(1)}, f32[2048,256]{1,0:T(8,128)S(1)}, f32[4,2048]{1,0:T(4,128)S(1)}) custom-call(bf16[2048,768]{1,0:T(8,128)(2,1)S(1)} %convolution_convert_fusion.1.q_ref.k_ref.v_ref, bf16[2048,768]{1,0:T(8,128)(2,1)S(1)} %convolution_convert_fusion.1.q_ref.k_ref.v_ref, ...), custom_call_target="tpu_custom_call" | custom-call | flops 1048576 | bytes 1048576 | tf_op jit(solution)/shard_map/attend/pallas_call | solution.py:327
  120.6 13.5 %all-to-all-done.1 = bf16[4,512,256]{1,2,0:T(8,128)(2,1)S(1)} async-done(((bf16[4,512,256]{1,2,0:T(8,128)(2,1)}), bf16[4,512,256]{1,2,0:T(8,128)(2,1)S(1)}, u32[]{:S(2)}, u32[]{:S(2)}) %all-to-all-start.1) | async-done | bytes 1048608 | tf_op jit(solution)/shard_map/all_to_all | solution.py:630
  134.1 30.5 %all-gather.2.cloned.1.call-done.right_ref = bf16[1024,3072]{1,0:T(8,128)(2,1)} async-done(((bf16[128,3072]{1,0:T(8,128)(2,1)}), bf16[1024,3072]{1,0:T(8,128)(2,1)}) %all-gather.2.cloned.1.call-update) | async-done | bytes 6291472 | tf_op jit(solution)/shard_map/all_gather | solution.py:697
  196.7 30.1 %collective-permute-done.15.refs_1_ = bf16[1024,1024]{1,0:T(8,128)(2,1)} collective-permute-done((bf16[1024,1024]{1,0:T(8,128)(2,1)}, bf16[1024,1024]{1,0:T(8,128)(2,1)}, u32[]{:S(2)}, u32[]{:S(2)}) %collective-permute-start.15) | collective-permute-done | bytes 2097184 | tf_op jit(solution)/shard_map/ppermute | solution.py:61
  230.9 6.3 all-to-all-start.4
  237.2 18.9 %fusion.3 = (f32[1024,4096]{1,0:T(8,128)}, bf16[1024,4096]{1,0:T(8,128)(2,1)}) fusion(bf16[1024,1024]{1,0:T(8,128)(2,1)} %bitcast.194, bf16[4096,1024]{1,0:T(8,128)(2,1)} %constant_dynamic-update-slice_fusion.right_ref), kind=kOutput, calls=%fused_computation.4 | convolution fusion | flops 8631877632 | bytes 35651584 | tf_op jit(solution)/shard_map/dot_general | solution.py:44
  256.6 13.5 %collective-permute-done.18 = bf16[512,1024]{1,0:T(8,128)(2,1)} collective-permute-done((bf16[512,1024]{1,0:T(8,128)(2,1)}, bf16[512,1024]{1,0:T(8,128)(2,1)}, u32[]{:S(2)}, u32[]{:S(2)}) %collective-permute-start.18) | collective-permute-done | bytes 1048608 | tf_op jit(solution)/shard_map/ppermute | solution.py:61
  270.6 13.4 %pieces_product.1 = bf16[1024,1024]{1,0:T(8,128)(2,1)S(1)} custom-call(bf16[1024,4096]{1,0:T(8,128)(2,1)} %get-tuple-element.124.left_ref, bf16[1024,1024]{1,0:T(8,128)(2,1)} %bitcast.25.refs_0_, bf16[1024,1024]{1,0:T(8,128)(2,1)} %collective-permute-done.15.refs_1_, bf16[1024,1024]{1,0:T(8,128)(2,1)} %collective-permute-done.16.refs_2_, ...), custom_call_target="tpu_custom_call" | custom-call | flops 1048576 | bytes 1048576 | tf_op jit(solution)/shard_map/pieces_product/pallas_call | solution.py:533
  299.9 16.2 %pieces_slope_product.1.left_ref = bf16[1024,4096]{1,0:T(8,128)(2,1)} custom-call(bf16[1024,1024]{1,0:T(8,128)(2,1)S(1)} %bitcast.192, f32[1024,4096]{1,0:T(8,128)} %get-tuple-element.123.slope_ref, bf16[1024,1024]{1,0:T(8,128)(2,1)} %bitcast.25.refs_0_, bf16[1024,1024]{1,0:T(8,128)(2,1)} %collective-permute-done.15.refs_1_, ...), custom_call_target="tpu_custom_call" | custom-call | flops 1048576 | bytes 1048576 | tf_op jit(solution)/shard_map/pieces_slope_product/pallas_call | solution.py:561
  319.5 12.9 %product.3 = bf16[1024,1024]{1,0:T(8,128)(2,1)S(1)} custom-call(bf16[1024,4096]{1,0:T(8,128)(2,1)S(1)} %copy-done, bf16[4096,1024]{1,0:T(8,128)(2,1)} %constant_dynamic-update-slice_fusion.right_ref), custom_call_target="tpu_custom_call" | custom-call | flops 1048576 | bytes 1048576 | tf_op jit(solution)/shard_map/product/pallas_call | solution.py:456
  333.8 10.9 %gelu_product.1 = (bf16[2048,1024]{1,0:T(8,128)(2,1)S(1)}, f32[2048,1024]{1,0:T(8,128)}) custom-call(bf16[2048,1024]{1,0:T(8,128)(2,1)S(1)} %copy-done.7, bf16[1024,3072]{1,0:T(8,128)(2,1)} %all-gather.2.cloned.1.call-done.right_ref), custom_call_target="tpu_custom_call" | custom-call | flops 1048576 | bytes 1048576 | tf_op jit(solution)/shard_map/gelu_product/pallas_call | solution.py:481
  344.6 6.6 product.4
  355.4 6.2 all-to-all-start.6
  365.0 9.6 %slope_product.1.left_ref.right_ref = bf16[2048,1024]{1,0:T(8,128)(2,1)S(1)} custom-call(bf16[2048,1024]{1,0:T(8,128)(2,1)S(1)} %copy-done.10, bf16[1024,3072]{1,0:T(8,128)(2,1)} %all-gather.2.cloned.1.call-done.right_ref, f32[2048,1024]{1,0:T(8,128)} %get-tuple-element.85.slope_ref), custom_call_target="tpu_custom_call" | custom-call | flops 1048576 | bytes 1048576 | tf_op jit(solution)/shard_map/slope_product/pallas_call | solution.py:504
  374.6 8.3 %product.5 = bf16[2048,1024]{1,0:T(8,128)(2,1)S(1)} custom-call(bf16[2048,1024]{1,0:T(8,128)(2,1)S(1)} %slope_product.1.left_ref.right_ref, bf16[1024,3072]{1,0:T(8,128)(2,1)} %all-gather.2.cloned.1.call-done.right_ref), custom_call_target="tpu_custom_call" | custom-call | flops 1048576 | bytes 1048576 | tf_op jit(solution)/shard_map/product/pallas_call | solution.py:456
  391.9 12.3 %outer_halves.2 = (bf16[2048,1024]{1,0:T(8,128)(2,1)S(1)}, bf16[2048,1024]{1,0:T(8,128)(2,1)S(1)}) custom-call(bf16[1024,4096]{1,0:T(8,128)(2,1)} %pieces_slope_product.1.left_ref, bf16[1024,1024]{1,0:T(8,128)(2,1)S(1)} %bitcast.195), custom_call_target="tpu_custom_call" | custom-call | flops 1048576 | bytes 1048576 | tf_op jit(solution)/shard_map/outer_halves/pallas_call | solution.py:592
  408.2 12.5 %outer_halves.3 = (bf16[2048,1024]{1,0:T(8,128)(2,1)S(1)}, bf16[2048,1024]{1,0:T(8,128)(2,1)S(1)}) custom-call(bf16[1024,4096]{1,0:T(8,128)(2,1)} %get-tuple-element.124.left_ref, bf16[1024,1024]{1,0:T(8,128)(2,1)S(1)} %bitcast.193), custom_call_target="tpu_custom_call" | custom-call | flops 1048576 | bytes 1048576 | tf_op jit(solution)/shard_map/outer_halves/pallas_call | solution.py:592
  454.0 6.0 fusion.24
  499.2 38.0 %attend_back.1 = bf16[2048,768]{1,0:T(8,128)(2,1)} custom-call(bf16[2048,768]{1,0:T(8,128)(2,1)} %copy-done.3, bf16[2048,768]{1,0:T(8,128)(2,1)} %copy-done.3, bf16[2048,768]{1,0:T(8,128)(2,1)} %copy-done.3, bf16[2048,256]{1,0:T(8,128)(2,1)} %bitcast.226, f32[2048,256]{1,0:T(8,128)} %copy-done.37, f32[4,2048]{1,0:T(4,128)} %copy-done.41), custom_call_target="tpu_custom_call" | custom-call | flops 68719476736 | bytes 7340032 | tf_op jit(solution)/shard_map/attend_back/pallas_call | solution.py:414
  541.2 15.8 %collective-permute-done.29 = bf16[1024,1024]{1,0:T(8,128)(2,1)} collective-permute-done((bf16[1024,1024]{1,0:T(8,128)(2,1)}, bf16[1024,1024]{1,0:T(8,128)(2,1)}, u32[]{:S(2)}, u32[]{:S(2)}) %collective-permute-start.29) | collective-permute-done | bytes 2097184 | tf_op jit(solution)/shard_map/ppermute | solution.py:61
  580.4 20.2 %collective-permute-done.41 = bf16[1024,1024]{1,0:T(8,128)(2,1)} collective-permute-done((bf16[1024,1024]{1,0:T(8,128)(2,1)}, bf16[1024,1024]{1,0:T(8,128)(2,1)}, u32[]{:S(2)}, u32[]{:S(2)}) %collective-permute-start.41) | collective-permute-done | bytes 2097184 | tf_op jit(solution)/shard_map/ppermute | solution.py:61
  622.6 7.0 %collective-permute-done.38 = bf16[144,512]{1,0:T(8,128)(2,1)S(1)} collective-permute-done((bf16[144,512]{1,0:T(8,128)(2,1)S(1)}, bf16[144,512]{1,0:T(8,128)(2,1)S(1)}, u32[]{:S(2)}, u32[]{:S(2)}) %collective-permute-start.38) | collective-permute-done | bytes 147488 | tf_op jit(solution)/shard_map/ppermute | solution.py:61
  632.2 7.0 %collective-permute-done.31 = bf16[512,1024]{1,0:T(8,128)(2,1)} collective-permute-done((bf16[512,1024]{1,0:T(8,128)(2,1)}, bf16[512,1024]{1,0:T(8,128)(2,1)}, u32[]{:S(2)}, u32[]{:S(2)}) %collective-permute-start.31) | collective-permute-done | bytes 1048608 | tf_op jit(solution)/shard_map/ppermute | solution.py:61
  (378 shorter events, 307.5 us)
Async XLA Ops:
  35.6 129.0 %all-gather.2.cloned.1.call-start = ((), (), s32[]{:S(2)}) async-start(), calls=%async_computation.10 | async-start | bytes 7077888 | tf_op jit(solution)/shard_map/all_gather | solution.py:697
  66.3 48.4 %collective-permute-start.10 = (bf16[1024,1024]{1,0:T(8,128)(2,1)}, bf16[1024,1024]{1,0:T(8,128)(2,1)}, u32[]{:S(2)}, u32[]{:S(2)}) collective-permute-start(bf16[1024,1024]{1,0:T(8,128)(2,1)} %bitcast.213), channel_id=1, source_target_pairs={{0,2},{1,3},{2,0},{3,1},{4,6},{5,7},{6,4},{7,5},{8,10},{9,11},{10,... | collective-permute-start | bytes 6291464 | tf_op jit(solution)/shard_map/ppermute | solution.py:61
  120.1 68.6 %collective-permute-start.11 = (bf16[1024,1024]{1,0:T(8,128)(2,1)}, bf16[1024,1024]{1,0:T(8,128)(2,1)}, u32[]{:S(2)}, u32[]{:S(2)}) collective-permute-start(bf16[1024,1024]{1,0:T(8,128)(2,1)} %collective-permute-done.10), channel_id=1, source_target_pairs={{0,1},{1,0},{2,3},{3,2},{4,5},{5,4},{6,7},{7,6},{8,9},{9,8},{10,11... | collective-permute-start | bytes 6291464 | tf_op jit(solution)/shard_map/ppermute | solution.py:61
  174.1 55.4 %all-to-all-start.3 = ((bf16[8,128,1024]{2,1,0:T(8,128)(2,1)}), bf16[8,128,1024]{2,1,0:T(8,128)(2,1)S(1)}, u32[]{:S(2)}, u32[]{:S(2)}) async-start(bf16[8,128,1024]{2,1,0:T(8,128)(2,1)} %bitcast.216), calls=%async_computation.3 | async-start | bytes 4194304 | tf_op jit(solution)/shard_map/all_to_all | solution.py:630
  177.9 48.9 %collective-permute-start.15 = (bf16[1024,1024]{1,0:T(8,128)(2,1)}, bf16[1024,1024]{1,0:T(8,128)(2,1)}, u32[]{:S(2)}, u32[]{:S(2)}) collective-permute-start(bf16[1024,1024]{1,0:T(8,128)(2,1)} %bitcast.25.refs_0_), channel_id=1, source_target_pairs={{0,2},{1,3},{2,0},{3,1},{4,6},{5,7},{6,4},{7,5},{8,10},{9,11},{10,... | collective-permute-start | bytes 6291464 | tf_op jit(solution)/shard_map/ppermute | solution.py:61
  191.9 64.3 %collective-permute-start.12 = (bf16[512,1024]{1,0:T(8,128)(2,1)}, bf16[512,1024]{1,0:T(8,128)(2,1)}, u32[]{:S(2)}, u32[]{:S(2)}) collective-permute-start(bf16[512,1024]{1,0:T(8,128)(2,1)} %fusion.39), channel_id=1, source_target_pairs={{0,2},{1,3},{2,0},{3,1},{4,6},{5,7},{6,4},{7,5},{8,10},{9,11},{10,... | collective-permute-start | bytes 3145736 | tf_op jit(solution)/shard_map/ppermute | solution.py:61
  195.2 74.8 %collective-permute-start.18 = (bf16[512,1024]{1,0:T(8,128)(2,1)}, bf16[512,1024]{1,0:T(8,128)(2,1)}, u32[]{:S(2)}, u32[]{:S(2)}) collective-permute-start(bf16[512,1024]{1,0:T(8,128)(2,1)} %fusion.23), channel_id=1, source_target_pairs={{0,2},{1,3},{2,0},{3,1},{4,6},{5,7},{6,4},{7,5},{8,10},{9,11},{10,... | collective-permute-start | bytes 3145736 | tf_op jit(solution)/shard_map/ppermute | solution.py:61
  196.7 73.4 %collective-permute-start.16 = (bf16[1024,1024]{1,0:T(8,128)(2,1)}, bf16[1024,1024]{1,0:T(8,128)(2,1)}, u32[]{:S(2)}, u32[]{:S(2)}) collective-permute-start(bf16[1024,1024]{1,0:T(8,128)(2,1)} %bitcast.25.refs_0_), channel_id=1, source_target_pairs={{0,1},{1,0},{2,3},{3,2},{4,5},{5,4},{6,7},{7,6},{8,9},{9,8},{10,11... | collective-permute-start | bytes 6291464 | tf_op jit(solution)/shard_map/ppermute | solution.py:61
  226.8 43.8 %collective-permute-start.17 = (bf16[1024,1024]{1,0:T(8,128)(2,1)}, bf16[1024,1024]{1,0:T(8,128)(2,1)}, u32[]{:S(2)}, u32[]{:S(2)}) collective-permute-start(bf16[1024,1024]{1,0:T(8,128)(2,1)} %collective-permute-done.15.refs_1_), channel_id=1, source_target_pairs={{0,1},{1,0},{2,3},{3,2},{4,5},{5,4},{6,7},{7,6},{8,9},{9,8},{10,11... | collective-permute-start | bytes 6291464 | tf_op jit(solution)/shard_map/ppermute | solution.py:61
  230.9 63.5 %all-to-all-start.4 = ((bf16[8,128,1024]{2,1,0:T(8,128)(2,1)}), bf16[8,128,1024]{2,1,0:T(8,128)(2,1)S(1)}, u32[]{:S(2)}, u32[]{:S(2)}) async-start(bf16[8,128,1024]{2,1,0:T(8,128)(2,1)} %bitcast.215), calls=%async_computation.4 | async-start | bytes 4194304 | tf_op jit(solution)/shard_map/all_to_all | solution.py:630
  294.3 61.1 %all-to-all-start.5 = ((bf16[8,128,1024]{2,1,0:T(8,128)(2,1)}), bf16[8,128,1024]{2,1,0:T(8,128)(2,1)}, u32[]{:S(2)}, u32[]{:S(2)}) async-start(bf16[8,128,1024]{2,1,0:T(8,128)(2,1)} %bitcast.197), calls=%async_computation.5 | async-start | bytes 4194304 | tf_op jit(solution)/shard_map/all_to_all | solution.py:630
  355.4 98.6 %all-to-all-start.6 = ((bf16[8,128,1024]{2,1,0:T(8,128)(2,1)}), bf16[8,128,1024]{2,1,0:T(8,128)(2,1)}, u32[]{:S(2)}, u32[]{:S(2)}) async-start(bf16[8,128,1024]{2,1,0:T(8,128)(2,1)} %bitcast.196), calls=%async_computation.6 | async-start | bytes 4194304 | tf_op jit(solution)/shard_map/all_to_all | solution.py:630
  386.9 57.0 %collective-permute-start.21 = (bf16[512,1024]{1,0:T(8,128)(2,1)}, bf16[512,1024]{1,0:T(8,128)(2,1)}, u32[]{:S(2)}, u32[]{:S(2)}) collective-permute-start(bf16[512,1024]{1,0:T(8,128)(2,1)} %get-tuple-element.132), channel_id=1, source_target_pairs={{0,1},{1,0},{2,3},{3,2},{4,5},{5,4},{6,7},{7,6},{8,9},{9,8},{10,11... | collective-permute-start | bytes 3145736 | tf_op jit(solution)/shard_map/ppermute | solution.py:61
  386.9 61.3 %collective-permute-start.25 = (bf16[512,1024]{1,0:T(8,128)(2,1)}, bf16[512,1024]{1,0:T(8,128)(2,1)}, u32[]{:S(2)}, u32[]{:S(2)}) collective-permute-start(bf16[512,1024]{1,0:T(8,128)(2,1)} %get-tuple-element.130), channel_id=1, source_target_pairs={{0,1},{1,0},{2,3},{3,2},{4,5},{5,4},{6,7},{7,6},{8,9},{9,8},{10,11... | collective-permute-start | bytes 3145736 | tf_op jit(solution)/shard_map/ppermute | solution.py:61
  390.4 53.5 %collective-permute-start.23 = (bf16[512,1024]{1,0:T(8,128)(2,1)}, bf16[512,1024]{1,0:T(8,128)(2,1)}, u32[]{:S(2)}, u32[]{:S(2)}) collective-permute-start(bf16[512,1024]{1,0:T(8,128)(2,1)} %add_convert_fusion.7), channel_id=1, source_target_pairs={{0,2},{1,3},{2,0},{3,1},{4,6},{5,7},{6,4},{7,5},{8,10},{9,11},{10,... | collective-permute-start | bytes 3145736 | tf_op jit(solution)/shard_map/ppermute | solution.py:61
  428.5 144.7 %collective-permute-start.42 = (bf16[1024,1024]{1,0:T(8,128)(2,1)}, bf16[1024,1024]{1,0:T(8,128)(2,1)}, u32[]{:S(2)}, u32[]{:S(2)}) collective-permute-start(bf16[1024,1024]{1,0:T(8,128)(2,1)} %get-tuple-element.126), channel_id=1, source_target_pairs={{0,1},{1,0},{2,3},{3,2},{4,5},{5,4},{6,7},{7,6},{8,9},{9,8},{10,11... | collective-permute-start | bytes 6291464 | tf_op jit(solution)/shard_map/ppermute | solution.py:61
  443.9 39.5 %collective-permute-start.27 = (bf16[1024,1024]{1,0:T(8,128)(2,1)}, bf16[1024,1024]{1,0:T(8,128)(2,1)}, u32[]{:S(2)}, u32[]{:S(2)}) collective-permute-start(bf16[1024,1024]{1,0:T(8,128)(2,1)} %get-tuple-element.127), channel_id=1, source_target_pairs={{0,1},{1,0},{2,3},{3,2},{4,5},{5,4},{6,7},{7,6},{8,9},{9,8},{10,11... | collective-permute-start | bytes 6291464 | tf_op jit(solution)/shard_map/ppermute | solution.py:61
  443.9 136.5 %collective-permute-start.39 = (bf16[1024,1024]{1,0:T(8,128)(2,1)}, bf16[1024,1024]{1,0:T(8,128)(2,1)}, u32[]{:S(2)}, u32[]{:S(2)}) collective-permute-start(bf16[1024,1024]{1,0:T(8,128)(2,1)} %get-tuple-element.128), channel_id=1, source_target_pairs={{0,1},{1,0},{2,3},{3,2},{4,5},{5,4},{6,7},{7,6},{8,9},{9,8},{10,11... | collective-permute-start | bytes 6291464 | tf_op jit(solution)/shard_map/ppermute | solution.py:61
  448.2 41.4 %collective-permute-start.40 = (bf16[1024,1024]{1,0:T(8,128)(2,1)}, bf16[1024,1024]{1,0:T(8,128)(2,1)}, u32[]{:S(2)}, u32[]{:S(2)}) collective-permute-start(bf16[1024,1024]{1,0:T(8,128)(2,1)} %get-tuple-element.129), channel_id=1, source_target_pairs={{0,1},{1,0},{2,3},{3,2},{4,5},{5,4},{6,7},{7,6},{8,9},{9,8},{10,11... | collective-permute-start | bytes 6291464 | tf_op jit(solution)/shard_map/ppermute | solution.py:61
  482.6 158.7 %reduce-scatter.2.cloned.1.call-start = ((), (), s32[]{:S(2)}) async-start(), calls=%async_computation.11 | async-start | bytes 4718592 | tf_op jit(solution)/shard_map/reduce_scatter | solution.py:787
  497.1 40.5 %collective-permute-start.32 = (bf16[256,1024]{1,0:T(8,128)(2,1)S(1)}, bf16[256,1024]{1,0:T(8,128)(2,1)S(1)}, u32[]{:S(2)}, u32[]{:S(2)}) collective-permute-start(bf16[256,1024]{1,0:T(8,128)(2,1)S(1)} %dynamic-slice_bitcast_fusion.4), channel_id=1, source_target_pairs={{0,2},{1,3},{2,0},{3,1},{4,6},{5,7},{6,4},{7,5},{8,10},{9,11},{10,... | collective-permute-start | bytes 1572872 | tf_op jit(solution)/shard_map/ppermute | solution.py:61
  497.5 59.5 %collective-permute-start.29 = (bf16[1024,1024]{1,0:T(8,128)(2,1)}, bf16[1024,1024]{1,0:T(8,128)(2,1)}, u32[]{:S(2)}, u32[]{:S(2)}) collective-permute-start(bf16[1024,1024]{1,0:T(8,128)(2,1)} %add_convert_fusion.3), channel_id=1, source_target_pairs={{0,2},{1,3},{2,0},{3,1},{4,6},{5,7},{6,4},{7,5},{8,10},{9,11},{10,... | collective-permute-start | bytes 6291464 | tf_op jit(solution)/shard_map/ppermute | solution.py:61
  537.2 63.4 %collective-permute-start.41 = (bf16[1024,1024]{1,0:T(8,128)(2,1)}, bf16[1024,1024]{1,0:T(8,128)(2,1)}, u32[]{:S(2)}, u32[]{:S(2)}) collective-permute-start(bf16[1024,1024]{1,0:T(8,128)(2,1)} %add_convert_fusion.1), channel_id=1, source_target_pairs={{0,2},{1,3},{2,0},{3,1},{4,6},{5,7},{6,4},{7,5},{8,10},{9,11},{10,... | collective-permute-start | bytes 6291464 | tf_op jit(solution)/shard_map/ppermute | solution.py:61
  569.8 39.0 %collective-permute-start.30 = (bf16[2,512,1024]{2,1,0:T(8,128)(2,1)}, bf16[2,512,1024]{2,1,0:T(8,128)(2,1)}, u32[]{:S(2)}, u32[]{:S(2)}) collective-permute-start(bf16[2,512,1024]{2,1,0:T(8,128)(2,1)} %dynamic-slice_bitcast_fusion), channel_id=1, source_target_pairs={{0,1},{1,0},{2,3},{3,2},{4,5},{5,4},{6,7},{7,6},{8,9},{9,8},{10,11... | collective-permute-start | bytes 6291464 | tf_op jit(solution)/shard_map/ppermute | solution.py:61
  (95 other events, 996.5 us)
Sparse Core Ops, SparseCore 0:
  66.3 98.2 all-gather.1
  487.1 89.9 reduce-scatter.1

commit v4 on v3

--- a/solution.py
+++ b/solution.py
@@ -182,7 +182,7 @@
     return pieces[0]
 
 
-def scatter_sum(partial, order, hold=None, taps=None):
+def scatter_sum(partial, order, hold=None, taps=None, beside=None):
     count = 1 << len(order)
     rows = partial.shape[0] // count
     remaining = sorted(order, key=weights_of(order).get, reverse=True)
@@ -194,6 +194,8 @@
         bit = (lax.axis_index(axis) // stride) % 2
         mine = lax.dynamic_index_in_dim(held, bit, place, keepdims=False)
         theirs = lax.dynamic_index_in_dim(held, 1 - bit, place, keepdims=False)
+        if beside is not None and number == len(order) - 1:
+            mine = after(mine, beside())
         held = mine.astype(jnp.float32) + exchange(theirs, digit).astype(jnp.float32)
         if number < len(order) - 1:
             held = held.astype(jnp.bfloat16)
@@ -571,40 +573,40 @@
     )(left, slope, *pieces)
 
 
-def outer_kernel(half, left_ref, right_ref, later_ref, first_ref):
-    value = dot(left_ref[...], right_ref[...], ((0,), (0,))).astype(later_ref.dtype)
-
-    @pl.when(pl.program_id(0) < half)
-    def _():
-        later_ref[...] = value
-
-    @pl.when(pl.program_id(0) >= half)
-    def _():
-        first_ref[...] = value
-
-
-def outer_halves(left, right):
+def outer_kernel(per, left_ref, right_ref, *outs):
+    value = dot(left_ref[...], right_ref[...], ((0,), (0,))).astype(jnp.bfloat16)
+    for number, out in enumerate(outs):
+
+        @pl.when(pl.program_id(0) // per == number)
+        def _():
+            out[...] = value
+
+
+def outer_pieces(left, right, count):
     rows, tall = left.shape
     width = right.shape[1]
-    tile = min(512, tall // 2)
+    size = tall // count
+    tile = min(512, size)
+    per = size // tile
     half = tall // 2 // tile
-    shape = jax.ShapeDtypeStruct((tall // 2, width), jnp.bfloat16)
-    return pl.pallas_call(
-        functools.partial(outer_kernel, half),
+
+    def piece(number):
+        return pl.BlockSpec((tile, width), lambda i: (jnp.clip(i - number * per, 0, per - 1), 0))
+
+    outs = pl.pallas_call(
+        functools.partial(outer_kernel, per),
         grid=(2 * half,),
         in_specs=[
             pl.BlockSpec((rows, tile), lambda i: (0, jnp.where(i < half, i + half, i - half))),
             pl.BlockSpec((rows, width), lambda i: (0, 0)),
         ],
-        out_specs=[
-            pl.BlockSpec((tile, width), lambda i: (jnp.minimum(i, half - 1), 0)),
-            pl.BlockSpec((tile, width), lambda i: (jnp.maximum(i - half, 0), 0)),
-        ],
-        out_shape=[shape, shape],
+        out_specs=[piece(number) for number in range(count)],
+        out_shape=[jax.ShapeDtypeStruct((size, width), jnp.bfloat16)] * count,
         compiler_params=ROOM,
         cost_estimate=LITTLE,
-        name="outer_halves",
+        name="outer_pieces",
     )(left, right)
+    return outs[: count // 2], outs[count // 2 :]
 
 
 def outer(left, right):
@@ -750,48 +752,38 @@
     dense_in = jnp.concatenate(gather_pieces(normed_two_low, order_e, acts), axis=0)
     dense_grad = jnp.concatenate(gather_pieces(grad_dense_low, order_e, acts), axis=0)
     expert_grad = after(expert_grad, expert_out, dense_in, dense_grad)
-    grad_inners = pieces_slope_product(expert_grad, downs, expert_slope)
-    grad_expert_in = product(grad_inners, full_up, width)
+    def fold(kept, got):
+        return (kept.astype(jnp.float32) + got.astype(jnp.float32)).astype(jnp.bfloat16)
+
+    def outer_fold(later, kept):
+        got = [exchange(piece, order_e[-1]) for piece in later]
+        pieces = [fold(k, g) for k, g in zip(kept[1:], got[1:])]
+        return kept[0], got[0], pieces
+
+    later_downs, kept_downs = outer_pieces(acts, expert_grad, n_es)
+    own_downs, got_downs, pass_downs = outer_fold(later_downs, kept_downs)
+    grad_inners = pieces_slope_product(after(expert_grad, later_downs[0]), downs, expert_slope)
+    grad_expert_in = product(after(grad_inners, pass_downs[0]), full_up, width)
+    last_downs = exchange(pass_downs[0], order_e[0])
     out_home = to_experts(after(expert_out, expert_grad))
 
     activated_low, slope = gelu_product(after(dense_in, grad_expert_in), dense_weights, units)
     dense_part = product(activated_low, dense_weights, width, place=2)
-    grad_home = to_experts(after(grad_expert_in, out_home, dense_part))
+    grad_home = to_experts(after(grad_expert_in, out_home))
     dense_folded = fold_all_but_last(split_pieces(dense_part), order_e)
     dense = sum_pieces(dense_folded, order_e[:1])
     grad_inner_low = slope_product(after(dense_grad, dense_part), dense_weights, slope, width, 2)
-    grad_normed_part = product(grad_inner_low, dense_weights, units, ((1,), (1,)))
+    grad_normed_part = product(after(grad_inner_low, last_downs, dense_folded[1]), dense_weights, units, ((1,), (1,)))
     grad_normed_folded = fold_all_but_last(split_pieces(grad_normed_part), order_e)
     grad_normed_dense = sum_pieces(grad_normed_folded, order_e[:1])
 
-    def outer_fold(later, kept):
-        half = later.shape[0]
-        size = half // (n_es // 2)
-        pieces = [
-            (
-                kept[i : i + size].astype(jnp.float32)
-                + exchange(later[i : i + size], order_e[-1]).astype(jnp.float32)
-            ).astype(jnp.bfloat16)
-            for i in range(0, half, size)
-        ]
-        return fold_all_but_last(pieces, order_e[:-1])
-
-    later_ups, kept_ups = outer_halves(grad_inners, after(expert_in, grad_normed_part, dense_folded[1]))
-    later_downs, kept_downs = outer_halves(acts, after(expert_grad, later_ups))
-    grad_w_back = outer(activated_low, after(dense_grad, later_downs, grad_normed_folded[1]))
-    grad_w_in = outer(after(dense_in, later_downs), grad_inner_low)
-    grad_home = after(grad_home, later_downs, grad_w_back, grad_w_in, dense, grad_normed_dense)
+    later_ups, kept_ups = outer_pieces(grad_inners, after(expert_in, grad_normed_part), n_es)
+    grad_w_back = outer(activated_low, after(dense_grad, later_ups[0], grad_normed_folded[1]))
+    grad_w_in = outer(after(dense_in, later_ups[0]), grad_inner_low)
+    dense_stack = jnp.concatenate([g.reshape(n_ep, -1, width) for g in (grad_w_in, grad_w_back)], axis=1)
+    grad_home = after(grad_home, dense_stack, dense, grad_normed_dense)
     out_home = after(out_home, grad_home)
-    grad_ups = outer_fold(later_ups, after(kept_ups, grad_home))
-    grad_downs = outer_fold(later_downs, after(kept_downs, grad_home))
-    dense_sum = lax.psum_scatter(
-        after(
-            jnp.concatenate([g.reshape(n_ep, -1, width) for g in (grad_w_in, grad_w_back)], axis=1), grad_home
-        ),
-        "ep",
-        scatter_dimension=0,
-        tiled=True,
-    )[0]
+    own_ups, got_ups, pass_ups = outer_fold(later_ups, [after(kept, grad_home) for kept in kept_ups])
     expert_tokens = dot(in_slot, out_home, ((0,), (0,))) * keep
     grad_expert_home = dot(in_slot, grad_home, ((0,), (0,)))
 
@@ -824,74 +816,89 @@
     grad_mine = swap_groups(grad_attended.reshape(rows, n_es, group).transpose(1, 0, 2), "es").reshape(
         n_es * rows, group
     )
+    dense_sum = lax.psum_scatter(after(dense_stack, grad_home), "ep", scatter_dimension=0, tiled=True)[0]
     grad_w_out = dot(attended, after(grad_att_low, grad_attended), ((0,), (0,))).astype(jnp.bfloat16)
-    by_es = grad_w_out.reshape(n_ep, n_es, stripe, width).transpose(1, 0, 2, 3)
-    taps = []
-    out_part = scatter_sum(by_es.reshape(n_es * n_ep * stripe, width), order_e[::-1], taps=taps).astype(jnp.bfloat16)
-    grad_mine = after(grad_mine, grad_downs[1], taps[0])
-    last_downs = exchange(after(grad_downs[1], grad_mine), order_e[0])
-    grad_qkv = attend_back(qkv, after(grad_mine, grad_downs[1]), attended_full, logs)
-    last_ups = exchange(after(grad_ups[1], grad_qkv), order_e[0])
-    grad_ups, grad_downs = (
-        pieces[0].astype(jnp.float32) + last.astype(jnp.float32)
-        for pieces, last in ((grad_ups, last_ups), (grad_downs, last_downs))
-    )
-    grad_qkv = after(grad_qkv, last_downs)
-    taps = []
+    by_es = grad_w_out.reshape(n_ep, n_es // 2, 2, stripe, width).transpose(2, 1, 0, 3, 4)
+    out_folded = scatter_sum(by_es.reshape(n_es * n_ep * stripe, width), order_e[-1:]).astype(jnp.bfloat16)
+    grad_mine = after(grad_mine, pass_ups[0], out_folded)
+    last_ups = exchange(after(pass_ups[0], grad_mine), order_e[0])
+    grad_qkv = after(attend_back(qkv, grad_mine, attended_full, logs), last_ups)
+    out_part = scatter_sum(after(out_folded, grad_qkv), order_e[:-1][::-1]).astype(jnp.bfloat16)
     back_e = order_e[::-1]
     grad_rows_part = dot(grad_qkv, w_heads, ((1,), (1,))).astype(jnp.bfloat16)
-    grad_rows = scatter_sum(grad_rows_part, back_e, taps=taps)
     grad_w_heads = dot(normed_all, after(grad_qkv, grad_rows_part), ((0,), (0,)))
     column_sums = jnp.sum(grad_qkv.astype(jnp.float32), axis=0, keepdims=True)
     grad_w_heads_low = grad_w_heads.astype(jnp.bfloat16)
     heads_wide = w_heads.astype(jnp.float32)
     grad_bias_one = jnp.sum(heads_wide * column_sums, axis=1)
     grad_gain_one = (jnp.sum(heads_wide * grad_w_heads, axis=1) - bias_one[0] * grad_bias_one) / gain_one[0]
+    taps, chain, sums = [], [], []
+
+    def last_sums():
+        back_z = order_z[::-1]
+        back_y = [order_z[1], order_z[-1], *order_z[2:-1], order_z[0]] if len(order_z) > 2 else back_z
+        small_grads = jnp.stack(
+            [grad_gain_one, grad_bias_one, grad_gain_two, grad_bias_two, grad_coef[0], grad_coef[1]]
+        )
+        small_grads = small_grads.astype(jnp.bfloat16).reshape(6, n_ep, n_es * stripe).transpose(1, 0, 2)
+        extra = 16
+        small_grads = jnp.pad(small_grads, ((0, 0), (0, extra - 6), (0, 3 * group - n_es * stripe)))
+        joined = jnp.concatenate([grad_w_heads_low.reshape(n_ep, n_es * stripe, 3 * group), small_grads], axis=1)
+        by_columns = out_part.reshape(n_ep, stripe, n_es, group).transpose(0, 2, 1, 3).reshape(n_ep, -1, group)
+        by_columns = jnp.pad(by_columns, ((0, 0), (0, extra), (0, 0)))
+        joined = jnp.concatenate([joined, by_columns], axis=2).reshape(-1, 4 * group)
+        cut = 2 * group
+        joined = jnp.concatenate(
+            [scatter_sum(joined[:, :cut], back_z, hold=taps[:1], taps=chain), scatter_sum(joined[:, cut:], back_y)], axis=1
+        )
+        joined = joined.astype(jnp.bfloat16)
+        small_sum = joined[n_es * stripe :][:6, : n_es * stripe].reshape(6, n_es, stripe).transpose(1, 0, 2)
+        small_sum = jnp.pad(small_sum, ((0, 0), (0, stripe - 6), (0, tile - stripe)))
+        sums.append(joined)
+        sums.append(
+            jnp.concatenate(
+                [
+                    joined[: n_es * stripe, : 3 * group].reshape(n_es, stripe, 3 * group),
+                    small_sum,
+                    dense_sum[: n_es * stripe].reshape(n_es, stripe, units),
+                ],
+                axis=2,
+            )
+        )
+        return sums[1]
+
+    grad_rows = scatter_sum(grad_rows_part, back_e, taps=taps, beside=last_sums)
+    joined, outgoing = sums
+    last = swap_groups(outgoing, "es")
     _, unit_one, inverse_one = norm_forward(inputs, gain_one, bias_one)
     grad_inputs_norm, _, _ = norm_backward(grad_rows, unit_one, inverse_one, gain_one)
     grad_tokens = grad_hidden + grad_inputs_norm
-
-    back_z = order_z[::-1]
-    back_y = [order_z[1], order_z[-1], *order_z[2:-1], order_z[0]] if len(order_z) > 2 else back_z
-    small_grads = jnp.stack(
-        [grad_gain_one, grad_bias_one, grad_gain_two, grad_bias_two, grad_coef[0], grad_coef[1]]
-    )
-    small_grads = small_grads.astype(jnp.bfloat16).reshape(6, n_ep, n_es * stripe).transpose(1, 0, 2)
-    extra = 16
-    small_grads = jnp.pad(small_grads, ((0, 0), (0, extra - 6), (0, 3 * group - n_es * stripe)))
-    joined = jnp.concatenate([grad_w_heads_low.reshape(n_ep, n_es * stripe, 3 * group), small_grads], axis=1)
-    by_columns = out_part.reshape(n_ep, stripe, n_es, group).transpose(0, 2, 1, 3).reshape(n_ep, -1, group)
-    by_columns = jnp.pad(by_columns, ((0, 0), (0, extra), (0, 0)))
-    joined = jnp.concatenate([joined, by_columns], axis=2).reshape(-1, 4 * group)
-    cut = 2 * group
-    joined = jnp.concatenate(
-        [scatter_sum(joined[:, :cut], back_z, hold=taps[:1]), scatter_sum(joined[:, cut:], back_y)], axis=1
-    )
     grad_w_out = (
-        joined[: n_es * stripe, 3 * group :].reshape(n_es, stripe, group).transpose(1, 0, 2).reshape(stripe, width)
-    )
-    joined = joined.astype(jnp.bfloat16)
-    small_sum = joined[n_es * stripe :][:6, : n_es * stripe].reshape(6, n_es, stripe).transpose(1, 0, 2)
-    small_sum = jnp.pad(small_sum, ((0, 0), (0, stripe - 6), (0, tile - stripe)))
-    last = swap_groups(
-        jnp.concatenate(
-            [
-                joined[: n_es * stripe, : 3 * group].reshape(n_es, stripe, 3 * group),
-                small_sum,
-                dense_sum[: n_es * stripe].reshape(n_es, stripe, units),
-            ],
-            axis=2,
-        ),
-        "es",
-    ).astype(jnp.float32)
+        joined[: n_es * stripe, 3 * group :]
+        .reshape(n_es, stripe, group)
+        .transpose(1, 0, 2)
+        .reshape(stripe, width)
+        .astype(jnp.float32)
+    )
+    grad_ups, grad_downs = (
+        after(own, chain[0]).astype(jnp.float32) + got.astype(jnp.float32) + came.astype(jnp.float32)
+        for own, got, came in ((own_ups, got_ups, last_ups), (own_downs, got_downs, last_downs))
+    )
     cut = 3 * group
-    grad_w_qkv = last[:, :, :cut].reshape(n_es, stripe, 3, group).transpose(1, 2, 0, 3).reshape(stripe, 3 * width)
-    small_sum = jnp.sum(last[:, :6, cut : cut + stripe], axis=0)
+    grad_w_qkv = (
+        last[:, :, :cut]
+        .reshape(n_es, stripe, 3, group)
+        .transpose(1, 2, 0, 3)
+        .reshape(stripe, 3 * width)
+        .astype(jnp.float32)
+    )
+    small_sum = jnp.sum(last[:, :6, cut : cut + stripe].astype(jnp.float32), axis=0)
     grad_fc_in = (
         last[:, :, cut + tile :]
         .reshape(n_es, stripe, n_ep, block)
         .transpose(1, 2, 0, 3)
         .reshape(stripe, n_ep * n_es * block)
+        .astype(jnp.float32)
     )
     return (
         out_tokens,

time: 681 us -> 658 us (0.966)
  local copies, waits for them, and re-layouts: 80 us -> 66.9 us
  waiting for transfers between devices: 183 us -> 171 us
    ppermute x43, waiting for transfers between devices: 127 us -> 111 us  [exchange(): return lax.ppermute(x, axis, [(i, i ^ stride) for i in range(size)])]
    slice x6 -> x2, local copies, waits for them, and re-layouts: 7.26 us -> 0.18 us  [the longest x1 0.18 us: last_sums(): joined[:, cut:]]
    unnamed x142 -> x138, local copies, waits for them, and re-layouts: 45.6 us -> 40.7 us
  transfers between devices with their start and end apart: 54 -> 54, of which waited for: 22 -> 23; matrix products, arithmetic and copies ran while one was open for 24% -> 25% of each run, Pallas kernels for 27% -> 26%
where the time goes in v4:
time: 658 us; the launch traced here: 648 us
  Pallas kernels  189 us (29%)
  waiting for transfers between devices  171 us (26%)
  starting transfers between devices  78.3 us (12%)
  local copies, waits for them, and re-layouts  66.9 us (10%)
  other arithmetic  65 us (10%)
  matrix products  62.4 us (9%)
  between operations  15.5 us (2%)
    ppermute x43, waiting for transfers between devices, exchange(): return lax.ppermute(x, axis, [(i, i ^ stride) for i in range(size)])  111 us
    dot_general x12, matrix products, dot(): lax.dot_general(left, right, (contract, ((), ())), preferred_element_type...  57.9 us
    all_to_all x9, starting transfers between devices, swap_groups(): return lax.all_to_all(x, axis, split_axis=0, concat_axis=0, tiled=True)  42.8 us
    unnamed x138, local copies, waits for them, and re-layouts  40.7 us
    pallas_call x1, Pallas kernels, attend_back(): pl.pallas_call(functools.partial(attend_back_kernel, heads, bq, bk), grid...  37.9 us
    ppermute x43, starting transfers between devices, exchange(): return lax.ppermute(x, axis, [(i, i ^ stride) for i in range(size)])  35.3 us
    all_gather x1, waiting for transfers between devices, on_device(): lax.all_gather(after(jnp.concatenate([more, w_fc_out], axis=1), w_heads),...  30.5 us
    pallas_call x2, Pallas kernels, outer_pieces(): pl.pallas_call(functools.partial(outer_kernel, per), grid=(2 * half,), in...  29 us
  transfers between devices with their start and end apart: 54, of which 23 were waited for; matrix products, arithmetic and copies ran while one was open for 25% of the time, Pallas kernels for 26%

profile of v4, /device:TPU:0, one launch (start us, length us, event | category | flops | bytes accessed | tf_op | source)
XLA Modules:
  0.0 648.4 jit_solution(13609780349863397184)
XLA Ops:
  53.0 8.0 %collective-permute-done.8.refs_3_ = bf16[4,128,384]{2,1,0:T(8,128)(2,1)} collective-permute-done((bf16[4,128,384]{2,1,0:T(8,128)(2,1)S(1)}, bf16[4,128,384]{2,1,0:T(8,128)(2,1)}, u32[]{:S(2)}, u32[]{:S(2)}) %collective-permute-start.8) | collective-permute-done | bytes 393248 | tf_op jit(solution)/shard_map/ppermute | solution.py:61
  73.6 6.0 norm_place.1
  83.3 24.0 %attend.1 = (bf16[2048,256]{1,0:T(8,128)(2,1)S(1)}, f32[2048,256]{1,0:T(8,128)S(1)}, f32[4,2048]{1,0:T(4,128)S(1)}) custom-call(bf16[2048,768]{1,0:T(8,128)(2,1)S(1)} %convolution_convert_fusion.1.q_ref.k_ref.v_ref, bf16[2048,768]{1,0:T(8,128)(2,1)S(1)} %convolution_convert_fusion.1.q_ref.k_ref.v_ref, ...), custom_call_target="tpu_custom_call" | custom-call | flops 1048576 | bytes 1048576 | tf_op jit(solution)/shard_map/attend/pallas_call | solution.py:329
  120.6 13.5 %all-to-all-done.1 = bf16[4,512,256]{1,2,0:T(8,128)(2,1)S(1)} async-done(((bf16[4,512,256]{1,2,0:T(8,128)(2,1)}), bf16[4,512,256]{1,2,0:T(8,128)(2,1)S(1)}, u32[]{:S(2)}, u32[]{:S(2)}) %all-to-all-start.1) | async-done | bytes 1048608 | tf_op jit(solution)/shard_map/all_to_all | solution.py:632
  134.1 30.5 %all-gather.2.cloned.1.call-done.right_ref = bf16[1024,3072]{1,0:T(8,128)(2,1)} async-done(((bf16[128,3072]{1,0:T(8,128)(2,1)}), bf16[1024,3072]{1,0:T(8,128)(2,1)}) %all-gather.2.cloned.1.call-update) | async-done | bytes 6291472 | tf_op jit(solution)/shard_map/all_gather | solution.py:699
  196.9 30.0 %collective-permute-done.15.refs_1_ = bf16[1024,1024]{1,0:T(8,128)(2,1)} collective-permute-done((bf16[1024,1024]{1,0:T(8,128)(2,1)}, bf16[1024,1024]{1,0:T(8,128)(2,1)}, u32[]{:S(2)}, u32[]{:S(2)}) %collective-permute-start.15) | collective-permute-done | bytes 2097184 | tf_op jit(solution)/shard_map/ppermute | solution.py:61
  230.9 6.1 all-to-all-start.4
  237.0 18.9 %fusion.3 = (f32[1024,4096]{1,0:T(8,128)}, bf16[1024,4096]{1,0:T(8,128)(2,1)}) fusion(bf16[1024,1024]{1,0:T(8,128)(2,1)} %bitcast.192, bf16[4096,1024]{1,0:T(8,128)(2,1)} %constant_dynamic-update-slice_fusion.right_ref), kind=kOutput, calls=%fused_computation.4 | convolution fusion | flops 8631877632 | bytes 35651584 | tf_op jit(solution)/shard_map/dot_general | solution.py:44
  256.4 13.7 %collective-permute-done.18 = bf16[512,1024]{1,0:T(8,128)(2,1)} collective-permute-done((bf16[512,1024]{1,0:T(8,128)(2,1)}, bf16[512,1024]{1,0:T(8,128)(2,1)}, u32[]{:S(2)}, u32[]{:S(2)}) %collective-permute-start.18) | collective-permute-done | bytes 1048608 | tf_op jit(solution)/shard_map/ppermute | solution.py:61
  270.6 13.4 %pieces_product.1 = bf16[1024,1024]{1,0:T(8,128)(2,1)S(1)} custom-call(bf16[1024,4096]{1,0:T(8,128)(2,1)} %get-tuple-element.138.left_ref, bf16[1024,1024]{1,0:T(8,128)(2,1)} %bitcast.25.refs_0_, bf16[1024,1024]{1,0:T(8,128)(2,1)} %collective-permute-done.15.refs_1_, bf16[1024,1024]{1,0:T(8,128)(2,1)} %collective-permute-done.16.refs_2_, ...), custom_call_target="tpu_custom_call" | custom-call | flops 1048576 | bytes 1048576 | tf_op jit(solution)/shard_map/pieces_product/pallas_call | solution.py:535
  294.4 14.2 %outer_pieces.2 = (bf16[1024,1024]{1,0:T(8,128)(2,1)}, bf16[1024,1024]{1,0:T(8,128)(2,1)}, bf16[1024,1024]{1,0:T(8,128)(2,1)S(1)}, bf16[1024,1024]{1,0:T(8,128)(2,1)S(1)}) custom-call(bf16[1024,4096]{1,0:T(8,128)(2,1)} %get-tuple-element.138.left_ref, bf16[1024,1024]{1,0:T(8,128)(2,1)S(1)} %bitcast.190), custom_call_target="tpu_custom_call" | custom-call | flops 1048576 | bytes 1048576 | tf_op jit(solution)/shard_map/outer_pieces/pallas_call | solution.py:596
  311.3 6.1 all-to-all-start.5
  323.4 16.3 %pieces_slope_product.1.left_ref = bf16[1024,4096]{1,0:T(8,128)(2,1)} custom-call(bf16[1024,1024]{1,0:T(8,128)(2,1)S(1)} %bitcast.191, f32[1024,4096]{1,0:T(8,128)} %get-tuple-element.137.slope_ref, bf16[1024,1024]{1,0:T(8,128)(2,1)} %bitcast.25.refs_0_, bf16[1024,1024]{1,0:T(8,128)(2,1)} %collective-permute-done.15.refs_1_, ...), custom_call_target="tpu_custom_call" | custom-call | flops 1048576 | bytes 1048576 | tf_op jit(solution)/shard_map/pieces_slope_product/pallas_call | solution.py:563
  343.1 13.7 %product.3 = bf16[1024,1024]{1,0:T(8,128)(2,1)} custom-call(bf16[1024,4096]{1,0:T(8,128)(2,1)S(1)} %copy-done, bf16[4096,1024]{1,0:T(8,128)(2,1)} %constant_dynamic-update-slice_fusion.right_ref), custom_call_target="tpu_custom_call" | custom-call | flops 1048576 | bytes 1048576 | tf_op jit(solution)/shard_map/product/pallas_call | solution.py:458
  356.8 10.9 %gelu_product.1 = (bf16[2048,1024]{1,0:T(8,128)(2,1)S(1)}, f32[2048,1024]{1,0:T(8,128)}) custom-call(bf16[2048,1024]{1,0:T(8,128)(2,1)S(1)} %copy-done.7, bf16[1024,3072]{1,0:T(8,128)(2,1)} %all-gather.2.cloned.1.call-done.right_ref), custom_call_target="tpu_custom_call" | custom-call | flops 1048576 | bytes 1048576 | tf_op jit(solution)/shard_map/gelu_product/pallas_call | solution.py:483
  367.7 8.1 %product.4 = bf16[2048,1024]{1,0:T(8,128)(2,1)S(1)} custom-call(bf16[2048,1024]{1,0:T(8,128)(2,1)S(1)} %get-tuple-element.94.left_ref, bf16[1024,3072]{1,0:T(8,128)(2,1)} %all-gather.2.cloned.1.call-done.right_ref), custom_call_target="tpu_custom_call" | custom-call | flops 1048576 | bytes 1048576 | tf_op jit(solution)/shard_map/product/pallas_call | solution.py:458
  378.2 6.0 all-to-all-start.6
  386.6 9.6 %slope_product.1.left_ref.right_ref = bf16[2048,1024]{1,0:T(8,128)(2,1)S(1)} custom-call(bf16[2048,1024]{1,0:T(8,128)(2,1)S(1)} %copy-done.10, bf16[1024,3072]{1,0:T(8,128)(2,1)} %all-gather.2.cloned.1.call-done.right_ref, f32[2048,1024]{1,0:T(8,128)} %get-tuple-element.98.slope_ref), custom_call_target="tpu_custom_call" | custom-call | flops 1048576 | bytes 1048576 | tf_op jit(solution)/shard_map/slope_product/pallas_call | solution.py:506
  399.7 6.8 %product.5 = bf16[2048,1024]{1,0:T(8,128)(2,1)S(1)} custom-call(bf16[2048,1024]{1,0:T(8,128)(2,1)S(1)} %slope_product.1.left_ref.right_ref, bf16[1024,3072]{1,0:T(8,128)(2,1)} %all-gather.2.cloned.1.call-done.right_ref), custom_call_target="tpu_custom_call" | custom-call | flops 1048576 | bytes 1048576 | tf_op jit(solution)/shard_map/product/pallas_call | solution.py:458
  412.6 14.8 %outer_pieces.3 = (bf16[1024,1024]{1,0:T(8,128)(2,1)}, bf16[1024,1024]{1,0:T(8,128)(2,1)}, bf16[1024,1024]{1,0:T(8,128)(2,1)S(1)}, bf16[1024,1024]{1,0:T(8,128)(2,1)S(1)}) custom-call(bf16[1024,4096]{1,0:T(8,128)(2,1)} %pieces_slope_product.1.left_ref, bf16[1024,1024]{1,0:T(8,128)(2,1)S(1)} %bitcast.193), custom_call_target="tpu_custom_call" | custom-call | flops 1048576 | bytes 1048576 | tf_op jit(solution)/shard_map/outer_pieces/pallas_call | solution.py:596
  446.5 9.9 %collective-permute-done.28 = bf16[512,1024]{1,0:T(8,128)(2,1)} collective-permute-done((bf16[512,1024]{1,0:T(8,128)(2,1)}, bf16[512,1024]{1,0:T(8,128)(2,1)}, u32[]{:S(2)}, u32[]{:S(2)}) %collective-permute-start.28) | collective-permute-done | bytes 1048608 | tf_op jit(solution)/shard_map/ppermute | solution.py:61
  499.8 37.9 %attend_back.1 = bf16[2048,768]{1,0:T(8,128)(2,1)} custom-call(bf16[2048,768]{1,0:T(8,128)(2,1)} %copy-done.3, bf16[2048,768]{1,0:T(8,128)(2,1)} %copy-done.3, bf16[2048,768]{1,0:T(8,128)(2,1)} %copy-done.3, bf16[2048,256]{1,0:T(8,128)(2,1)} %bitcast.41.g_ref, f32[2048,256]{1,0:T(8,128)} %copy-done.33, f32[4,2048]{1,0:T(4,128)} %copy-done.37), custom_call_target="tpu_custom_call" | custom-call | flops 68719476736 | bytes 7340032 | tf_op jit(solution)/shard_map/attend_back/pallas_call | solution.py:416
  537.7 9.1 %collective-permute-done.31 = bf16[1024,1024]{1,0:T(8,128)(2,1)S(1)} collective-permute-done((bf16[1024,1024]{1,0:T(8,128)(2,1)}, bf16[1024,1024]{1,0:T(8,128)(2,1)S(1)}, u32[]{:S(2)}, u32[]{:S(2)}) %collective-permute-start.31) | collective-permute-done | bytes 2097184 | tf_op jit(solution)/shard_map/ppermute | solution.py:61
  548.8 7.3 %convolution_convert_fusion = bf16[2048,1024]{1,0:T(8,128)(2,1)} fusion(bf16[2048,768]{1,0:T(8,128)(2,1)} %attend_back.1, bf16[1024,768]{1,0:T(8,128)(2,1)S(1)} %copy-done.36), kind=kOutput, calls=%fused_computation.29 | convolution fusion | flops 3223322624 | bytes 8912896 | tf_op jit(solution)/shard_map/dot_general | solution.py:44
  (372 shorter events, 297.9 us)
Async XLA Ops:
  20.1 26.1 %collective-permute-start = (bf16[512,1024]{1,0:T(8,128)(2,1)S(1)}, bf16[512,1024]{1,0:T(8,128)(2,1)S(1)}, u32[]{:S(2)}, u32[]{:S(2)}) collective-permute-start(bf16[512,1024]{1,0:T(8,128)(2,1)S(1)} %copy-done.4), channel_id=1, source_target_pairs={{0,2},{1,3},{2,0},{3,1},{4,6},{5,7},{6,4},{7,5},{8,10},{9,11},{10,... | collective-permute-start | bytes 3145736 | tf_op jit(solution)/shard_map/ppermute | solution.py:61
  35.6 129.0 %all-gather.2.cloned.1.call-start = ((), (), s32[]{:S(2)}) async-start(), calls=%async_computation.10 | async-start | bytes 7077888 | tf_op jit(solution)/shard_map/all_gather | solution.py:699
  66.3 48.4 %collective-permute-start.10 = (bf16[1024,1024]{1,0:T(8,128)(2,1)}, bf16[1024,1024]{1,0:T(8,128)(2,1)}, u32[]{:S(2)}, u32[]{:S(2)}) collective-permute-start(bf16[1024,1024]{1,0:T(8,128)(2,1)} %bitcast.213), channel_id=1, source_target_pairs={{0,2},{1,3},{2,0},{3,1},{4,6},{5,7},{6,4},{7,5},{8,10},{9,11},{10,... | collective-permute-start | bytes 6291464 | tf_op jit(solution)/shard_map/ppermute | solution.py:61
  120.2 68.7 %collective-permute-start.11 = (bf16[1024,1024]{1,0:T(8,128)(2,1)}, bf16[1024,1024]{1,0:T(8,128)(2,1)}, u32[]{:S(2)}, u32[]{:S(2)}) collective-permute-start(bf16[1024,1024]{1,0:T(8,128)(2,1)} %collective-permute-done.10), channel_id=1, source_target_pairs={{0,1},{1,0},{2,3},{3,2},{4,5},{5,4},{6,7},{7,6},{8,9},{9,8},{10,11... | collective-permute-start | bytes 6291464 | tf_op jit(solution)/shard_map/ppermute | solution.py:61
  174.2 55.4 %all-to-all-start.3 = ((bf16[8,128,1024]{2,1,0:T(8,128)(2,1)}), bf16[8,128,1024]{2,1,0:T(8,128)(2,1)S(1)}, u32[]{:S(2)}, u32[]{:S(2)}) async-start(bf16[8,128,1024]{2,1,0:T(8,128)(2,1)} %bitcast.216), calls=%async_computation.3 | async-start | bytes 4194304 | tf_op jit(solution)/shard_map/all_to_all | solution.py:632
  177.9 48.9 %collective-permute-start.15 = (bf16[1024,1024]{1,0:T(8,128)(2,1)}, bf16[1024,1024]{1,0:T(8,128)(2,1)}, u32[]{:S(2)}, u32[]{:S(2)}) collective-permute-start(bf16[1024,1024]{1,0:T(8,128)(2,1)} %bitcast.25.refs_0_), channel_id=1, source_target_pairs={{0,2},{1,3},{2,0},{3,1},{4,6},{5,7},{6,4},{7,5},{8,10},{9,11},{10,... | collective-permute-start | bytes 6291464 | tf_op jit(solution)/shard_map/ppermute | solution.py:61
  192.1 63.9 %collective-permute-start.12 = (bf16[512,1024]{1,0:T(8,128)(2,1)}, bf16[512,1024]{1,0:T(8,128)(2,1)}, u32[]{:S(2)}, u32[]{:S(2)}) collective-permute-start(bf16[512,1024]{1,0:T(8,128)(2,1)} %fusion.38), channel_id=1, source_target_pairs={{0,2},{1,3},{2,0},{3,1},{4,6},{5,7},{6,4},{7,5},{8,10},{9,11},{10,... | collective-permute-start | bytes 3145736 | tf_op jit(solution)/shard_map/ppermute | solution.py:61
  195.4 74.7 %collective-permute-start.18 = (bf16[512,1024]{1,0:T(8,128)(2,1)}, bf16[512,1024]{1,0:T(8,128)(2,1)}, u32[]{:S(2)}, u32[]{:S(2)}) collective-permute-start(bf16[512,1024]{1,0:T(8,128)(2,1)} %fusion.23), channel_id=1, source_target_pairs={{0,2},{1,3},{2,0},{3,1},{4,6},{5,7},{6,4},{7,5},{8,10},{9,11},{10,... | collective-permute-start | bytes 3145736 | tf_op jit(solution)/shard_map/ppermute | solution.py:61
  196.9 73.2 %collective-permute-start.16 = (bf16[1024,1024]{1,0:T(8,128)(2,1)}, bf16[1024,1024]{1,0:T(8,128)(2,1)}, u32[]{:S(2)}, u32[]{:S(2)}) collective-permute-start(bf16[1024,1024]{1,0:T(8,128)(2,1)} %bitcast.25.refs_0_), channel_id=1, source_target_pairs={{0,1},{1,0},{2,3},{3,2},{4,5},{5,4},{6,7},{7,6},{8,9},{9,8},{10,11... | collective-permute-start | bytes 6291464 | tf_op jit(solution)/shard_map/ppermute | solution.py:61
  226.9 43.8 %collective-permute-start.17 = (bf16[1024,1024]{1,0:T(8,128)(2,1)}, bf16[1024,1024]{1,0:T(8,128)(2,1)}, u32[]{:S(2)}, u32[]{:S(2)}) collective-permute-start(bf16[1024,1024]{1,0:T(8,128)(2,1)} %collective-permute-done.15.refs_1_), channel_id=1, source_target_pairs={{0,1},{1,0},{2,3},{3,2},{4,5},{5,4},{6,7},{7,6},{8,9},{9,8},{10,11... | collective-permute-start | bytes 6291464 | tf_op jit(solution)/shard_map/ppermute | solution.py:61
  230.9 63.5 %all-to-all-start.4 = ((bf16[8,128,1024]{2,1,0:T(8,128)(2,1)}), bf16[8,128,1024]{2,1,0:T(8,128)(2,1)S(1)}, u32[]{:S(2)}, u32[]{:S(2)}) async-start(bf16[8,128,1024]{2,1,0:T(8,128)(2,1)} %bitcast.215), calls=%async_computation.4 | async-start | bytes 4194304 | tf_op jit(solution)/shard_map/all_to_all | solution.py:632
  255.9 34.1 %collective-permute-start.13 = (bf16[512,1024]{1,0:T(8,128)(2,1)}, bf16[512,1024]{1,0:T(8,128)(2,1)S(1)}, u32[]{:S(2)}, u32[]{:S(2)}) collective-permute-start(bf16[512,1024]{1,0:T(8,128)(2,1)} %fusion.38), channel_id=1, source_target_pairs={{0,1},{1,0},{2,3},{3,2},{4,5},{5,4},{6,7},{7,6},{8,9},{9,8},{10,11... | collective-permute-start | bytes 3145736 | tf_op jit(solution)/shard_map/ppermute | solution.py:61
  256.1 34.1 %collective-permute-start.14 = (bf16[512,1024]{1,0:T(8,128)(2,1)}, bf16[512,1024]{1,0:T(8,128)(2,1)S(1)}, u32[]{:S(2)}, u32[]{:S(2)}) collective-permute-start(bf16[512,1024]{1,0:T(8,128)(2,1)} %collective-permute-done.12), channel_id=1, source_target_pairs={{0,1},{1,0},{2,3},{3,2},{4,5},{5,4},{6,7},{7,6},{8,9},{9,8},{10,11... | collective-permute-start | bytes 3145736 | tf_op jit(solution)/shard_map/ppermute | solution.py:61
  311.3 67.0 %all-to-all-start.5 = ((bf16[8,128,1024]{2,1,0:T(8,128)(2,1)}), bf16[8,128,1024]{2,1,0:T(8,128)(2,1)}, u32[]{:S(2)}, u32[]{:S(2)}) async-start(bf16[8,128,1024]{2,1,0:T(8,128)(2,1)} %bitcast.194), calls=%async_computation.5 | async-start | bytes 4194304 | tf_op jit(solution)/shard_map/all_to_all | solution.py:632
  321.9 77.7 %collective-permute-start.25 = (bf16[1024,1024]{1,0:T(8,128)(2,1)}, bf16[1024,1024]{1,0:T(8,128)(2,1)}, u32[]{:S(2)}, u32[]{:S(2)}) collective-permute-start(bf16[1024,1024]{1,0:T(8,128)(2,1)} %add_convert_fusion.1), channel_id=1, source_target_pairs={{0,2},{1,3},{2,0},{3,1},{4,6},{5,7},{6,4},{7,5},{8,10},{9,11},{10,... | collective-permute-start | bytes 6291464 | tf_op jit(solution)/shard_map/ppermute | solution.py:61
  378.2 81.9 %all-to-all-start.6 = ((bf16[8,128,1024]{2,1,0:T(8,128)(2,1)}), bf16[8,128,1024]{2,1,0:T(8,128)(2,1)}, u32[]{:S(2)}, u32[]{:S(2)}) async-start(bf16[8,128,1024]{2,1,0:T(8,128)(2,1)} %bitcast.32), calls=%async_computation.6 | async-start | bytes 4194304 | tf_op jit(solution)/shard_map/all_to_all | solution.py:632
  384.2 234.8 %reduce-scatter.2.cloned.1.call-start = ((), (), s32[]{:S(2)}) async-start(), calls=%async_computation.11 | async-start | bytes 4718592 | tf_op jit(solution)/shard_map/reduce_scatter | solution.py:819
  408.3 26.3 %collective-permute-start.24 = (bf16[512,1024]{1,0:T(8,128)(2,1)}, bf16[512,1024]{1,0:T(8,128)(2,1)}, u32[]{:S(2)}, u32[]{:S(2)}) collective-permute-start(bf16[512,1024]{1,0:T(8,128)(2,1)} %add_convert_fusion.5), channel_id=1, source_target_pairs={{0,2},{1,3},{2,0},{3,1},{4,6},{5,7},{6,4},{7,5},{8,10},{9,11},{10,... | collective-permute-start | bytes 3145736 | tf_op jit(solution)/shard_map/ppermute | solution.py:61
  408.8 37.6 %collective-permute-start.27 = (bf16[512,1024]{1,0:T(8,128)(2,1)}, bf16[512,1024]{1,0:T(8,128)(2,1)}, u32[]{:S(2)}, u32[]{:S(2)}) collective-permute-start(bf16[512,1024]{1,0:T(8,128)(2,1)} %get-tuple-element.140), channel_id=1, source_target_pairs={{0,1},{1,0},{2,3},{3,2},{4,5},{5,4},{6,7},{7,6},{8,9},{9,8},{10,11... | collective-permute-start | bytes 3145736 | tf_op jit(solution)/shard_map/ppermute | solution.py:61
  411.8 44.5 %collective-permute-start.28 = (bf16[512,1024]{1,0:T(8,128)(2,1)}, bf16[512,1024]{1,0:T(8,128)(2,1)}, u32[]{:S(2)}, u32[]{:S(2)}) collective-permute-start(bf16[512,1024]{1,0:T(8,128)(2,1)} %add_convert_fusion.4), channel_id=1, source_target_pairs={{0,2},{1,3},{2,0},{3,1},{4,6},{5,7},{6,4},{7,5},{8,10},{9,11},{10,... | collective-permute-start | bytes 3145736 | tf_op jit(solution)/shard_map/ppermute | solution.py:61
  428.7 59.3 %collective-permute-start.29 = (bf16[1024,1024]{1,0:T(8,128)(2,1)}, bf16[1024,1024]{1,0:T(8,128)(2,1)}, u32[]{:S(2)}, u32[]{:S(2)}) collective-permute-start(bf16[1024,1024]{1,0:T(8,128)(2,1)} %get-tuple-element.108), channel_id=1, source_target_pairs={{0,1},{1,0},{2,3},{3,2},{4,5},{5,4},{6,7},{7,6},{8,9},{9,8},{10,11... | collective-permute-start | bytes 6291464 | tf_op jit(solution)/shard_map/ppermute | solution.py:61
  478.7 107.2 %collective-permute-start.42 = (bf16[1024,1024]{1,0:T(8,128)(2,1)}, bf16[1024,1024]{1,0:T(8,128)(2,1)}, u32[]{:S(2)}, u32[]{:S(2)}) collective-permute-start(bf16[1024,1024]{1,0:T(8,128)(2,1)} %get-tuple-element.88), channel_id=1, source_target_pairs={{0,1},{1,0},{2,3},{3,2},{4,5},{5,4},{6,7},{7,6},{8,9},{9,8},{10,11... | collective-permute-start | bytes 6291464 | tf_op jit(solution)/shard_map/ppermute | solution.py:61
  479.3 112.5 %collective-permute-start.41 = (bf16[1024,1024]{1,0:T(8,128)(2,1)}, bf16[1024,1024]{1,0:T(8,128)(2,1)}, u32[]{:S(2)}, u32[]{:S(2)}) collective-permute-start(bf16[1024,1024]{1,0:T(8,128)(2,1)} %get-tuple-element.101), channel_id=1, source_target_pairs={{0,1},{1,0},{2,3},{3,2},{4,5},{5,4},{6,7},{7,6},{8,9},{9,8},{10,11... | collective-permute-start | bytes 6291464 | tf_op jit(solution)/shard_map/ppermute | solution.py:61
  499.5 47.4 %collective-permute-start.31 = (bf16[1024,1024]{1,0:T(8,128)(2,1)}, bf16[1024,1024]{1,0:T(8,128)(2,1)S(1)}, u32[]{:S(2)}, u32[]{:S(2)}) collective-permute-start(bf16[1024,1024]{1,0:T(8,128)(2,1)} %add_convert_fusion), channel_id=1, source_target_pairs={{0,2},{1,3},{2,0},{3,1},{4,6},{5,7},{6,4},{7,5},{8,10},{9,11},{10,... | collective-permute-start | bytes 6291464 | tf_op jit(solution)/shard_map/ppermute | solution.py:61
  (93 other events, 904.9 us)
Sparse Core Ops, SparseCore 0:
  66.3 98.2 all-gather.1
  479.5 88.2 reduce-scatter.1

commit v5 on v4

--- a/solution.py
+++ b/solution.py
@@ -822,11 +822,11 @@
     out_folded = scatter_sum(by_es.reshape(n_es * n_ep * stripe, width), order_e[-1:]).astype(jnp.bfloat16)
     grad_mine = after(grad_mine, pass_ups[0], out_folded)
     last_ups = exchange(after(pass_ups[0], grad_mine), order_e[0])
-    grad_qkv = after(attend_back(qkv, grad_mine, attended_full, logs), last_ups)
+    grad_qkv = attend_back(qkv, grad_mine, attended_full, logs)
     out_part = scatter_sum(after(out_folded, grad_qkv), order_e[:-1][::-1]).astype(jnp.bfloat16)
     back_e = order_e[::-1]
     grad_rows_part = dot(grad_qkv, w_heads, ((1,), (1,))).astype(jnp.bfloat16)
-    grad_w_heads = dot(normed_all, after(grad_qkv, grad_rows_part), ((0,), (0,)))
+    grad_w_heads = dot(normed_all, after(grad_qkv, grad_rows_part, last_ups), ((0,), (0,)))
     column_sums = jnp.sum(grad_qkv.astype(jnp.float32), axis=0, keepdims=True)
     grad_w_heads_low = grad_w_heads.astype(jnp.bfloat16)
     heads_wide = w_heads.astype(jnp.float32)

time: 658 us -> 655 us (level)
    unnamed x138 -> x130, local copies, waits for them, and re-layouts: 40.7 us -> 41.7 us
  transfers between devices with their start and end apart: 54 -> 54, of which waited for: 23 -> 22; matrix products, arithmetic and copies ran while one was open for 25% -> 25% of each run, Pallas kernels for 26% -> 27%
where the time goes in v5:
time: 655 us; the launch traced here: 645 us
  Pallas kernels  189 us (29%)
  waiting for transfers between devices  168 us (26%)
  starting transfers between devices  77.9 us (12%)
  local copies, waits for them, and re-layouts  65.7 us (10%)
  matrix products  64.2 us (10%)
  other arithmetic  64 us (10%)
  between operations  15.4 us (2%)
    ppermute x43, waiting for transfers between devices, exchange(): return lax.ppermute(x, axis, [(i, i ^ stride) for i in range(size)])  109 us
    dot_general x12, matrix products, dot(): lax.dot_general(left, right, (contract, ((), ())), preferred_element_type...  59.7 us
    all_to_all x9, starting transfers between devices, swap_groups(): return lax.all_to_all(x, axis, split_axis=0, concat_axis=0, tiled=True)  42.5 us
    unnamed x130, local copies, waits for them, and re-layouts  41.7 us
    pallas_call x1, Pallas kernels, attend_back(): pl.pallas_call(functools.partial(attend_back_kernel, heads, bq, bk), grid...  38.1 us
    ppermute x43, starting transfers between devices, exchange(): return lax.ppermute(x, axis, [(i, i ^ stride) for i in range(size)])  35.1 us
    all_gather x1, waiting for transfers between devices, on_device(): lax.all_gather(after(jnp.concatenate([more, w_fc_out], axis=1), w_heads),...  30.5 us
    pallas_call x2, Pallas kernels, outer_pieces(): pl.pallas_call(functools.partial(outer_kernel, per), grid=(2 * half,), in...  29 us
  transfers between devices with their start and end apart: 54, of which 22 were waited for; matrix products, arithmetic and copies ran while one was open for 25% of the time, Pallas kernels for 27%

profile of v5, /device:TPU:0, one launch (start us, length us, event | category | flops | bytes accessed | tf_op | source)
XLA Modules:
  0.0 644.8 jit_solution(7626270171494418679)
XLA Ops:
  53.0 8.0 %collective-permute-done.8.refs_3_ = bf16[4,128,384]{2,1,0:T(8,128)(2,1)} collective-permute-done((bf16[4,128,384]{2,1,0:T(8,128)(2,1)S(1)}, bf16[4,128,384]{2,1,0:T(8,128)(2,1)}, u32[]{:S(2)}, u32[]{:S(2)}) %collective-permute-start.8) | collective-permute-done | bytes 393248 | tf_op jit(solution)/shard_map/ppermute | solution.py:61
  83.3 24.0 %attend.1 = (bf16[2048,256]{1,0:T(8,128)(2,1)S(1)}, f32[2048,256]{1,0:T(8,128)S(1)}, f32[4,2048]{1,0:T(4,128)S(1)}) custom-call(bf16[2048,768]{1,0:T(8,128)(2,1)S(1)} %convolution_convert_fusion.1.q_ref.k_ref.v_ref, bf16[2048,768]{1,0:T(8,128)(2,1)S(1)} %convolution_convert_fusion.1.q_ref.k_ref.v_ref, ...), custom_call_target="tpu_custom_call" | custom-call | flops 1048576 | bytes 1048576 | tf_op jit(solution)/shard_map/attend/pallas_call | solution.py:329
  120.6 13.5 %all-to-all-done.1 = bf16[4,512,256]{1,2,0:T(8,128)(2,1)S(1)} async-done(((bf16[4,512,256]{1,2,0:T(8,128)(2,1)}), bf16[4,512,256]{1,2,0:T(8,128)(2,1)S(1)}, u32[]{:S(2)}, u32[]{:S(2)}) %all-to-all-start.1) | async-done | bytes 1048608 | tf_op jit(solution)/shard_map/all_to_all | solution.py:632
  134.1 30.5 %all-gather.2.cloned.1.call-done.right_ref = bf16[1024,3072]{1,0:T(8,128)(2,1)} async-done(((bf16[128,3072]{1,0:T(8,128)(2,1)}), bf16[1024,3072]{1,0:T(8,128)(2,1)}) %all-gather.2.cloned.1.call-update) | async-done | bytes 6291472 | tf_op jit(solution)/shard_map/all_gather | solution.py:699
  196.9 29.9 %collective-permute-done.15.refs_1_ = bf16[1024,1024]{1,0:T(8,128)(2,1)} collective-permute-done((bf16[1024,1024]{1,0:T(8,128)(2,1)}, bf16[1024,1024]{1,0:T(8,128)(2,1)}, u32[]{:S(2)}, u32[]{:S(2)}) %collective-permute-start.15) | collective-permute-done | bytes 2097184 | tf_op jit(solution)/shard_map/ppermute | solution.py:61
  230.8 6.1 all-to-all-start.4
  237.0 18.9 %fusion.3 = (f32[1024,4096]{1,0:T(8,128)}, bf16[1024,4096]{1,0:T(8,128)(2,1)}) fusion(bf16[1024,1024]{1,0:T(8,128)(2,1)} %bitcast.192, bf16[4096,1024]{1,0:T(8,128)(2,1)} %constant_dynamic-update-slice_fusion.right_ref), kind=kOutput, calls=%fused_computation.4 | convolution fusion | flops 8631877632 | bytes 35651584 | tf_op jit(solution)/shard_map/dot_general | solution.py:44
  256.4 13.7 %collective-permute-done.18 = bf16[512,1024]{1,0:T(8,128)(2,1)} collective-permute-done((bf16[512,1024]{1,0:T(8,128)(2,1)}, bf16[512,1024]{1,0:T(8,128)(2,1)}, u32[]{:S(2)}, u32[]{:S(2)}) %collective-permute-start.18) | collective-permute-done | bytes 1048608 | tf_op jit(solution)/shard_map/ppermute | solution.py:61
  270.6 13.4 %pieces_product.1 = bf16[1024,1024]{1,0:T(8,128)(2,1)S(1)} custom-call(bf16[1024,4096]{1,0:T(8,128)(2,1)} %get-tuple-element.136.left_ref, bf16[1024,1024]{1,0:T(8,128)(2,1)} %bitcast.25.refs_0_, bf16[1024,1024]{1,0:T(8,128)(2,1)} %collective-permute-done.15.refs_1_, bf16[1024,1024]{1,0:T(8,128)(2,1)} %collective-permute-done.16.refs_2_, ...), custom_call_target="tpu_custom_call" | custom-call | flops 1048576 | bytes 1048576 | tf_op jit(solution)/shard_map/pieces_product/pallas_call | solution.py:535
  294.3 14.2 %outer_pieces.2 = (bf16[1024,1024]{1,0:T(8,128)(2,1)}, bf16[1024,1024]{1,0:T(8,128)(2,1)}, bf16[1024,1024]{1,0:T(8,128)(2,1)S(1)}, bf16[1024,1024]{1,0:T(8,128)(2,1)S(1)}) custom-call(bf16[1024,4096]{1,0:T(8,128)(2,1)} %get-tuple-element.136.left_ref, bf16[1024,1024]{1,0:T(8,128)(2,1)S(1)} %bitcast.190), custom_call_target="tpu_custom_call" | custom-call | flops 1048576 | bytes 1048576 | tf_op jit(solution)/shard_map/outer_pieces/pallas_call | solution.py:596
  311.2 6.1 all-to-all-start.5
  323.4 16.3 %pieces_slope_product.1.left_ref = bf16[1024,4096]{1,0:T(8,128)(2,1)} custom-call(bf16[1024,1024]{1,0:T(8,128)(2,1)S(1)} %bitcast.191, f32[1024,4096]{1,0:T(8,128)} %get-tuple-element.135.slope_ref, bf16[1024,1024]{1,0:T(8,128)(2,1)} %bitcast.25.refs_0_, bf16[1024,1024]{1,0:T(8,128)(2,1)} %collective-permute-done.15.refs_1_, ...), custom_call_target="tpu_custom_call" | custom-call | flops 1048576 | bytes 1048576 | tf_op jit(solution)/shard_map/pieces_slope_product/pallas_call | solution.py:563
  343.1 13.7 %product.3 = bf16[1024,1024]{1,0:T(8,128)(2,1)} custom-call(bf16[1024,4096]{1,0:T(8,128)(2,1)S(1)} %copy-done, bf16[4096,1024]{1,0:T(8,128)(2,1)} %constant_dynamic-update-slice_fusion.right_ref), custom_call_target="tpu_custom_call" | custom-call | flops 1048576 | bytes 1048576 | tf_op jit(solution)/shard_map/product/pallas_call | solution.py:458
  356.7 10.9 %gelu_product.1 = (bf16[2048,1024]{1,0:T(8,128)(2,1)S(1)}, f32[2048,1024]{1,0:T(8,128)}) custom-call(bf16[2048,1024]{1,0:T(8,128)(2,1)S(1)} %copy-done.7, bf16[1024,3072]{1,0:T(8,128)(2,1)} %all-gather.2.cloned.1.call-done.right_ref), custom_call_target="tpu_custom_call" | custom-call | flops 1048576 | bytes 1048576 | tf_op jit(solution)/shard_map/gelu_product/pallas_call | solution.py:483
  367.6 8.1 %product.4 = bf16[2048,1024]{1,0:T(8,128)(2,1)S(1)} custom-call(bf16[2048,1024]{1,0:T(8,128)(2,1)S(1)} %get-tuple-element.93.left_ref, bf16[1024,3072]{1,0:T(8,128)(2,1)} %all-gather.2.cloned.1.call-done.right_ref), custom_call_target="tpu_custom_call" | custom-call | flops 1048576 | bytes 1048576 | tf_op jit(solution)/shard_map/product/pallas_call | solution.py:458
  386.5 9.6 %slope_product.1.left_ref.right_ref = bf16[2048,1024]{1,0:T(8,128)(2,1)S(1)} custom-call(bf16[2048,1024]{1,0:T(8,128)(2,1)S(1)} %copy-done.10, bf16[1024,3072]{1,0:T(8,128)(2,1)} %all-gather.2.cloned.1.call-done.right_ref, f32[2048,1024]{1,0:T(8,128)} %get-tuple-element.97.slope_ref), custom_call_target="tpu_custom_call" | custom-call | flops 1048576 | bytes 1048576 | tf_op jit(solution)/shard_map/slope_product/pallas_call | solution.py:506
  399.6 6.8 %product.5 = bf16[2048,1024]{1,0:T(8,128)(2,1)S(1)} custom-call(bf16[2048,1024]{1,0:T(8,128)(2,1)S(1)} %slope_product.1.left_ref.right_ref, bf16[1024,3072]{1,0:T(8,128)(2,1)} %all-gather.2.cloned.1.call-done.right_ref), custom_call_target="tpu_custom_call" | custom-call | flops 1048576 | bytes 1048576 | tf_op jit(solution)/shard_map/product/pallas_call | solution.py:458
  412.6 14.8 %outer_pieces.3 = (bf16[1024,1024]{1,0:T(8,128)(2,1)}, bf16[1024,1024]{1,0:T(8,128)(2,1)}, bf16[1024,1024]{1,0:T(8,128)(2,1)S(1)}, bf16[1024,1024]{1,0:T(8,128)(2,1)S(1)}) custom-call(bf16[1024,4096]{1,0:T(8,128)(2,1)} %pieces_slope_product.1.left_ref, bf16[1024,1024]{1,0:T(8,128)(2,1)S(1)} %bitcast.193), custom_call_target="tpu_custom_call" | custom-call | flops 1048576 | bytes 1048576 | tf_op jit(solution)/shard_map/outer_pieces/pallas_call | solution.py:596
  446.2 10.0 %collective-permute-done.28 = bf16[512,1024]{1,0:T(8,128)(2,1)} collective-permute-done((bf16[512,1024]{1,0:T(8,128)(2,1)}, bf16[512,1024]{1,0:T(8,128)(2,1)}, u32[]{:S(2)}, u32[]{:S(2)}) %collective-permute-start.28) | collective-permute-done | bytes 1048608 | tf_op jit(solution)/shard_map/ppermute | solution.py:61
  499.9 38.1 %attend_back.1 = bf16[2048,768]{1,0:T(8,128)(2,1)} custom-call(bf16[2048,768]{1,0:T(8,128)(2,1)} %copy-done.3, bf16[2048,768]{1,0:T(8,128)(2,1)} %copy-done.3, bf16[2048,768]{1,0:T(8,128)(2,1)} %copy-done.3, bf16[2048,256]{1,0:T(8,128)(2,1)} %bitcast.41.g_ref, f32[2048,256]{1,0:T(8,128)} %copy-done.32, f32[4,2048]{1,0:T(4,128)} %copy-done.36), custom_call_target="tpu_custom_call" | custom-call | flops 68719476736 | bytes 7340032 | tf_op jit(solution)/shard_map/attend_back/pallas_call | solution.py:416
  550.2 7.9 %collective-permute-done.33 = bf16[256,1024]{1,0:T(8,128)(2,1)S(1)} collective-permute-done((bf16[256,1024]{1,0:T(8,128)(2,1)S(1)}, bf16[256,1024]{1,0:T(8,128)(2,1)S(1)}, u32[]{:S(2)}, u32[]{:S(2)}) %collective-permute-start.33) | collective-permute-done | bytes 524320 | tf_op jit(solution)/shard_map/ppermute | solution.py:61
  560.7 8.2 %fusion.10 = (f32[1024]{0:T(1024)S(1)}, f32[1024]{0:T(1024)S(1)}, bf16[1024,768]{1,0:T(8,128)(2,1)}) fusion(bf16[1024,768]{1,0:T(8,128)(2,1)S(1)} %copy-done.35, f32[768]{0:T(1024)S(1)} %convert_reduce_fusion, bf16[2048,1024]{1,0:T(8,128)(2,1)} %copy-done.19, bf16[2048,768]{1,0:T(8,128)(2,1)} %attend_back.1), kind=kOutput, calls=%fused_computation.32 | convolution fusion | flops 3225942016 | bytes 10497024 | tf_op jit(solution)/shard_map/dot_general | solution.py:44
  578.9 6.3 collective-permute-done.34
  603.8 8.0 %collective-permute-done.39 = bf16[144,512]{1,0:T(8,128)(2,1)S(1)} collective-permute-done((bf16[144,512]{1,0:T(8,128)(2,1)S(1)}, bf16[144,512]{1,0:T(8,128)(2,1)S(1)}, u32[]{:S(2)}, u32[]{:S(2)}) %collective-permute-start.39) | collective-permute-done | bytes 147488 | tf_op jit(solution)/shard_map/ppermute | solution.py:61
  (364 shorter events, 292.4 us)
Async XLA Ops:
  35.6 129.0 %all-gather.2.cloned.1.call-start = ((), (), s32[]{:S(2)}) async-start(), calls=%async_computation.10 | async-start | bytes 7077888 | tf_op jit(solution)/shard_map/all_gather | solution.py:699
  66.3 48.4 %collective-permute-start.10 = (bf16[1024,1024]{1,0:T(8,128)(2,1)}, bf16[1024,1024]{1,0:T(8,128)(2,1)}, u32[]{:S(2)}, u32[]{:S(2)}) collective-permute-start(bf16[1024,1024]{1,0:T(8,128)(2,1)} %bitcast.213), channel_id=1, source_target_pairs={{0,2},{1,3},{2,0},{3,1},{4,6},{5,7},{6,4},{7,5},{8,10},{9,11},{10,... | collective-permute-start | bytes 6291464 | tf_op jit(solution)/shard_map/ppermute | solution.py:61
  120.2 68.7 %collective-permute-start.11 = (bf16[1024,1024]{1,0:T(8,128)(2,1)}, bf16[1024,1024]{1,0:T(8,128)(2,1)}, u32[]{:S(2)}, u32[]{:S(2)}) collective-permute-start(bf16[1024,1024]{1,0:T(8,128)(2,1)} %collective-permute-done.10), channel_id=1, source_target_pairs={{0,1},{1,0},{2,3},{3,2},{4,5},{5,4},{6,7},{7,6},{8,9},{9,8},{10,11... | collective-permute-start | bytes 6291464 | tf_op jit(solution)/shard_map/ppermute | solution.py:61
  174.1 55.4 %all-to-all-start.3 = ((bf16[8,128,1024]{2,1,0:T(8,128)(2,1)}), bf16[8,128,1024]{2,1,0:T(8,128)(2,1)S(1)}, u32[]{:S(2)}, u32[]{:S(2)}) async-start(bf16[8,128,1024]{2,1,0:T(8,128)(2,1)} %bitcast.216), calls=%async_computation.3 | async-start | bytes 4194304 | tf_op jit(solution)/shard_map/all_to_all | solution.py:632
  177.9 48.9 %collective-permute-start.15 = (bf16[1024,1024]{1,0:T(8,128)(2,1)}, bf16[1024,1024]{1,0:T(8,128)(2,1)}, u32[]{:S(2)}, u32[]{:S(2)}) collective-permute-start(bf16[1024,1024]{1,0:T(8,128)(2,1)} %bitcast.25.refs_0_), channel_id=1, source_target_pairs={{0,2},{1,3},{2,0},{3,1},{4,6},{5,7},{6,4},{7,5},{8,10},{9,11},{10,... | collective-permute-start | bytes 6291464 | tf_op jit(solution)/shard_map/ppermute | solution.py:61
  192.1 63.9 %collective-permute-start.12 = (bf16[512,1024]{1,0:T(8,128)(2,1)}, bf16[512,1024]{1,0:T(8,128)(2,1)}, u32[]{:S(2)}, u32[]{:S(2)}) collective-permute-start(bf16[512,1024]{1,0:T(8,128)(2,1)} %fusion.38), channel_id=1, source_target_pairs={{0,2},{1,3},{2,0},{3,1},{4,6},{5,7},{6,4},{7,5},{8,10},{9,11},{10,... | collective-permute-start | bytes 3145736 | tf_op jit(solution)/shard_map/ppermute | solution.py:61
  195.4 74.6 %collective-permute-start.18 = (bf16[512,1024]{1,0:T(8,128)(2,1)}, bf16[512,1024]{1,0:T(8,128)(2,1)}, u32[]{:S(2)}, u32[]{:S(2)}) collective-permute-start(bf16[512,1024]{1,0:T(8,128)(2,1)} %fusion.23), channel_id=1, source_target_pairs={{0,2},{1,3},{2,0},{3,1},{4,6},{5,7},{6,4},{7,5},{8,10},{9,11},{10,... | collective-permute-start | bytes 3145736 | tf_op jit(solution)/shard_map/ppermute | solution.py:61
  196.9 73.2 %collective-permute-start.16 = (bf16[1024,1024]{1,0:T(8,128)(2,1)}, bf16[1024,1024]{1,0:T(8,128)(2,1)}, u32[]{:S(2)}, u32[]{:S(2)}) collective-permute-start(bf16[1024,1024]{1,0:T(8,128)(2,1)} %bitcast.25.refs_0_), channel_id=1, source_target_pairs={{0,1},{1,0},{2,3},{3,2},{4,5},{5,4},{6,7},{7,6},{8,9},{9,8},{10,11... | collective-permute-start | bytes 6291464 | tf_op jit(solution)/shard_map/ppermute | solution.py:61
  226.8 43.8 %collective-permute-start.17 = (bf16[1024,1024]{1,0:T(8,128)(2,1)}, bf16[1024,1024]{1,0:T(8,128)(2,1)}, u32[]{:S(2)}, u32[]{:S(2)}) collective-permute-start(bf16[1024,1024]{1,0:T(8,128)(2,1)} %collective-permute-done.15.refs_1_), channel_id=1, source_target_pairs={{0,1},{1,0},{2,3},{3,2},{4,5},{5,4},{6,7},{7,6},{8,9},{9,8},{10,11... | collective-permute-start | bytes 6291464 | tf_op jit(solution)/shard_map/ppermute | solution.py:61
  230.8 63.5 %all-to-all-start.4 = ((bf16[8,128,1024]{2,1,0:T(8,128)(2,1)}), bf16[8,128,1024]{2,1,0:T(8,128)(2,1)S(1)}, u32[]{:S(2)}, u32[]{:S(2)}) async-start(bf16[8,128,1024]{2,1,0:T(8,128)(2,1)} %bitcast.215), calls=%async_computation.4 | async-start | bytes 4194304 | tf_op jit(solution)/shard_map/all_to_all | solution.py:632
  255.9 34.1 %collective-permute-start.13 = (bf16[512,1024]{1,0:T(8,128)(2,1)}, bf16[512,1024]{1,0:T(8,128)(2,1)S(1)}, u32[]{:S(2)}, u32[]{:S(2)}) collective-permute-start(bf16[512,1024]{1,0:T(8,128)(2,1)} %fusion.38), channel_id=1, source_target_pairs={{0,1},{1,0},{2,3},{3,2},{4,5},{5,4},{6,7},{7,6},{8,9},{9,8},{10,11... | collective-permute-start | bytes 3145736 | tf_op jit(solution)/shard_map/ppermute | solution.py:61
  256.0 34.1 %collective-permute-start.14 = (bf16[512,1024]{1,0:T(8,128)(2,1)}, bf16[512,1024]{1,0:T(8,128)(2,1)S(1)}, u32[]{:S(2)}, u32[]{:S(2)}) collective-permute-start(bf16[512,1024]{1,0:T(8,128)(2,1)} %collective-permute-done.12), channel_id=1, source_target_pairs={{0,1},{1,0},{2,3},{3,2},{4,5},{5,4},{6,7},{7,6},{8,9},{9,8},{10,11... | collective-permute-start | bytes 3145736 | tf_op jit(solution)/shard_map/ppermute | solution.py:61
  311.2 66.9 %all-to-all-start.5 = ((bf16[8,128,1024]{2,1,0:T(8,128)(2,1)}), bf16[8,128,1024]{2,1,0:T(8,128)(2,1)}, u32[]{:S(2)}, u32[]{:S(2)}) async-start(bf16[8,128,1024]{2,1,0:T(8,128)(2,1)} %bitcast.194), calls=%async_computation.5 | async-start | bytes 4194304 | tf_op jit(solution)/shard_map/all_to_all | solution.py:632
  321.9 77.7 %collective-permute-start.25 = (bf16[1024,1024]{1,0:T(8,128)(2,1)}, bf16[1024,1024]{1,0:T(8,128)(2,1)}, u32[]{:S(2)}, u32[]{:S(2)}) collective-permute-start(bf16[1024,1024]{1,0:T(8,128)(2,1)} %add_convert_fusion.1), channel_id=1, source_target_pairs={{0,2},{1,3},{2,0},{3,1},{4,6},{5,7},{6,4},{7,5},{8,10},{9,11},{10,... | collective-permute-start | bytes 6291464 | tf_op jit(solution)/shard_map/ppermute | solution.py:61
  378.1 81.8 %all-to-all-start.6 = ((bf16[8,128,1024]{2,1,0:T(8,128)(2,1)}), bf16[8,128,1024]{2,1,0:T(8,128)(2,1)}, u32[]{:S(2)}, u32[]{:S(2)}) async-start(bf16[8,128,1024]{2,1,0:T(8,128)(2,1)} %bitcast.32), calls=%async_computation.6 | async-start | bytes 4194304 | tf_op jit(solution)/shard_map/all_to_all | solution.py:632
  384.1 231.6 %reduce-scatter.2.cloned.1.call-start = ((), (), s32[]{:S(2)}) async-start(), calls=%async_computation.11 | async-start | bytes 4718592 | tf_op jit(solution)/shard_map/reduce_scatter | solution.py:819
  408.1 26.3 %collective-permute-start.24 = (bf16[512,1024]{1,0:T(8,128)(2,1)}, bf16[512,1024]{1,0:T(8,128)(2,1)}, u32[]{:S(2)}, u32[]{:S(2)}) collective-permute-start(bf16[512,1024]{1,0:T(8,128)(2,1)} %add_convert_fusion.5), channel_id=1, source_target_pairs={{0,2},{1,3},{2,0},{3,1},{4,6},{5,7},{6,4},{7,5},{8,10},{9,11},{10,... | collective-permute-start | bytes 3145736 | tf_op jit(solution)/shard_map/ppermute | solution.py:61
  408.7 37.5 %collective-permute-start.27 = (bf16[512,1024]{1,0:T(8,128)(2,1)}, bf16[512,1024]{1,0:T(8,128)(2,1)}, u32[]{:S(2)}, u32[]{:S(2)}) collective-permute-start(bf16[512,1024]{1,0:T(8,128)(2,1)} %get-tuple-element.138), channel_id=1, source_target_pairs={{0,1},{1,0},{2,3},{3,2},{4,5},{5,4},{6,7},{7,6},{8,9},{9,8},{10,11... | collective-permute-start | bytes 3145736 | tf_op jit(solution)/shard_map/ppermute | solution.py:61
  411.7 44.5 %collective-permute-start.28 = (bf16[512,1024]{1,0:T(8,128)(2,1)}, bf16[512,1024]{1,0:T(8,128)(2,1)}, u32[]{:S(2)}, u32[]{:S(2)}) collective-permute-start(bf16[512,1024]{1,0:T(8,128)(2,1)} %add_convert_fusion.4), channel_id=1, source_target_pairs={{0,2},{1,3},{2,0},{3,1},{4,6},{5,7},{6,4},{7,5},{8,10},{9,11},{10,... | collective-permute-start | bytes 3145736 | tf_op jit(solution)/shard_map/ppermute | solution.py:61
  428.7 59.3 %collective-permute-start.29 = (bf16[1024,1024]{1,0:T(8,128)(2,1)}, bf16[1024,1024]{1,0:T(8,128)(2,1)}, u32[]{:S(2)}, u32[]{:S(2)}) collective-permute-start(bf16[1024,1024]{1,0:T(8,128)(2,1)} %get-tuple-element.107), channel_id=1, source_target_pairs={{0,1},{1,0},{2,3},{3,2},{4,5},{5,4},{6,7},{7,6},{8,9},{9,8},{10,11... | collective-permute-start | bytes 6291464 | tf_op jit(solution)/shard_map/ppermute | solution.py:61
  478.9 110.3 %collective-permute-start.42 = (bf16[1024,1024]{1,0:T(8,128)(2,1)}, bf16[1024,1024]{1,0:T(8,128)(2,1)}, u32[]{:S(2)}, u32[]{:S(2)}) collective-permute-start(bf16[1024,1024]{1,0:T(8,128)(2,1)} %get-tuple-element.87), channel_id=1, source_target_pairs={{0,1},{1,0},{2,3},{3,2},{4,5},{5,4},{6,7},{7,6},{8,9},{9,8},{10,11... | collective-permute-start | bytes 6291464 | tf_op jit(solution)/shard_map/ppermute | solution.py:61
  479.4 115.4 %collective-permute-start.41 = (bf16[1024,1024]{1,0:T(8,128)(2,1)}, bf16[1024,1024]{1,0:T(8,128)(2,1)}, u32[]{:S(2)}, u32[]{:S(2)}) collective-permute-start(bf16[1024,1024]{1,0:T(8,128)(2,1)} %get-tuple-element.100), channel_id=1, source_target_pairs={{0,1},{1,0},{2,3},{3,2},{4,5},{5,4},{6,7},{7,6},{8,9},{9,8},{10,11... | collective-permute-start | bytes 6291464 | tf_op jit(solution)/shard_map/ppermute | solution.py:61
  499.5 61.2 %collective-permute-start.32 = (bf16[1024,1024]{1,0:T(8,128)(2,1)}, bf16[1024,1024]{1,0:T(8,128)(2,1)}, u32[]{:S(2)}, u32[]{:S(2)}) collective-permute-start(bf16[1024,1024]{1,0:T(8,128)(2,1)} %add_convert_fusion), channel_id=1, source_target_pairs={{0,2},{1,3},{2,0},{3,1},{4,6},{5,7},{6,4},{7,5},{8,10},{9,11},{10,... | collective-permute-start | bytes 6291464 | tf_op jit(solution)/shard_map/ppermute | solution.py:61
  578.2 44.3 %collective-permute-start.40 = (bf16[512,1024]{1,0:T(8,128)(2,1)}, bf16[512,1024]{1,0:T(8,128)(2,1)S(1)}, u32[]{:S(2)}, u32[]{:S(2)}) collective-permute-start(bf16[512,1024]{1,0:T(8,128)(2,1)} %get-tuple-element.146), channel_id=1, source_target_pairs={{0,2},{1,3},{2,0},{3,1},{4,6},{5,7},{6,4},{7,5},{8,10},{9,11},{10,... | collective-permute-start | bytes 3145736 | tf_op jit(solution)/shard_map/ppermute | solution.py:61
  (89 other events, 934.0 us)
Sparse Core Ops, SparseCore 0:
  66.4 98.2 all-gather.1
  479.7 88.2 reduce-scatter.1

commit v6 on v5

--- a/solution.py
+++ b/solution.py
@@ -696,10 +696,8 @@
     gain_one, bias_one, gain_two, bias_two = (small[i : i + 1] for i in range(4))
     coef_full = small[4:6]
     normed_all = place_normed(token_pieces, order_e, me_es, gain_one, bias_one)
-    dense_weights = lax.all_gather(
-        after(jnp.concatenate([more, w_fc_out], axis=1), w_heads), "ep", axis=0, tiled=True
-    )
-    full_out = dense_weights[:, units : units + width]
+    own_in, own_out = more[:, :units], more[:, units:]
+    full_out = lax.all_gather(after(own_out, w_heads), "ep", axis=0, tiled=True)
     ups = gather_pieces(after(expert_up[0], token_pieces[1]), order_e)
 
     inputs = tokens.astype(jnp.float32)
@@ -708,6 +706,9 @@
     attended_mine = after(attended_mine, ups[1])
     attended = (
         swap_groups(attended_mine.reshape(n_es, rows, group), "es").transpose(1, 0, 2).reshape(rows, width)
+    )
+    dense_weights = lax.all_gather(
+        after(jnp.concatenate([own_in, w_fc_out], axis=1), attended), "ep", axis=0, tiled=True
     )
     hidden = inputs + dot(attended, full_out)
     normed_two, unit_two, inverse_two = norm_forward(hidden, gain_two, bias_two)
@@ -768,11 +769,11 @@
     out_home = to_experts(after(expert_out, expert_grad))
 
     activated_low, slope = gelu_product(after(dense_in, grad_expert_in), dense_weights, units)
-    dense_part = product(activated_low, dense_weights, width, place=2)
+    dense_part = product(activated_low, dense_weights, width, place=1)
     grad_home = to_experts(after(grad_expert_in, out_home))
     dense_folded = fold_all_but_last(split_pieces(dense_part), order_e)
     dense = sum_pieces(dense_folded, order_e[:1])
-    grad_inner_low = slope_product(after(dense_grad, dense_part), dense_weights, slope, width, 2)
+    grad_inner_low = slope_product(after(dense_grad, dense_part), dense_weights, slope, width, 1)
     grad_normed_part = product(after(grad_inner_low, last_downs, dense_folded[1]), dense_weights, units, ((1,), (1,)))
     grad_normed_folded = fold_all_but_last(split_pieces(grad_normed_part), order_e)
     grad_normed_dense = sum_pieces(grad_normed_folded, order_e[:1])

time: 655 us -> 653 us (level)
  local copies, waits for them, and re-layouts: 65.7 us -> 77.2 us
  Pallas kernels: 189 us -> 181 us
    all_to_all x9, waiting for transfers between devices: 28.4 us -> 72.6 us  [swap_groups(): return lax.all_to_all(x, axis, split_axis=0, concat_axis=0, tiled=True)]
    all_gather x1 -> x2, waiting for transfers between devices: 30.5 us -> 0.01 us  [the longest x1 0.01 us: on_device(): full_out = lax.all_gather(after(own_out, w_heads), 'ep', axis=0, tiled=True)]
    ppermute x43, waiting for transfers between devices: 109 us -> 94.6 us  [exchange(): return lax.ppermute(x, axis, [(i, i ^ stride) for i in range(size)])]
    unnamed x130 -> x146, local copies, waits for them, and re-layouts: 41.7 us -> 48.3 us
  transfers between devices with their start and end apart: 54 -> 55, of which waited for: 22 -> 24; matrix products, arithmetic and copies ran while one was open for 25% -> 24% of each run, Pallas kernels for 27% -> 28%
where the time goes in v6:
time: 653 us; the launch traced here: 643 us
  Pallas kernels  181 us (28%)
  waiting for transfers between devices  168 us (26%)
  local copies, waits for them, and re-layouts  77.2 us (12%)
  starting transfers between devices  74 us (11%)
  matrix products  64.8 us (10%)
  other arithmetic  62.5 us (10%)
  between operations  15.2 us (2%)
    ppermute x43, waiting for transfers between devices, exchange(): return lax.ppermute(x, axis, [(i, i ^ stride) for i in range(size)])  94.6 us
    all_to_all x9, waiting for transfers between devices, swap_groups(): return lax.all_to_all(x, axis, split_axis=0, concat_axis=0, tiled=True)  72.6 us
    dot_general x12, matrix products, dot(): lax.dot_general(left, right, (contract, ((), ())), preferred_element_type...  58.6 us
    unnamed x146, local copies, waits for them, and re-layouts  48.3 us
    all_to_all x9, starting transfers between devices, swap_groups(): return lax.all_to_all(x, axis, split_axis=0, concat_axis=0, tiled=True)  40.7 us
    pallas_call x1, Pallas kernels, attend_back(): pl.pallas_call(functools.partial(attend_back_kernel, heads, bq, bk), grid...  38 us
    ppermute x43, starting transfers between devices, exchange(): return lax.ppermute(x, axis, [(i, i ^ stride) for i in range(size)])  33.2 us
    pallas_call x2, Pallas kernels, outer_pieces(): pl.pallas_call(functools.partial(outer_kernel, per), grid=(2 * half,), in...  27.6 us
  transfers between devices with their start and end apart: 55, of which 24 were waited for; matrix products, arithmetic and copies ran while one was open for 24% of the time, Pallas kernels for 28%

profile of v6, /device:TPU:0, one launch (start us, length us, event | category | flops | bytes accessed | tf_op | source)
XLA Modules:
  0.0 642.8 jit_solution(8221405479211482832)
XLA Ops:
  70.2 6.0 norm_place.1
  80.0 24.0 %attend.1 = (bf16[2048,256]{1,0:T(8,128)(2,1)S(1)}, f32[2048,256]{1,0:T(8,128)S(1)}, f32[4,2048]{1,0:T(4,128)S(1)}) custom-call(bf16[2048,768]{1,0:T(8,128)(2,1)S(1)} %convolution_convert_fusion.1.q_ref.k_ref.v_ref, bf16[2048,768]{1,0:T(8,128)(2,1)S(1)} %convolution_convert_fusion.1.q_ref.k_ref.v_ref, ...), custom_call_target="tpu_custom_call" | custom-call | flops 1048576 | bytes 1048576 | tf_op jit(solution)/shard_map/attend/pallas_call | solution.py:329
  116.8 14.0 %all-to-all-done.1 = bf16[4,512,256]{1,2,0:T(8,128)(2,1)S(1)} async-done(((bf16[4,512,256]{1,2,0:T(8,128)(2,1)}), bf16[4,512,256]{1,2,0:T(8,128)(2,1)S(1)}, u32[]{:S(2)}, u32[]{:S(2)}) %all-to-all-start.1) | async-done | bytes 1048608 | tf_op jit(solution)/shard_map/all_to_all | solution.py:632
  138.4 6.2 all-to-all-start.3
  168.6 25.0 %collective-permute-done.15.refs_1_ = bf16[1024,1024]{1,0:T(8,128)(2,1)} collective-permute-done((bf16[1024,1024]{1,0:T(8,128)(2,1)}, bf16[1024,1024]{1,0:T(8,128)(2,1)}, u32[]{:S(2)}, u32[]{:S(2)}) %collective-permute-start.15) | collective-permute-done | bytes 2097184 | tf_op jit(solution)/shard_map/ppermute | solution.py:61
  193.6 15.9 %all-to-all-done.3 = bf16[8,128,1024]{2,1,0:T(8,128)(2,1)S(1)} async-done(((bf16[8,128,1024]{2,1,0:T(8,128)(2,1)}), bf16[8,128,1024]{2,1,0:T(8,128)(2,1)S(1)}, u32[]{:S(2)}, u32[]{:S(2)}) %all-to-all-start.3) | async-done | bytes 2097184 | tf_op jit(solution)/shard_map/all_to_all | solution.py:632
  214.8 19.0 %fusion.3 = (f32[1024,4096]{1,0:T(8,128)}, bf16[1024,4096]{1,0:T(8,128)(2,1)}) fusion(bf16[1024,1024]{1,0:T(8,128)(2,1)} %bitcast.194, bf16[4096,1024]{1,0:T(8,128)(2,1)} %constant_dynamic-update-slice_fusion.right_ref), kind=kOutput, calls=%fused_computation.4 | convolution fusion | flops 8631877632 | bytes 35651584 | tf_op jit(solution)/shard_map/dot_general | solution.py:44
  238.7 13.5 %pieces_product.1 = bf16[1024,1024]{1,0:T(8,128)(2,1)S(1)} custom-call(bf16[1024,4096]{1,0:T(8,128)(2,1)} %get-tuple-element.138.left_ref, bf16[1024,1024]{1,0:T(8,128)(2,1)} %bitcast.25.refs_0_, bf16[1024,1024]{1,0:T(8,128)(2,1)} %collective-permute-done.15.refs_1_, bf16[1024,1024]{1,0:T(8,128)(2,1)} %collective-permute-done.16.refs_2_, ...), custom_call_target="tpu_custom_call" | custom-call | flops 1048576 | bytes 1048576 | tf_op jit(solution)/shard_map/pieces_product/pallas_call | solution.py:535
  261.2 30.6 %all-to-all-done.4 = bf16[8,128,1024]{2,1,0:T(8,128)(2,1)S(1)} async-done(((bf16[8,128,1024]{2,1,0:T(8,128)(2,1)}), bf16[8,128,1024]{2,1,0:T(8,128)(2,1)S(1)}, u32[]{:S(2)}, u32[]{:S(2)}) %all-to-all-start.4) | async-done | bytes 2097184 | tf_op jit(solution)/shard_map/all_to_all | solution.py:632
  291.8 13.7 %outer_pieces.2 = (bf16[1024,1024]{1,0:T(8,128)(2,1)S(1)}, bf16[1024,1024]{1,0:T(8,128)(2,1)}, bf16[1024,1024]{1,0:T(8,128)(2,1)S(1)}, bf16[1024,1024]{1,0:T(8,128)(2,1)S(1)}) custom-call(bf16[1024,4096]{1,0:T(8,128)(2,1)} %get-tuple-element.138.left_ref, bf16[1024,1024]{1,0:T(8,128)(2,1)S(1)} %bitcast.192), custom_call_target="tpu_custom_call" | custom-call | flops 1048576 | bytes 1048576 | tf_op jit(solution)/shard_map/outer_pieces/pallas_call | solution.py:596
  320.4 16.3 %pieces_slope_product.1.left_ref = bf16[1024,4096]{1,0:T(8,128)(2,1)} custom-call(bf16[1024,1024]{1,0:T(8,128)(2,1)S(1)} %bitcast.193, f32[1024,4096]{1,0:T(8,128)} %get-tuple-element.137.slope_ref, bf16[1024,1024]{1,0:T(8,128)(2,1)} %bitcast.25.refs_0_, bf16[1024,1024]{1,0:T(8,128)(2,1)} %collective-permute-done.15.refs_1_, ...), custom_call_target="tpu_custom_call" | custom-call | flops 1048576 | bytes 1048576 | tf_op jit(solution)/shard_map/pieces_slope_product/pallas_call | solution.py:563
  340.1 13.5 %product.3 = bf16[1024,1024]{1,0:T(8,128)(2,1)} custom-call(bf16[1024,4096]{1,0:T(8,128)(2,1)S(1)} %copy-done, bf16[4096,1024]{1,0:T(8,128)(2,1)} %constant_dynamic-update-slice_fusion.right_ref), custom_call_target="tpu_custom_call" | custom-call | flops 1048576 | bytes 1048576 | tf_op jit(solution)/shard_map/product/pallas_call | solution.py:458
  358.0 9.4 %gelu_product.1 = (bf16[2048,1024]{1,0:T(8,128)(2,1)S(1)}, f32[2048,1024]{1,0:T(8,128)}) custom-call(bf16[2048,1024]{1,0:T(8,128)(2,1)S(1)} %copy-done.12, bf16[1024,2048]{1,0:T(8,128)(2,1)S(1)} %copy-done.1), custom_call_target="tpu_custom_call" | custom-call | flops 1048576 | bytes 1048576 | tf_op jit(solution)/shard_map/gelu_product/pallas_call | solution.py:483
  375.2 6.0 all-to-all-start.6
  385.6 8.9 %slope_product.1.left_ref.right_ref = bf16[2048,1024]{1,0:T(8,128)(2,1)S(1)} custom-call(bf16[2048,1024]{1,0:T(8,128)(2,1)S(1)} %copy-done.9, bf16[1024,2048]{1,0:T(8,128)(2,1)S(1)} %copy-done.3, f32[2048,1024]{1,0:T(8,128)} %get-tuple-element.99.slope_ref), custom_call_target="tpu_custom_call" | custom-call | flops 1048576 | bytes 1048576 | tf_op jit(solution)/shard_map/slope_product/pallas_call | solution.py:506
  409.5 13.9 %outer_pieces.3 = (bf16[1024,1024]{1,0:T(8,128)(2,1)S(1)}, bf16[1024,1024]{1,0:T(8,128)(2,1)}, bf16[1024,1024]{1,0:T(8,128)(2,1)S(1)}, bf16[1024,1024]{1,0:T(8,128)(2,1)S(1)}) custom-call(bf16[1024,4096]{1,0:T(8,128)(2,1)} %pieces_slope_product.1.left_ref, bf16[1024,1024]{1,0:T(8,128)(2,1)S(1)} %bitcast.195), custom_call_target="tpu_custom_call" | custom-call | flops 1048576 | bytes 1048576 | tf_op jit(solution)/shard_map/outer_pieces/pallas_call | solution.py:596
  443.0 10.1 %collective-permute-done.28 = bf16[512,1024]{1,0:T(8,128)(2,1)} collective-permute-done((bf16[512,1024]{1,0:T(8,128)(2,1)}, bf16[512,1024]{1,0:T(8,128)(2,1)}, u32[]{:S(2)}, u32[]{:S(2)}) %collective-permute-start.28) | collective-permute-done | bytes 1048608 | tf_op jit(solution)/shard_map/ppermute | solution.py:61
  497.1 38.0 %attend_back.1 = bf16[2048,768]{1,0:T(8,128)(2,1)} custom-call(bf16[2048,768]{1,0:T(8,128)(2,1)} %copy-done.7, bf16[2048,768]{1,0:T(8,128)(2,1)} %copy-done.7, bf16[2048,768]{1,0:T(8,128)(2,1)} %copy-done.7, bf16[2048,256]{1,0:T(8,128)(2,1)} %bitcast.41.g_ref, f32[2048,256]{1,0:T(8,128)} %copy-done.34, f32[4,2048]{1,0:T(4,128)} %copy-done.41), custom_call_target="tpu_custom_call" | custom-call | flops 68719476736 | bytes 7340032 | tf_op jit(solution)/shard_map/attend_back/pallas_call | solution.py:416
  536.8 5.8 convolution_convert_fusion
  547.2 8.1 %collective-permute-done.33 = bf16[256,1024]{1,0:T(8,128)(2,1)S(1)} collective-permute-done((bf16[256,1024]{1,0:T(8,128)(2,1)S(1)}, bf16[256,1024]{1,0:T(8,128)(2,1)S(1)}, u32[]{:S(2)}, u32[]{:S(2)}) %collective-permute-start.33) | collective-permute-done | bytes 524320 | tf_op jit(solution)/shard_map/ppermute | solution.py:61
  560.5 8.5 %fusion.10 = (f32[1024]{0:T(1024)S(1)}, f32[1024]{0:T(1024)S(1)}, bf16[1024,768]{1,0:T(8,128)(2,1)}) fusion(bf16[1024,768]{1,0:T(8,128)(2,1)} %copy-done.38, f32[768]{0:T(1024)S(1)} %convert_reduce_fusion, bf16[2048,1024]{1,0:T(8,128)(2,1)} %copy-done.21, bf16[2048,768]{1,0:T(8,128)(2,1)} %attend_back.1), kind=kOutput, calls=%fused_computation.32 | convolution fusion | flops 3225942016 | bytes 10497024 | tf_op jit(solution)/shard_map/dot_general | solution.py:44
  579.8 5.7 collective-permute-done.34
  590.1 5.7 add_bitcast_fusion
  604.7 9.8 %collective-permute-done.36 = bf16[144,512]{1,0:T(8,128)(2,1)S(1)} collective-permute-done((bf16[144,512]{1,0:T(8,128)(2,1)S(1)}, bf16[144,512]{1,0:T(8,128)(2,1)S(1)}, u32[]{:S(2)}, u32[]{:S(2)}) %collective-permute-start.36) | collective-permute-done | bytes 147488 | tf_op jit(solution)/shard_map/ppermute | solution.py:61
  (384 shorter events, 300.0 us)
Async XLA Ops:
  39.7 91.1 %all-gather.3.cloned.1.call-start = ((), (), s32[]{:S(2)}) async-start(), calls=%async_computation.10 | async-start | bytes 2359296 | tf_op jit(solution)/shard_map/all_gather | solution.py:700
  63.0 48.4 %collective-permute-start.10 = (bf16[1024,1024]{1,0:T(8,128)(2,1)}, bf16[1024,1024]{1,0:T(8,128)(2,1)}, u32[]{:S(2)}, u32[]{:S(2)}) collective-permute-start(bf16[1024,1024]{1,0:T(8,128)(2,1)} %bitcast.217), channel_id=1, source_target_pairs={{0,2},{1,3},{2,0},{3,1},{4,6},{5,7},{6,4},{7,5},{8,10},{9,11},{10,... | collective-permute-start | bytes 6291464 | tf_op jit(solution)/shard_map/ppermute | solution.py:61
  138.4 71.1 %all-to-all-start.3 = ((bf16[8,128,1024]{2,1,0:T(8,128)(2,1)}), bf16[8,128,1024]{2,1,0:T(8,128)(2,1)S(1)}, u32[]{:S(2)}, u32[]{:S(2)}) async-start(bf16[8,128,1024]{2,1,0:T(8,128)(2,1)} %bitcast.220), calls=%async_computation.3 | async-start | bytes 4194304 | tf_op jit(solution)/shard_map/all_to_all | solution.py:632
  144.6 209.0 %all-gather.5.cloned.1.call-start = ((), (), s32[]{:S(2)}) async-start(), calls=%async_computation.11 | async-start | bytes 4718592 | tf_op jit(solution)/shard_map/all_gather | solution.py:710
  144.8 48.8 %collective-permute-start.15 = (bf16[1024,1024]{1,0:T(8,128)(2,1)}, bf16[1024,1024]{1,0:T(8,128)(2,1)}, u32[]{:S(2)}, u32[]{:S(2)}) collective-permute-start(bf16[1024,1024]{1,0:T(8,128)(2,1)} %bitcast.25.refs_0_), channel_id=1, source_target_pairs={{0,2},{1,3},{2,0},{3,1},{4,6},{5,7},{6,4},{7,5},{8,10},{9,11},{10,... | collective-permute-start | bytes 6291464 | tf_op jit(solution)/shard_map/ppermute | solution.py:61
  156.4 81.6 %collective-permute-start.12 = (bf16[512,1024]{1,0:T(8,128)(2,1)}, bf16[512,1024]{1,0:T(8,128)(2,1)}, u32[]{:S(2)}, u32[]{:S(2)}) collective-permute-start(bf16[512,1024]{1,0:T(8,128)(2,1)} %copy-done.52), channel_id=1, source_target_pairs={{0,2},{1,3},{2,0},{3,1},{4,6},{5,7},{6,4},{7,5},{8,10},{9,11},{10,... | collective-permute-start | bytes 3145736 | tf_op jit(solution)/shard_map/ppermute | solution.py:61
  162.5 75.6 %collective-permute-start.18 = (bf16[512,1024]{1,0:T(8,128)(2,1)}, bf16[512,1024]{1,0:T(8,128)(2,1)}, u32[]{:S(2)}, u32[]{:S(2)}) collective-permute-start(bf16[512,1024]{1,0:T(8,128)(2,1)} %fusion.23), channel_id=1, source_target_pairs={{0,2},{1,3},{2,0},{3,1},{4,6},{5,7},{6,4},{7,5},{8,10},{9,11},{10,... | collective-permute-start | bytes 3145736 | tf_op jit(solution)/shard_map/ppermute | solution.py:61
  162.8 75.8 %collective-permute-start.16 = (bf16[1024,1024]{1,0:T(8,128)(2,1)}, bf16[1024,1024]{1,0:T(8,128)(2,1)}, u32[]{:S(2)}, u32[]{:S(2)}) collective-permute-start(bf16[1024,1024]{1,0:T(8,128)(2,1)} %bitcast.25.refs_0_), channel_id=1, source_target_pairs={{0,1},{1,0},{2,3},{3,2},{4,5},{5,4},{6,7},{7,6},{8,9},{9,8},{10,11... | collective-permute-start | bytes 6291464 | tf_op jit(solution)/shard_map/ppermute | solution.py:61
  193.6 45.1 %collective-permute-start.17 = (bf16[1024,1024]{1,0:T(8,128)(2,1)}, bf16[1024,1024]{1,0:T(8,128)(2,1)}, u32[]{:S(2)}, u32[]{:S(2)}) collective-permute-start(bf16[1024,1024]{1,0:T(8,128)(2,1)} %collective-permute-done.15.refs_1_), channel_id=1, source_target_pairs={{0,1},{1,0},{2,3},{3,2},{4,5},{5,4},{6,7},{7,6},{8,9},{9,8},{10,11... | collective-permute-start | bytes 6291464 | tf_op jit(solution)/shard_map/ppermute | solution.py:61
  210.8 81.0 %all-to-all-start.4 = ((bf16[8,128,1024]{2,1,0:T(8,128)(2,1)}), bf16[8,128,1024]{2,1,0:T(8,128)(2,1)S(1)}, u32[]{:S(2)}, u32[]{:S(2)}) async-start(bf16[8,128,1024]{2,1,0:T(8,128)(2,1)} %bitcast.219), calls=%async_computation.4 | async-start | bytes 4194304 | tf_op jit(solution)/shard_map/all_to_all | solution.py:632
  309.5 65.6 %all-to-all-start.5 = ((bf16[8,128,1024]{2,1,0:T(8,128)(2,1)}), bf16[8,128,1024]{2,1,0:T(8,128)(2,1)}, u32[]{:S(2)}, u32[]{:S(2)}) async-start(bf16[8,128,1024]{2,1,0:T(8,128)(2,1)} %bitcast.196), calls=%async_computation.5 | async-start | bytes 4194304 | tf_op jit(solution)/shard_map/all_to_all | solution.py:632
  318.9 79.0 %collective-permute-start.25 = (bf16[1024,1024]{1,0:T(8,128)(2,1)}, bf16[1024,1024]{1,0:T(8,128)(2,1)}, u32[]{:S(2)}, u32[]{:S(2)}) collective-permute-start(bf16[1024,1024]{1,0:T(8,128)(2,1)} %add_convert_fusion.1), channel_id=1, source_target_pairs={{0,2},{1,3},{2,0},{3,1},{4,6},{5,7},{6,4},{7,5},{8,10},{9,11},{10,... | collective-permute-start | bytes 6291464 | tf_op jit(solution)/shard_map/ppermute | solution.py:61
  375.2 81.7 %all-to-all-start.6 = ((bf16[8,128,1024]{2,1,0:T(8,128)(2,1)}), bf16[8,128,1024]{2,1,0:T(8,128)(2,1)}, u32[]{:S(2)}, u32[]{:S(2)}) async-start(bf16[8,128,1024]{2,1,0:T(8,128)(2,1)} %bitcast.32), calls=%async_computation.6 | async-start | bytes 4194304 | tf_op jit(solution)/shard_map/all_to_all | solution.py:632
  404.8 26.4 %collective-permute-start.22 = (bf16[512,1024]{1,0:T(8,128)(2,1)}, bf16[512,1024]{1,0:T(8,128)(2,1)}, u32[]{:S(2)}, u32[]{:S(2)}) collective-permute-start(bf16[512,1024]{1,0:T(8,128)(2,1)} %get-tuple-element.142), channel_id=1, source_target_pairs={{0,1},{1,0},{2,3},{3,2},{4,5},{5,4},{6,7},{7,6},{8,9},{9,8},{10,11... | collective-permute-start | bytes 3145736 | tf_op jit(solution)/shard_map/ppermute | solution.py:61
  405.0 26.3 %collective-permute-start.24 = (bf16[512,1024]{1,0:T(8,128)(2,1)}, bf16[512,1024]{1,0:T(8,128)(2,1)}, u32[]{:S(2)}, u32[]{:S(2)}) collective-permute-start(bf16[512,1024]{1,0:T(8,128)(2,1)} %add_convert_fusion.5), channel_id=1, source_target_pairs={{0,2},{1,3},{2,0},{3,1},{4,6},{5,7},{6,4},{7,5},{8,10},{9,11},{10,... | collective-permute-start | bytes 3145736 | tf_op jit(solution)/shard_map/ppermute | solution.py:61
  405.6 37.4 %collective-permute-start.27 = (bf16[512,1024]{1,0:T(8,128)(2,1)}, bf16[512,1024]{1,0:T(8,128)(2,1)}, u32[]{:S(2)}, u32[]{:S(2)}) collective-permute-start(bf16[512,1024]{1,0:T(8,128)(2,1)} %get-tuple-element.140), channel_id=1, source_target_pairs={{0,1},{1,0},{2,3},{3,2},{4,5},{5,4},{6,7},{7,6},{8,9},{9,8},{10,11... | collective-permute-start | bytes 3145736 | tf_op jit(solution)/shard_map/ppermute | solution.py:61
  408.6 44.5 %collective-permute-start.28 = (bf16[512,1024]{1,0:T(8,128)(2,1)}, bf16[512,1024]{1,0:T(8,128)(2,1)}, u32[]{:S(2)}, u32[]{:S(2)}) collective-permute-start(bf16[512,1024]{1,0:T(8,128)(2,1)} %add_convert_fusion.4), channel_id=1, source_target_pairs={{0,2},{1,3},{2,0},{3,1},{4,6},{5,7},{6,4},{7,5},{8,10},{9,11},{10,... | collective-permute-start | bytes 3145736 | tf_op jit(solution)/shard_map/ppermute | solution.py:61
  426.1 60.0 %collective-permute-start.29 = (bf16[1024,1024]{1,0:T(8,128)(2,1)}, bf16[1024,1024]{1,0:T(8,128)(2,1)}, u32[]{:S(2)}, u32[]{:S(2)}) collective-permute-start(bf16[1024,1024]{1,0:T(8,128)(2,1)} %get-tuple-element.109), channel_id=1, source_target_pairs={{0,1},{1,0},{2,3},{3,2},{4,5},{5,4},{6,7},{7,6},{8,9},{9,8},{10,11... | collective-permute-start | bytes 6291464 | tf_op jit(solution)/shard_map/ppermute | solution.py:61
  475.1 115.0 %collective-permute-start.42 = (bf16[1024,1024]{1,0:T(8,128)(2,1)S(1)}, bf16[1024,1024]{1,0:T(8,128)(2,1)}, u32[]{:S(2)}, u32[]{:S(2)}) collective-permute-start(bf16[1024,1024]{1,0:T(8,128)(2,1)S(1)} %copy-done.36), channel_id=1, source_target_pairs={{0,1},{1,0},{2,3},{3,2},{4,5},{5,4},{6,7},{7,6},{8,9},{9,8},{10,11... | collective-permute-start | bytes 6291464 | tf_op jit(solution)/shard_map/ppermute | solution.py:61
  475.6 120.2 %collective-permute-start.41 = (bf16[1024,1024]{1,0:T(8,128)(2,1)}, bf16[1024,1024]{1,0:T(8,128)(2,1)}, u32[]{:S(2)}, u32[]{:S(2)}) collective-permute-start(bf16[1024,1024]{1,0:T(8,128)(2,1)} %copy-done.37), channel_id=1, source_target_pairs={{0,1},{1,0},{2,3},{3,2},{4,5},{5,4},{6,7},{7,6},{8,9},{9,8},{10,11... | collective-permute-start | bytes 6291464 | tf_op jit(solution)/shard_map/ppermute | solution.py:61
  482.2 135.1 %reduce-scatter.2.cloned.1.call-start = ((), (), s32[]{:S(2)}) async-start(), calls=%async_computation.12 | async-start | bytes 4718592 | tf_op jit(solution)/shard_map/reduce_scatter | solution.py:820
  496.7 63.8 %collective-permute-start.32 = (bf16[1024,1024]{1,0:T(8,128)(2,1)}, bf16[1024,1024]{1,0:T(8,128)(2,1)}, u32[]{:S(2)}, u32[]{:S(2)}) collective-permute-start(bf16[1024,1024]{1,0:T(8,128)(2,1)} %add_convert_fusion), channel_id=1, source_target_pairs={{0,2},{1,3},{2,0},{3,1},{4,6},{5,7},{6,4},{7,5},{8,10},{9,11},{10,... | collective-permute-start | bytes 6291464 | tf_op jit(solution)/shard_map/ppermute | solution.py:61
  545.8 29.1 %collective-permute-start.31 = (bf16[2,512,1024]{2,1,0:T(8,128)(2,1)}, bf16[2,512,1024]{2,1,0:T(8,128)(2,1)}, u32[]{:S(2)}, u32[]{:S(2)}) collective-permute-start(bf16[2,512,1024]{2,1,0:T(8,128)(2,1)} %dynamic-slice_bitcast_fusion), channel_id=1, source_target_pairs={{0,1},{1,0},{2,3},{3,2},{4,5},{5,4},{6,7},{7,6},{8,9},{9,8},{10,11... | collective-permute-start | bytes 6291464 | tf_op jit(solution)/shard_map/ppermute | solution.py:61
  579.0 44.5 %collective-permute-start.40 = (bf16[512,1024]{1,0:T(8,128)(2,1)}, bf16[512,1024]{1,0:T(8,128)(2,1)}, u32[]{:S(2)}, u32[]{:S(2)}) collective-permute-start(bf16[512,1024]{1,0:T(8,128)(2,1)} %get-tuple-element.148), channel_id=1, source_target_pairs={{0,2},{1,3},{2,0},{3,1},{4,6},{5,7},{6,4},{7,5},{8,10},{9,11},{10,... | collective-permute-start | bytes 3145736 | tf_op jit(solution)/shard_map/ppermute | solution.py:61
  (98 other events, 889.1 us)
Sparse Core Ops, SparseCore 0:
  63.0 50.2 all-gather.2
  156.5 127.9 all-gather.4
  486.6 89.7 reduce-scatter.1
